TPU v7x, 32 devices: a whole 2x2x4 slice. The times are simulated.
32 devices in a mesh: section: 4 (over y, x), dp: 8 (over z, core).
Axes of the slice: x: 2, y: 2, z: 4, core: 2. Of those that a mesh axis runs over, the one named last changes fastest.
Arguments:
- tokens: bfloat16 [8192, 384], P(('section', 'dp')), may hold values from -6 to 6
- cotangent: bfloat16 [8192, 384], P(('section', 'dp')), may hold values from -6 to 6
- lengths: int32 [4, 8], P(None, 'dp'), may hold values from 32 to 256, as said below
- gain_one: bfloat16 [384], P('section'), may hold values from 0.099609375 to 1.8984375
- mixing_one: bfloat16 [384, 1152], P(None, 'section'), may hold values from -0.3125 to 0.3125
- output_one: bfloat16 [384, 384], P(None, 'section'), may hold values from -2.5 to 2.5
- gain_two: bfloat16 [384], P('section'), may hold values from 0.099609375 to 1.8984375
- up_two: bfloat16 [384, 1536], P(None, 'section'), may hold values from -0.3125 to 0.3125
- down_two: bfloat16 [1536, 384], P('section'), may hold values from -0.15625 to 0.15625
- gain_three: bfloat16 [384], P('section'), may hold values from 0.099609375 to 1.8984375
- pair_three: bfloat16 [384, 768], P(None, 'section'), may hold values from -0.3125 to 0.3125
- fresh_three: bfloat16 [384, 192], P(None, 'section'), may hold values from -0.3125 to 0.3125
- output_three: bfloat16 [384, 384], P(None, 'section'), may hold values from -2.5 to 2.5
- gain_four: bfloat16 [384], P('section'), may hold values from 0.099609375 to 1.8984375
- up_four: bfloat16 [384, 1536], P(None, 'section'), may hold values from -0.3125 to 0.3125
- down_four: bfloat16 [1536, 384], P('section'), may hold values from -0.15625 to 0.15625
Outputs:
- output: float32 [8192, 384], P(('section', 'dp'))
- input_grad: float32 [8192, 384], P(('section', 'dp'))
- grad_gain_one: float32 [384], replicated
- grad_mixing_one: float32 [384, 1152], replicated
- grad_output_one: float32 [384, 384], replicated
- grad_gain_two: float32 [384], replicated
- grad_up_two: float32 [384, 1536], replicated
- grad_down_two: float32 [1536, 384], replicated
- grad_gain_three: float32 [384], replicated
- grad_pair_three: float32 [384, 768], replicated
- grad_fresh_three: float32 [384, 192], replicated
- grad_output_three: float32 [384, 384], replicated
- grad_gain_four: float32 [384], replicated
- grad_up_four: float32 [384, 1536], replicated
- grad_down_four: float32 [1536, 384], replicated
Inputs may be any that keep to these rules, and one draw needn't show every extreme that they name: lengths[m, r] is the number of valid positions of the sequence that starts at row (m * 8 + r) * 256; in every draw each data group r has some sequence 256 long, and some sequence has 32 positions.
All inputs are finite; a program needn't handle non-finite values.
Results may differ from a plain program's by a relative error of at most 0.019.
Values may be sent and summed in bfloat16 or wider, within the bound.
No kernel may reach another device: no remote copies, remote signals or barrier semaphores. Data moves between devices by JAX's collectives and lax.ppermute only.
A program may use at most 192 MiB of HBM per device.

v0:
```python
import jax
import jax.numpy as jnp
from jax import lax
from jax.sharding import PartitionSpec as P

D = 384
HEADS = 6
HEAD = 64
SHARED = 3


EPSILON = 1e-05
MASKED = -1e30
GELU_SCALE = 0.7978845608028654
block_limit = 512


def shortened(shard):
    return jax.tree.map(lambda a: a.astype(jnp.bfloat16) if a.dtype == jnp.float32 else a, shard)


def from_behind(value, axis, steps):
    count = lax.axis_size(axis)
    leading, last = (max(0, -steps), min(count, count - steps))
    return lax.ppermute(value, axis, [(source, source + steps) for source in range(leading, last)])


def layer_norm(hidden, norm_gain):
    centred = hidden - jnp.mean(hidden, -1, keepdims=True)
    spread = jnp.mean(centred * centred, -1, keepdims=True)
    return centred * lax.rsqrt(spread + EPSILON) * norm_gain


def gelu(upward):
    return (
        0.5 * upward * (1.0 + jnp.tanh(GELU_SCALE * (upward + 0.044715 * upward * upward * upward)))
    )


def product(left, right):
    return jnp.dot(left, right, preferred_element_type=jnp.float32)


def inner_rows(left, right):
    return lax.dot_general(
        left, right, (((0,), (0,)), ((), ())), preferred_element_type=jnp.float32
    )


def inner_cols(left, right):
    return lax.dot_general(
        left, right, (((1,), (1,)), ((), ())), preferred_element_type=jnp.float32
    )


def split_heads(matrix):
    return matrix.reshape(matrix.shape[0], HEADS, HEAD)


def norm_back(hidden, norm_gain, grad_normed):
    normed_out, pullback = jax.vjp(layer_norm, hidden, norm_gain)
    return pullback(grad_normed)


def block_scores(query_heads, key_heads, first_row, last_row, length):
    scores = jnp.einsum(
        "qhd,khd->hqk",
        query_heads[first_row:last_row],
        key_heads[:last_row],
        preferred_element_type=jnp.float32,
    ) * HEAD ** (-0.5)
    row_index = jnp.arange(first_row, last_row)[:, None]
    col_index = jnp.arange(last_row)[None, :]
    allowed = (col_index <= row_index) & (col_index < length)
    return jnp.where(allowed[None], scores, MASKED)


def attend_forward(queries, key_rows, values, length):
    total_rows = queries.shape[0]
    block_rows = min(total_rows, block_limit)
    query_heads = split_heads(queries)
    key_heads = split_heads(key_rows)
    value_heads = split_heads(values)
    pieces = []
    sums_kept = []
    for first_row in range(0, total_rows, block_rows):
        last_row = first_row + block_rows
        scores = block_scores(query_heads, key_heads, first_row, last_row, length)
        row_peak = jnp.max(scores, -1, keepdims=True)
        raised = jnp.exp(scores - row_peak)
        totals = jnp.sum(raised, -1, keepdims=True)
        probability = (raised / totals).astype(jnp.bfloat16)
        blended = jnp.einsum(
            "hqk,khd->qhd", probability, value_heads[:last_row], preferred_element_type=jnp.float32
        )
        pieces.append(blended.reshape(block_rows, HEADS * HEAD))
        sums_kept.append((row_peak + jnp.log(totals))[:, :, 0])
    return (jnp.concatenate(pieces, 0), jnp.concatenate(sums_kept, 1))


def attend_backward(queries, key_rows, values, grad_mixed, log_sums, length):
    total_rows = queries.shape[0]
    block_rows = min(total_rows, block_limit)
    query_heads = split_heads(queries)
    key_heads = split_heads(key_rows)
    value_heads = split_heads(values)
    grad_heads = split_heads(grad_mixed)
    grad_keys = jnp.zeros((total_rows, HEADS, HEAD), jnp.float32)
    grad_values = jnp.zeros((total_rows, HEADS, HEAD), jnp.float32)
    scores = block_scores(query_heads, key_heads, 0, block_rows, length)
    probability = jnp.exp(scores - log_sums[:, 0:block_rows, None])
    rounded = probability.astype(jnp.bfloat16)
    grad_prob = jnp.einsum(
        "qhd,khd->hqk", grad_heads, value_heads, preferred_element_type=jnp.float32
    )
    centre = jnp.sum(probability * grad_prob, -1, keepdims=True)
    grad_scores = (probability * (grad_prob - centre)).astype(jnp.bfloat16)
    query_part = jnp.einsum(
        "hqk,khd->qhd", grad_scores, key_heads, preferred_element_type=jnp.float32
    ) * HEAD ** (-0.5)
    query_pieces = [query_part]
    key_part = jnp.einsum(
        "hqk,qhd->khd", grad_scores, query_heads, preferred_element_type=jnp.float32
    ) * HEAD ** (-0.5)
    value_part = jnp.einsum("hqk,qhd->khd", rounded, grad_heads, preferred_element_type=jnp.float32)
    grad_keys = grad_keys.at[:block_rows].add(key_part)
    grad_values = grad_values.at[:block_rows].add(value_part)
    width_all = HEADS * HEAD
    grad_queries = jnp.concatenate(query_pieces, 0).reshape(total_rows, width_all)
    return (
        grad_queries,
        grad_keys.reshape(total_rows, width_all),
        grad_values.reshape(total_rows, width_all),
    )


def first_forward(hidden, length, norm_gain, mixing, output):
    normed = layer_norm(hidden, norm_gain).astype(jnp.bfloat16)
    mixed_rows = product(normed, mixing).astype(jnp.bfloat16)
    attended, log_sums = attend_forward(
        mixed_rows[:, :D], mixed_rows[:, D : 2 * D], mixed_rows[:, 2 * D :], length
    )
    attended = attended.astype(jnp.bfloat16)
    return (
        hidden + product(attended, output),
        mixed_rows[:, 2 * D : 2 * D + SHARED * HEAD],
        attended,
        log_sums,
    )


def first_backward(
    hidden, length, attended, log_sums, grad_out, grad_shared, norm_gain, mixing, output
):
    normed = layer_norm(hidden, norm_gain).astype(jnp.bfloat16)
    mixed_rows = product(normed, mixing).astype(jnp.bfloat16)
    grad_low = grad_out.astype(jnp.bfloat16)
    grad_output = inner_rows(attended, grad_low)
    grad_attended = inner_cols(grad_low, output).astype(jnp.bfloat16)
    grad_query, grad_key, grad_value = attend_backward(
        mixed_rows[:, :D],
        mixed_rows[:, D : 2 * D],
        mixed_rows[:, 2 * D :],
        grad_attended,
        log_sums,
        length,
    )
    shared_width = SHARED * HEAD
    grad_value = jnp.concatenate(
        [grad_value[:, :shared_width] + grad_shared, grad_value[:, shared_width:]], 1
    )
    grad_mixed = jnp.concatenate([grad_query, grad_key, grad_value], 1).astype(jnp.bfloat16)
    grad_mixing = inner_rows(normed, grad_mixed)
    grad_hidden, grad_gain = norm_back(hidden, norm_gain, inner_cols(grad_mixed, mixing))
    return (grad_out + grad_hidden, (grad_gain, grad_mixing, grad_output))


def feed_forward(hidden, norm_gain, up_weight, down_weight):
    normed = layer_norm(hidden, norm_gain).astype(jnp.bfloat16)
    active = gelu(product(normed, up_weight)).astype(jnp.bfloat16)
    return hidden + product(active, down_weight)


def feed_backward(hidden, grad_out, norm_gain, up_weight, down_weight):
    normed = layer_norm(hidden, norm_gain).astype(jnp.bfloat16)
    active, gelu_pull = jax.vjp(gelu, product(normed, up_weight))
    active = active.astype(jnp.bfloat16)
    grad_low = grad_out.astype(jnp.bfloat16)
    grad_down = inner_rows(active, grad_low)
    grad_upward = gelu_pull(inner_cols(grad_low, down_weight))[0].astype(jnp.bfloat16)
    grad_up = inner_rows(normed, grad_upward)
    grad_hidden, grad_gain = norm_back(hidden, norm_gain, inner_cols(grad_upward, up_weight))
    return (grad_out + grad_hidden, (grad_gain, grad_up, grad_down))


def third_forward(hidden, length, shared, norm_gain, pair_weight, fresh_weight, output):
    normed = layer_norm(hidden, norm_gain).astype(jnp.bfloat16)
    pair_rows = product(normed, pair_weight).astype(jnp.bfloat16)
    fresh_rows = product(normed, fresh_weight).astype(jnp.bfloat16)
    values = jnp.concatenate([shared, fresh_rows], 1)
    attended, log_sums = attend_forward(pair_rows[:, :D], pair_rows[:, D:], values, length)
    attended = attended.astype(jnp.bfloat16)
    return (hidden + product(attended, output), shared, attended, log_sums)


def third_backward(
    hidden,
    length,
    shared,
    attended,
    log_sums,
    grad_out,
    norm_gain,
    pair_weight,
    fresh_weight,
    output,
):
    normed = layer_norm(hidden, norm_gain).astype(jnp.bfloat16)
    pair_rows = product(normed, pair_weight).astype(jnp.bfloat16)
    fresh_rows = product(normed, fresh_weight).astype(jnp.bfloat16)
    values = jnp.concatenate([shared, fresh_rows], 1)
    grad_low = grad_out.astype(jnp.bfloat16)
    grad_output = inner_rows(attended, grad_low)
    grad_attended = inner_cols(grad_low, output).astype(jnp.bfloat16)
    grad_query, grad_key, grad_value = attend_backward(
        pair_rows[:, :D], pair_rows[:, D:], values, grad_attended, log_sums, length
    )
    shared_width = SHARED * HEAD
    grad_pair = jnp.concatenate([grad_query, grad_key], 1).astype(jnp.bfloat16)
    grad_fresh = grad_value[:, shared_width:].astype(jnp.bfloat16)
    grad_pair_weight = inner_rows(normed, grad_pair)
    grad_fresh_weight = inner_rows(normed, grad_fresh)
    grad_normed = inner_cols(grad_pair, pair_weight) + inner_cols(grad_fresh, fresh_weight)
    grad_hidden, grad_gain = norm_back(hidden, norm_gain, grad_normed)
    shared_grad = grad_value[:, :shared_width].astype(jnp.bfloat16)
    return (
        grad_out + grad_hidden,
        shared_grad,
        (grad_gain, grad_pair_weight, grad_fresh_weight, grad_output),
    )


def unpack(weights):
    part_one = (weights[0].astype(jnp.float32), weights[1], weights[2])
    part_two = (weights[3].astype(jnp.float32), weights[4], weights[5])
    part_three = (weights[6].astype(jnp.float32), weights[7], weights[8], weights[9])
    part_four = (weights[10].astype(jnp.float32), weights[11], weights[12])
    return (part_one, part_two, part_three, part_four)


def take_slot(buffer, slot_index):
    return lax.dynamic_index_in_dim(buffer, slot_index, 0, False)


def keep_slot(buffer, fresh_value, slot_index, active):
    previous = lax.dynamic_index_in_dim(buffer, slot_index, 0, False)
    return lax.dynamic_update_index_in_dim(
        buffer, jnp.where(active, fresh_value, previous), slot_index, 0
    )


def add_up(running, fresh_grads):
    return tuple((total + extra for total, extra in zip(running, fresh_grads)))


def zero_grads(members):
    return tuple((jnp.zeros(member.shape, jnp.float32) for member in members))


def shards(
    tokens,
    cotangent,
    lengths,
    gain_one,
    mixing_one,
    output_one,
    gain_two,
    up_two,
    down_two,
    gain_three,
    pair_three,
    fresh_three,
    output_three,
    gain_four,
    up_four,
    down_four,
):
    row_count = tokens.shape[0]
    local_lengths = lengths[:, 0]
    section_index = lax.axis_index("section")
    gathered = (
        lax.all_gather(tokens, "section", axis=0, tiled=True),
        lax.all_gather(cotangent, "section", axis=0, tiled=True),
        lax.all_gather(gain_one, "section", axis=0, tiled=True),
        lax.all_gather(mixing_one, "section", axis=1, tiled=True),
        lax.all_gather(output_one, "section", axis=1, tiled=True),
        lax.all_gather(gain_two, "section", axis=0, tiled=True),
        lax.all_gather(up_two, "section", axis=1, tiled=True),
        lax.all_gather(down_two, "section", axis=0, tiled=True),
        lax.all_gather(gain_three, "section", axis=0, tiled=True),
        lax.all_gather(pair_three, "section", axis=1, tiled=True),
        lax.all_gather(fresh_three, "section", axis=1, tiled=True),
        lax.all_gather(output_three, "section", axis=1, tiled=True),
        lax.all_gather(gain_four, "section", axis=0, tiled=True),
        lax.all_gather(up_four, "section", axis=1, tiled=True),
        lax.all_gather(down_four, "section", axis=0, tiled=True),
    )
    section_count = lax.axis_size("section")
    last_section = section_count - 1
    token_all = gathered[0].reshape(section_count, row_count, D)
    seed_all = gathered[1].reshape(section_count, row_count, D)
    part_one, part_two, part_three, part_four = unpack(gathered[2:])
    shared_width = SHARED * HEAD
    zero_rows = jnp.zeros((row_count, D), jnp.float32)
    zero_attended = jnp.zeros((row_count, D), jnp.bfloat16)
    zero_sums = jnp.zeros((HEADS, row_count), jnp.float32)
    zero_values = jnp.zeros((row_count, shared_width), jnp.bfloat16)

    def run_first(section_entry, value_in, length):
        return first_forward(section_entry.astype(jnp.float32), length, *part_one)

    def run_second(section_entry, value_in, length):
        return (
            feed_forward(section_entry.astype(jnp.float32), *part_two),
            value_in,
            zero_attended,
            zero_sums,
        )

    def run_third(section_entry, value_in, length):
        return third_forward(section_entry.astype(jnp.float32), length, value_in, *part_three)

    def run_fourth(section_entry, value_in, length):
        return (
            feed_forward(section_entry.astype(jnp.float32), *part_four),
            value_in,
            zero_attended,
            zero_sums,
        )

    def run_spare(section_entry, value_in, length):
        return (zero_rows, value_in, zero_attended, zero_sums)

    stash_in = jnp.zeros((section_count, row_count, D), jnp.bfloat16)
    stash_attended = jnp.zeros((section_count, row_count, D), jnp.bfloat16)
    stash_sums = jnp.zeros((section_count, HEADS, row_count), jnp.float32)
    stash_values = jnp.zeros((section_count, row_count, shared_width), jnp.bfloat16)
    results = jnp.zeros((section_count, row_count, D), jnp.float32)
    incoming = zero_attended
    carried = zero_values
    for tick_index in range(2 * section_count - 1):
        micro_slot = tick_index - section_index
        active = (micro_slot >= 0) & (micro_slot < section_count)
        slot_index = jnp.clip(micro_slot, 0, last_section)
        length = local_lengths[slot_index]
        section_entry = jnp.where(section_index == 0, take_slot(token_all, slot_index), incoming)
        value_in = carried
        result, value_out, attended, log_sums = lax.switch(
            jnp.where(active, section_index, 4),
            [run_first, run_second, run_third, run_fourth, run_spare],
            section_entry,
            value_in,
            length,
        )
        stash_in = keep_slot(stash_in, section_entry, slot_index, active)
        stash_attended = keep_slot(stash_attended, attended, slot_index, active)
        stash_sums = keep_slot(stash_sums, log_sums, slot_index, active)
        stash_values = keep_slot(stash_values, value_in, slot_index, active)
        results = keep_slot(results, result, slot_index, active & (section_index == last_section))
        outgoing = result.astype(jnp.bfloat16)
        incoming, carried = (
            from_behind(outgoing, "section", 1),
            from_behind(shortened(value_out), "section", 1).astype(value_out.dtype),
        )
    grads_one = zero_grads(part_one)
    grads_two = zero_grads(part_two)
    grads_three = zero_grads(part_three)
    grads_four = zero_grads(part_four)
    grad_results = jnp.zeros((section_count, row_count, D), jnp.float32)
    back_in = zero_attended
    back_values = zero_values
    for tick_index in range(2 * section_count - 1):
        micro_slot = tick_index - last_section + section_index
        active = (micro_slot >= 0) & (micro_slot < section_count)
        slot_index = jnp.clip(micro_slot, 0, last_section)
        length = local_lengths[slot_index]
        valid_rows = (jnp.arange(row_count) < length)[:, None]
        seeded = jnp.where(valid_rows, take_slot(seed_all, slot_index).astype(jnp.float32), 0.0)
        grad_now = jnp.where(section_index == last_section, seeded, back_in.astype(jnp.float32))
        grad_shared = back_values.astype(jnp.float32)
        section_entry = take_slot(stash_in, slot_index).astype(jnp.float32)
        attended = take_slot(stash_attended, slot_index)
        log_sums = take_slot(stash_sums, slot_index)
        shared = take_slot(stash_values, slot_index)

        def back_first(running):
            grad_in, fresh_grads = first_backward(
                section_entry, length, attended, log_sums, grad_now, grad_shared, *part_one
            )
            return (grad_in, zero_values, add_up(running, fresh_grads))

        def back_second(running):
            grad_in, fresh_grads = feed_backward(section_entry, grad_now, *part_two)
            return (grad_in, back_values, add_up(running, fresh_grads))

        def back_third(running):
            grad_in, shared_grad, fresh_grads = third_backward(
                section_entry, length, shared, attended, log_sums, grad_now, *part_three
            )
            return (grad_in, shared_grad, add_up(running, fresh_grads))

        def back_fourth(running):
            grad_in, fresh_grads = feed_backward(section_entry, grad_now, *part_four)
            return (grad_in, zero_values, add_up(running, fresh_grads))

        def skip_section(running):
            return (zero_rows, zero_values, running)

        entry_one, values_one, grads_one = lax.cond(
            active & (section_index == 0), back_first, skip_section, grads_one
        )
        entry_two, values_two, grads_two = lax.cond(
            active & (section_index == 1), back_second, skip_section, grads_two
        )
        entry_three, values_three, grads_three = lax.cond(
            active & (section_index == 2), back_third, skip_section, grads_three
        )
        entry_four, values_four, grads_four = lax.cond(
            active & (section_index == 3), back_fourth, skip_section, grads_four
        )
        grad_entry = entry_one + entry_two + entry_three + entry_four
        value_grad = values_one + values_two + values_three + values_four
        grad_results = keep_slot(
            grad_results, grad_entry, slot_index, active & (section_index == 0)
        )
        outgoing = grad_entry.astype(jnp.bfloat16)
        back_in, back_values = from_behind((outgoing, value_grad), "section", -1)
    output, input_grad = (
        lax.psum_scatter(
            results.reshape(section_count * row_count, D).astype(jnp.bfloat16),
            "section",
            scatter_dimension=0,
            tiled=True,
        ).astype(jnp.float32),
        lax.psum_scatter(
            grad_results.reshape(section_count * row_count, D).astype(jnp.bfloat16),
            "section",
            scatter_dimension=0,
            tiled=True,
        ).astype(jnp.float32),
    )
    local_grads = grads_one + grads_two + grads_three + grads_four
    totals = lax.psum(local_grads, ("section", "dp"))
    return (output, input_grad) + tuple(totals)


def solution(mesh):
    return jax.shard_map(
        shards,
        mesh=mesh,
        in_specs=(
            P(("section", "dp"), None),
            P(("section", "dp"), None),
            P(None, "dp"),
            P("section"),
            P(None, "section"),
            P(None, "section"),
            P("section"),
            P(None, "section"),
            P("section", None),
            P("section"),
            P(None, "section"),
            P(None, "section"),
            P(None, "section"),
            P("section"),
            P(None, "section"),
            P("section", None),
        ),
        out_specs=(
            P(("section", "dp"), None),
            P(("section", "dp"), None),
            P(),
            P(),
            P(),
            P(),
            P(),
            P(),
            P(),
            P(),
            P(),
            P(),
            P(),
            P(),
            P(),
        ),
        check_vma=False,
    )
```

profile of v0, /device:TPU:0, one launch (start us, length us, event | category | flops | bytes accessed | tf_op | source)
XLA Modules:
  0.0 931.1 jit_solution(3867599863265053190)
XLA Ops:
  10.3 16.5 %all_gather.45 = bf16[1024,384]{1,0:T(8,128)(2,1)S(1)} all-gather(bf16[256,384]{1,0:T(8,128)(2,1)} %param.219), channel_id=1, replica_groups=mesh['section'=4,'dp'=8] {'section'}, dimensions={0}, use_global_device_ids=true | all-gather | bytes 983040 | tf_op jit(solution)/shard_map/all_gather | solution.py:292
  26.8 8.8 all_gather.48
  37.9 9.9 %all-reduce.7 = (bf16[384]{0:T(512)(128)(2,1)S(1)}, bf16[384]{0:T(512)(128)(2,1)S(1)}, bf16[384]{0:T(512)(128)(2,1)S(1)}, bf16[384]{0:T(512)(128)(2,1)S(1)}) all-reduce(bf16[384]{0:T(512)(128)(2,1)S(1)} %dynamic-update-slice.56, bf16[384]{0:T(512)(128)(2,1)S(1)} %dynamic-update-slice.57, ...), channel_id=1, replica_groups=mesh['section'=4,'dp'=8] {'section'}, use_global_device_ids=true, to_apply=%add.1 | all-reduce | flops 1536 | bytes 6144
  48.9 14.5 %all_gather.47 = bf16[384,1152]{0,1:T(8,128)(2,1)S(1)} all-gather(bf16[384,288]{0,1:T(8,128)(2,1)S(1)} %copy-done.235), channel_id=1, replica_groups=mesh['section'=4,'dp'=8] {'section'}, dimensions={1}, use_global_device_ids=true | all-gather | bytes 1105920 | tf_op jit(solution)/shard_map/all_gather | solution.py:295
  63.5 8.3 all_gather.53
  71.7 9.6 %all_gather.55 = bf16[384,384]{0,1:T(8,128)(2,1)S(1)} all-gather(bf16[384,96]{0,1:T(8,128)(2,1)S(1)} %copy-done.255), channel_id=1, replica_groups=mesh['section'=4,'dp'=8] {'section'}, dimensions={1}, use_global_device_ids=true | all-gather | bytes 368640 | tf_op jit(solution)/shard_map/all_gather | solution.py:303
  81.3 12.1 %all_gather.54 = bf16[384,768]{0,1:T(8,128)(2,1)S(1)} all-gather(bf16[384,192]{0,1:T(8,128)(2,1)} %param.229), channel_id=1, replica_groups=mesh['section'=4,'dp'=8] {'section'}, dimensions={1}, use_global_device_ids=true | all-gather | bytes 737280 | tf_op jit(solution)/shard_map/all_gather | solution.py:301
  100.8 11.8 %all_gather.59 = bf16[1024,384]{1,0:T(8,128)(2,1)S(1)} all-gather(bf16[256,384]{1,0:T(8,128)(2,1)S(1)} %copy-done.247), channel_id=1, replica_groups=mesh['section'=4,'dp'=8] {'section'}, dimensions={0}, use_global_device_ids=true | all-gather | bytes 983040 | tf_op jit(solution)/shard_map/all_gather | solution.py:293
  114.4 21.7 %all-gather.11.cloned.1.call-done = bf16[1536,384]{1,0:T(8,128)(2,1)} async-done(((bf16[384,384]{1,0:T(8,128)(2,1)}), bf16[1536,384]{1,0:T(8,128)(2,1)}) %all-gather.11.cloned.1.call-update) | async-done | bytes 1179664 | tf_op jit(solution)/shard_map/all_gather | solution.py:306
  136.1 11.9 %conditional.35 = (bf16[256,384]{1,0:T(8,128)(2,1)}, bf16[256,192]{1,0:T(8,128)(2,1)S(1)}, f32[6,256]{1,0:T(8,128)S(1)}, bf16[256,384]{1,0:T(8,128)(2,1)S(1)}) conditional(s32[]{:T(128)} %clamp.21, (bf16[256,384]{1,0:T(8,128)(2,1)S(1)}, f32[384]{0:T(512)S(1)}, bf16[384,1152]{0,1:T(8,128)(2,1)S(1)}, s32[]{:T(128)}, ...), branch_computations={%region_0.5_spmd, %region_5.8_spmd, %region_8.13_spmd, %region_13.... | conditional | flops 608895232 | bytes 14740572 | solution.py:358
  163.2 14.8 %conditional.36 = (bf16[256,384]{1,0:T(8,128)(2,1)}, bf16[256,192]{0,1:T(8,128)(2,1)}, f32[6,256]{1,0:T(8,128)S(1)}, bf16[256,384]{1,0:T(8,128)(2,1)}) conditional(s32[]{:T(128)} %clamp.22, (bf16[256,384]{1,0:T(8,128)(2,1)S(1)}, f32[384]{0:T(512)S(1)}, bf16[384,1152]{0,1:T(8,128)(2,1)S(1)}, s32[]{:T(128)}, ...), branch_computations={%region_17.22_spmd, %region_22.25_spmd, %region_25.30_spmd, %regio... | conditional | flops 608895232 | bytes 17460424 | solution.py:358
  194.2 15.0 %conditional.37 = (bf16[256,384]{1,0:T(8,128)(2,1)}, bf16[256,192]{0,1:T(8,128)(2,1)}, f32[6,256]{1,0:T(8,128)S(1)}, bf16[256,384]{1,0:T(8,128)(2,1)}) conditional(s32[]{:T(128)} %clamp.23, (bf16[256,384]{1,0:T(8,128)(2,1)S(1)}, f32[384]{0:T(512)S(1)}, bf16[384,1152]{0,1:T(8,128)(2,1)S(1)}, s32[]{:T(128)}, ...), branch_computations={%region_34.39_spmd, %region_39.42_spmd, %region_42.47_spmd, %regio... | conditional | flops 608895232 | bytes 17460424 | solution.py:358
  225.5 14.8 %conditional.38 = (bf16[256,384]{1,0:T(8,128)(2,1)}, bf16[256,192]{0,1:T(8,128)(2,1)}, f32[6,256]{1,0:T(8,128)S(1)}, bf16[256,384]{1,0:T(8,128)(2,1)}) conditional(s32[]{:T(128)} %clamp.24, (bf16[256,384]{1,0:T(8,128)(2,1)S(1)}, f32[384]{0:T(512)S(1)}, bf16[384,1152]{0,1:T(8,128)(2,1)S(1)}, s32[]{:T(128)}, ...), branch_computations={%region_51.56_spmd, %region_56.59_spmd, %region_59.64_spmd, %regio... | conditional | flops 608895232 | bytes 17460424 | solution.py:358
  258.7 5.1 collective-permute-start.8
  280.6 7.3 collective-permute-start.11
  302.7 4.4 conditional.45
  307.1 4.1 conditional.44
  327.6 4.6 collective-permute-done.13
  336.5 5.8 conditional.46
  352.2 5.5 collective-permute-done.15
  363.2 5.6 conditional.50
  378.5 43.0 %collective-permute-done.17 = bf16[256,192]{1,0:T(8,128)(2,1)S(1)} collective-permute-done((bf16[256,192]{1,0:T(8,128)(2,1)S(1)}, bf16[256,192]{1,0:T(8,128)(2,1)S(1)}, u32[]{:S(2)}, u32[]{:S(2)}) %collective-permute-start.17) | collective-permute-done | bytes 98336 | tf_op jit(solution)/shard_map/ppermute | solution.py:25
  426.0 36.2 %conditional.54 = (f32[256,384]{1,0:T(8,128)}, f32[384]{0:T(512)S(1)}, f32[384,1152]{1,0:T(8,128)}, f32[384,384]{1,0:T(8,128)}) conditional(s32[]{:T(128)} %convert_element_type.1293, (f32[384]{0:T(512)S(1)}, f32[384,1152]{1,0:T(8,128)}, f32[384,384]{1,0:T(8,128)}) %tuple.636, (f32[256,384]{1,0:T(8,128)S(1)}, f32[384]{0:T(512)S(1)}, ...), branch_computations={%region_210.211_spmd, %region_211.218_spmd} | conditional | flops 1094943232 | bytes 48577484 | solution.py:419
  457.7 3.4 convolution_add_fusion.49
  471.4 4.6 collective-permute-done.19
  481.1 36.2 %conditional.58 = (f32[256,384]{1,0:T(8,128)}, f32[384]{0:T(512)S(1)}, f32[384,1152]{1,0:T(8,128)}, f32[384,384]{1,0:T(8,128)}) conditional(s32[]{:T(128)} %convert_element_type.1304, (f32[384]{0:T(512)S(1)}, f32[384,1152]{1,0:T(8,128)}, f32[384,384]{1,0:T(8,128)}) %tuple.644, (f32[256,384]{1,0:T(8,128)S(1)}, f32[384]{0:T(512)S(1)}, ...), branch_computations={%region_240.241_spmd, %region_241.248_spmd} | conditional | flops 1094943232 | bytes 48577484 | solution.py:419
  526.8 4.6 collective-permute-done.21
  536.4 36.0 %conditional.62 = (f32[256,384]{1,0:T(8,128)}, f32[384]{0:T(512)S(1)}, f32[384,1152]{1,0:T(8,128)}, f32[384,384]{1,0:T(8,128)}) conditional(s32[]{:T(128)} %convert_element_type.1315, (f32[384]{0:T(512)S(1)}, f32[384,1152]{1,0:T(8,128)}, f32[384,384]{1,0:T(8,128)}) %tuple.652, (f32[256,384]{1,0:T(8,128)S(1)}, f32[384]{0:T(512)S(1)}, ...), branch_computations={%region_270.271_spmd, %region_271.278_spmd} | conditional | flops 1094943232 | bytes 48577484 | solution.py:419
  581.8 4.2 collective-permute-done.23
  590.4 25.8 %conditional.66 = (f32[256,384]{1,0:T(8,128)}, f32[384]{0:T(512)S(1)}, f32[384,1152]{1,0:T(8,128)}, f32[384,384]{1,0:T(8,128)}) conditional(s32[]{:T(128)} %convert_element_type.1326, (f32[384]{0:T(512)S(1)}, f32[384,1152]{1,0:T(8,128)}, f32[384,384]{1,0:T(8,128)}) %tuple.660, (f32[256,384]{1,0:T(8,128)S(1)}, f32[384]{0:T(512)S(1)}, ...), branch_computations={%region_300.301_spmd, %region_301.308_spmd} | conditional | flops 1094943232 | bytes 46201636 | solution.py:419
  620.0 39.4 %all-reduce.5 = (f32[384]{0:T(512)}, f32[384]{0:T(512)}, f32[384]{0:T(512)}, f32[384]{0:T(512)}) all-reduce(f32[384]{0:T(512)S(1)} %get-tuple-element.2661, f32[384]{0:T(512)S(1)} %get-tuple-element.2664, f32[384]{0:T(512)S(1)} %get-tuple-element.2667, ...), channel_id=1, replica_groups=mesh['section'=4,'dp'=8] {'section','dp'}, use_global_device_ids=true, to_apply=%region_331.332 | all-reduce | flops 1536 | bytes 12288 | tf_op jit(solution)/shard_map/psum | solution.py:453
  662.8 246.4 %all-reduce.10.cloned.1.call-done = (f32[384,1152]{1,0:T(8,128)}, f32[384,384]{1,0:T(8,128)}, f32[384,1536]{1,0:T(8,128)}, f32[1536,384]{1,0:T(8,128)}, f32[384,...) async-done(((f32[384,1152]{1,0:T(8,128)}, f32[384,384]{1,0:T(8,128)}, f32[384,1536]{1,0:T(8,128)}, ...) | async-done | bytes 13860880 | tf_op jit(solution)/shard_map/psum | solution.py:453
  (754 shorter events, 423.7 us)
Async XLA Ops:
  7.3 107.1 %all-gather.5.cloned.1.call-start = ((), (), s32[]{:S(2)}) async-start(), calls=%async_computation.2 | async-start | bytes 1474560 | tf_op jit(solution)/shard_map/all_gather | solution.py:298
  8.0 106.4 %all-gather.7.cloned.1.call-start = ((), (), s32[]{:S(2)}) async-start(), calls=%async_computation.3 | async-start | bytes 1474560 | tf_op jit(solution)/shard_map/all_gather | solution.py:299
  8.7 105.6 %all-gather.9.cloned.1.call-start = ((), (), s32[]{:S(2)}) async-start(), calls=%async_computation.4 | async-start | bytes 1474560 | tf_op jit(solution)/shard_map/all_gather | solution.py:305
  9.5 126.6 %all-gather.11.cloned.1.call-start = ((), (), s32[]{:S(2)}) async-start(), calls=%async_computation.5 | async-start | bytes 1474560 | tf_op jit(solution)/shard_map/all_gather | solution.py:306
  10.1 649.3 %reduce-scatter.3.cloned.1.call-start = ((), (), s32[]{:S(2)}) async-start(), calls=%async_computation.6 | async-start | bytes 983040 | tf_op jit(solution)/shard_map/reduce_scatter | solution.py:439
  71.7 205.7 %copy-start.39 = (bf16[384,192]{0,1:T(8,128)(2,1)}, bf16[384,192]{0,1:T(8,128)(2,1)S(1)}, u32[]{:S(2)}) copy-start(bf16[384,192]{0,1:T(8,128)(2,1)S(1)} %all_gather.53) | copy-start | bytes 442372
  148.0 11.8 %collective-permute-start = (bf16[256,384]{1,0:T(8,128)(2,1)}, bf16[256,384]{1,0:T(8,128)(2,1)}, u32[]{:S(2)}, u32[]{:S(2)}) collective-permute-start(bf16[256,384]{1,0:T(8,128)(2,1)} %get-tuple-element.2517), channel_id=1, source_target_pairs={{0,8},{8,16},{16,24},{1,9},{9,17},{17,25},{2,10},{10,18},{18,26},{... | collective-permute-start | bytes 589832 | tf_op jit(solution)/shard_map/ppermute | solution.py:25
  150.7 6.9 collective-permute-start.1
  178.0 12.9 %collective-permute-start.2 = (bf16[256,384]{1,0:T(8,128)(2,1)}, bf16[256,384]{1,0:T(8,128)(2,1)S(1)}, u32[]{:S(2)}, u32[]{:S(2)}) collective-permute-start(bf16[256,384]{1,0:T(8,128)(2,1)} %get-tuple-element.2519), channel_id=1, source_target_pairs={{0,8},{8,16},{16,24},{1,9},{9,17},{17,25},{2,10},{10,18},{18,26},{... | collective-permute-start | bytes 589832 | tf_op jit(solution)/shard_map/ppermute | solution.py:25
  179.4 9.3 collective-permute-start.3
  209.3 12.9 %collective-permute-start.4 = (bf16[256,384]{1,0:T(8,128)(2,1)}, bf16[256,384]{1,0:T(8,128)(2,1)S(1)}, u32[]{:S(2)}, u32[]{:S(2)}) collective-permute-start(bf16[256,384]{1,0:T(8,128)(2,1)} %get-tuple-element.2521), channel_id=1, source_target_pairs={{0,8},{8,16},{16,24},{1,9},{9,17},{17,25},{2,10},{10,18},{18,26},{... | collective-permute-start | bytes 589832 | tf_op jit(solution)/shard_map/ppermute | solution.py:25
  210.7 9.3 collective-permute-start.5
  240.2 13.1 %collective-permute-start.6 = (bf16[256,384]{1,0:T(8,128)(2,1)}, bf16[256,384]{1,0:T(8,128)(2,1)S(1)}, u32[]{:S(2)}, u32[]{:S(2)}) collective-permute-start(bf16[256,384]{1,0:T(8,128)(2,1)} %get-tuple-element.2523), channel_id=1, source_target_pairs={{0,8},{8,16},{16,24},{1,9},{9,17},{17,25},{2,10},{10,18},{18,26},{... | collective-permute-start | bytes 589832 | tf_op jit(solution)/shard_map/ppermute | solution.py:25
  241.7 9.4 %collective-permute-start.7 = (bf16[256,192]{0,1:T(8,128)(2,1)}, bf16[256,192]{0,1:T(8,128)(2,1)S(1)}, u32[]{:S(2)}, u32[]{:S(2)}) collective-permute-start(bf16[256,192]{0,1:T(8,128)(2,1)} %get-tuple-element.2524), channel_id=1, source_target_pairs={{0,8},{8,16},{16,24},{1,9},{9,17},{17,25},{2,10},{10,18},{18,26},{... | collective-permute-start | bytes 294920 | tf_op jit(solution)/shard_map/ppermute | solution.py:25
  258.7 15.5 %collective-permute-start.8 = (bf16[256,384]{1,0:T(8,128)(2,1)}, bf16[256,384]{1,0:T(8,128)(2,1)S(1)}, u32[]{:S(2)}, u32[]{:S(2)}) collective-permute-start(bf16[256,384]{1,0:T(8,128)(2,1)} %get-tuple-element.2525), channel_id=1, source_target_pairs={{0,8},{8,16},{16,24},{1,9},{9,17},{17,25},{2,10},{10,18},{18,26},{... | collective-permute-start | bytes 589832 | tf_op jit(solution)/shard_map/ppermute | solution.py:25
  263.8 8.2 collective-permute-start.9
  278.4 14.4 %collective-permute-start.10 = (bf16[256,384]{1,0:T(8,128)(2,1)S(1)}, bf16[256,384]{1,0:T(8,128)(2,1)S(1)}, u32[]{:S(2)}, u32[]{:S(2)}) collective-permute-start(bf16[256,384]{1,0:T(8,128)(2,1)S(1)} %get-tuple-element.2527), channel_id=1, source_target_pairs={{0,8},{8,16},{16,24},{1,9},{9,17},{17,25},{2,10},{10,18},{18,26},{... | collective-permute-start | bytes 589832 | tf_op jit(solution)/shard_map/ppermute | solution.py:25
  280.6 10.7 %collective-permute-start.11 = (bf16[256,192]{0,1:T(8,128)(2,1)}, bf16[256,192]{0,1:T(8,128)(2,1)S(1)}, u32[]{:S(2)}, u32[]{:S(2)}) collective-permute-start(bf16[256,192]{0,1:T(8,128)(2,1)} %copy-done.249), channel_id=1, source_target_pairs={{0,8},{8,16},{16,24},{1,9},{9,17},{17,25},{2,10},{10,18},{18,26},{... | collective-permute-start | bytes 294920 | tf_op jit(solution)/shard_map/ppermute | solution.py:25
  320.8 12.2 %collective-permute-start.12 = (bf16[256,384]{1,0:T(8,128)(2,1)}, bf16[256,384]{1,0:T(8,128)(2,1)}, u32[]{:S(2)}, u32[]{:S(2)}) collective-permute-start(bf16[256,384]{1,0:T(8,128)(2,1)} %get-tuple-element.3270), channel_id=1, source_target_pairs={{8,0},{16,8},{24,16},{9,1},{17,9},{25,17},{10,2},{18,10},{26,18},{... | collective-permute-start | bytes 589832 | tf_op jit(solution)/shard_map/ppermute | solution.py:25
  324.7 7.5 collective-permute-start.13
  346.1 12.9 %collective-permute-start.14 = (bf16[256,384]{1,0:T(8,128)(2,1)S(1)}, bf16[256,384]{1,0:T(8,128)(2,1)S(1)}, u32[]{:S(2)}, u32[]{:S(2)}) collective-permute-start(bf16[256,384]{1,0:T(8,128)(2,1)S(1)} %get-tuple-element.3268), channel_id=1, source_target_pairs={{8,0},{16,8},{24,16},{9,1},{17,9},{25,17},{10,2},{18,10},{26,18},{... | collective-permute-start | bytes 589832 | tf_op jit(solution)/shard_map/ppermute | solution.py:25
  349.2 8.4 collective-permute-start.15
  371.7 50.6 %collective-permute-start.16 = (bf16[256,384]{1,0:T(8,128)(2,1)S(1)}, bf16[256,384]{1,0:T(8,128)(2,1)S(1)}, u32[]{:S(2)}, u32[]{:S(2)}) collective-permute-start(bf16[256,384]{1,0:T(8,128)(2,1)S(1)} %get-tuple-element.3266), channel_id=1, source_target_pairs={{8,0},{16,8},{24,16},{9,1},{17,9},{25,17},{10,2},{18,10},{26,18},{... | collective-permute-start | bytes 589832 | tf_op jit(solution)/shard_map/ppermute | solution.py:25
  375.6 46.0 %collective-permute-start.17 = (bf16[256,192]{1,0:T(8,128)(2,1)S(1)}, bf16[256,192]{1,0:T(8,128)(2,1)S(1)}, u32[]{:S(2)}, u32[]{:S(2)}) collective-permute-start(bf16[256,192]{1,0:T(8,128)(2,1)S(1)} %add.1764), channel_id=1, source_target_pairs={{8,0},{16,8},{24,16},{9,1},{17,9},{25,17},{10,2},{18,10},{26,18},{... | collective-permute-start | bytes 294920 | tf_op jit(solution)/shard_map/ppermute | solution.py:25
  465.2 11.5 %collective-permute-start.18 = (bf16[256,384]{1,0:T(8,128)(2,1)}, bf16[256,384]{1,0:T(8,128)(2,1)}, u32[]{:S(2)}, u32[]{:S(2)}) collective-permute-start(bf16[256,384]{1,0:T(8,128)(2,1)} %get-tuple-element.3264), channel_id=1, source_target_pairs={{8,0},{16,8},{24,16},{9,1},{17,9},{25,17},{10,2},{18,10},{26,18},{... | collective-permute-start | bytes 589832 | tf_op jit(solution)/shard_map/ppermute | solution.py:25
  467.4 193.7 %reduce-scatter.5.cloned.1.call-start = ((), (), s32[]{:S(2)}) async-start(), calls=%async_computation.7 | async-start | bytes 983040 | tf_op jit(solution)/shard_map/reduce_scatter | solution.py:445
  468.5 7.5 collective-permute-start.19
  521.0 11.1 %collective-permute-start.20 = (bf16[256,384]{1,0:T(8,128)(2,1)S(1)}, bf16[256,384]{1,0:T(8,128)(2,1)S(1)}, u32[]{:S(2)}, u32[]{:S(2)}) collective-permute-start(bf16[256,384]{1,0:T(8,128)(2,1)S(1)} %get-tuple-element.3262), channel_id=1, source_target_pairs={{8,0},{16,8},{24,16},{9,1},{17,9},{25,17},{10,2},{18,10},{26,18},{... | collective-permute-start | bytes 589832 | tf_op jit(solution)/shard_map/ppermute | solution.py:25
  523.9 7.5 collective-permute-start.21
  576.0 10.7 %collective-permute-start.22 = (bf16[256,384]{1,0:T(8,128)(2,1)S(1)}, bf16[256,384]{1,0:T(8,128)(2,1)S(1)}, u32[]{:S(2)}, u32[]{:S(2)}) collective-permute-start(bf16[256,384]{1,0:T(8,128)(2,1)S(1)} %get-tuple-element.3260), channel_id=1, source_target_pairs={{8,0},{16,8},{24,16},{9,1},{17,9},{25,17},{10,2},{18,10},{26,18},{... | collective-permute-start | bytes 589832 | tf_op jit(solution)/shard_map/ppermute | solution.py:25
  578.9 7.1 collective-permute-start.23
  619.2 290.0 %all-reduce.10.cloned.1.call-start = ((), (), s32[]{:S(2)}) async-start(), calls=%async_computation.8 | async-start | bytes 27721728 | tf_op jit(solution)/shard_map/psum | solution.py:453
  (144 other events, 1201.3 us)
Sparse Core Ops, SparseCore 0:
  9.9 32.0 all-gather.4
  43.9 32.0 all-gather.6
  77.8 29.3 all-gather.8
  108.9 27.1 all-gather.10
  467.5 33.4 reduce-scatter.2
  619.3 25.1 reduce-scatter.4
  652.1 257.0 all-reduce.9
where the time goes:
time: 944 us; the launch traced here: 931 us
  waiting for transfers between devices  338 us (36%)
  local copies, waits for them, and re-layouts  195 us (21%)
  blocking collectives  131 us (14%)
  other arithmetic  109 us (12%)
  matrix products  59.7 us (6%)
  starting transfers between devices  44.3 us (5%)
  loops' own time  37.3 us (4%)
  between operations  16.3 us (2%)
    psum x1, waiting for transfers between devices, shards(): totals = lax.psum(local_grads, ('section', 'dp'))  246 us
    ppermute x24, waiting for transfers between devices, from_behind(): lax.ppermute(value, axis, [(source, source + steps) for source in range(l...  66.5 us
    dynamic_update_slice x41, other arithmetic, keep_slot(): lax.dynamic_update_index_in_dim(buffer, jnp.where(active, fresh_value, pr...  55.8 us
    dynamic_slice x30, local copies, waits for them, and re-layouts, keep_slot(): previous = lax.dynamic_index_in_dim(buffer, slot_index, 0, False)  45.5 us
    ppermute x24, starting transfers between devices, from_behind(): lax.ppermute(value, axis, [(source, source + steps) for source in range(l...  44.1 us
    psum x1, blocking collectives, shards(): totals = lax.psum(local_grads, ('section', 'dp'))  39.4 us
    another operation x7, loops' own time, shards(): lax.cond(active & (section_index == 0), back_first, skip_section, grads_one)  34.1 us
    unnamed x160, local copies, waits for them, and re-layouts  24.7 us
  transfers between devices with their start and end apart: 31, of which 8 were waited for; matrix products, arithmetic and copies ran while one was open for 19% of the time, Pallas kernels for 0%

commit v1 on v0

--- a/solution.py
+++ b/solution.py
@@ -240,31 +240,8 @@
     )
 
 
-def unpack(weights):
-    part_one = (weights[0].astype(jnp.float32), weights[1], weights[2])
-    part_two = (weights[3].astype(jnp.float32), weights[4], weights[5])
-    part_three = (weights[6].astype(jnp.float32), weights[7], weights[8], weights[9])
-    part_four = (weights[10].astype(jnp.float32), weights[11], weights[12])
-    return (part_one, part_two, part_three, part_four)
-
-
-def take_slot(buffer, slot_index):
-    return lax.dynamic_index_in_dim(buffer, slot_index, 0, False)
-
-
-def keep_slot(buffer, fresh_value, slot_index, active):
-    previous = lax.dynamic_index_in_dim(buffer, slot_index, 0, False)
-    return lax.dynamic_update_index_in_dim(
-        buffer, jnp.where(active, fresh_value, previous), slot_index, 0
-    )
-
-
-def add_up(running, fresh_grads):
-    return tuple((total + extra for total, extra in zip(running, fresh_grads)))
-
-
-def zero_grads(members):
-    return tuple((jnp.zeros(member.shape, jnp.float32) for member in members))
+def gathered(shard, axis):
+    return lax.all_gather(shard, "section", axis=axis, tiled=True)
 
 
 def shards(
@@ -285,173 +262,51 @@
     up_four,
     down_four,
 ):
-    row_count = tokens.shape[0]
-    local_lengths = lengths[:, 0]
     section_index = lax.axis_index("section")
-    gathered = (
-        lax.all_gather(tokens, "section", axis=0, tiled=True),
-        lax.all_gather(cotangent, "section", axis=0, tiled=True),
-        lax.all_gather(gain_one, "section", axis=0, tiled=True),
-        lax.all_gather(mixing_one, "section", axis=1, tiled=True),
-        lax.all_gather(output_one, "section", axis=1, tiled=True),
-        lax.all_gather(gain_two, "section", axis=0, tiled=True),
-        lax.all_gather(up_two, "section", axis=1, tiled=True),
-        lax.all_gather(down_two, "section", axis=0, tiled=True),
-        lax.all_gather(gain_three, "section", axis=0, tiled=True),
-        lax.all_gather(pair_three, "section", axis=1, tiled=True),
-        lax.all_gather(fresh_three, "section", axis=1, tiled=True),
-        lax.all_gather(output_three, "section", axis=1, tiled=True),
-        lax.all_gather(gain_four, "section", axis=0, tiled=True),
-        lax.all_gather(up_four, "section", axis=1, tiled=True),
-        lax.all_gather(down_four, "section", axis=0, tiled=True),
-    )
-    section_count = lax.axis_size("section")
-    last_section = section_count - 1
-    token_all = gathered[0].reshape(section_count, row_count, D)
-    seed_all = gathered[1].reshape(section_count, row_count, D)
-    part_one, part_two, part_three, part_four = unpack(gathered[2:])
-    shared_width = SHARED * HEAD
-    zero_rows = jnp.zeros((row_count, D), jnp.float32)
-    zero_attended = jnp.zeros((row_count, D), jnp.bfloat16)
-    zero_sums = jnp.zeros((HEADS, row_count), jnp.float32)
-    zero_values = jnp.zeros((row_count, shared_width), jnp.bfloat16)
-
-    def run_first(section_entry, value_in, length):
-        return first_forward(section_entry.astype(jnp.float32), length, *part_one)
-
-    def run_second(section_entry, value_in, length):
-        return (
-            feed_forward(section_entry.astype(jnp.float32), *part_two),
-            value_in,
-            zero_attended,
-            zero_sums,
-        )
-
-    def run_third(section_entry, value_in, length):
-        return third_forward(section_entry.astype(jnp.float32), length, value_in, *part_three)
-
-    def run_fourth(section_entry, value_in, length):
-        return (
-            feed_forward(section_entry.astype(jnp.float32), *part_four),
-            value_in,
-            zero_attended,
-            zero_sums,
-        )
-
-    def run_spare(section_entry, value_in, length):
-        return (zero_rows, value_in, zero_attended, zero_sums)
-
-    stash_in = jnp.zeros((section_count, row_count, D), jnp.bfloat16)
-    stash_attended = jnp.zeros((section_count, row_count, D), jnp.bfloat16)
-    stash_sums = jnp.zeros((section_count, HEADS, row_count), jnp.float32)
-    stash_values = jnp.zeros((section_count, row_count, shared_width), jnp.bfloat16)
-    results = jnp.zeros((section_count, row_count, D), jnp.float32)
-    incoming = zero_attended
-    carried = zero_values
-    for tick_index in range(2 * section_count - 1):
-        micro_slot = tick_index - section_index
-        active = (micro_slot >= 0) & (micro_slot < section_count)
-        slot_index = jnp.clip(micro_slot, 0, last_section)
-        length = local_lengths[slot_index]
-        section_entry = jnp.where(section_index == 0, take_slot(token_all, slot_index), incoming)
-        value_in = carried
-        result, value_out, attended, log_sums = lax.switch(
-            jnp.where(active, section_index, 4),
-            [run_first, run_second, run_third, run_fourth, run_spare],
-            section_entry,
-            value_in,
-            length,
-        )
-        stash_in = keep_slot(stash_in, section_entry, slot_index, active)
-        stash_attended = keep_slot(stash_attended, attended, slot_index, active)
-        stash_sums = keep_slot(stash_sums, log_sums, slot_index, active)
-        stash_values = keep_slot(stash_values, value_in, slot_index, active)
-        results = keep_slot(results, result, slot_index, active & (section_index == last_section))
-        outgoing = result.astype(jnp.bfloat16)
-        incoming, carried = (
-            from_behind(outgoing, "section", 1),
-            from_behind(shortened(value_out), "section", 1).astype(value_out.dtype),
-        )
-    grads_one = zero_grads(part_one)
-    grads_two = zero_grads(part_two)
-    grads_three = zero_grads(part_three)
-    grads_four = zero_grads(part_four)
-    grad_results = jnp.zeros((section_count, row_count, D), jnp.float32)
-    back_in = zero_attended
-    back_values = zero_values
-    for tick_index in range(2 * section_count - 1):
-        micro_slot = tick_index - last_section + section_index
-        active = (micro_slot >= 0) & (micro_slot < section_count)
-        slot_index = jnp.clip(micro_slot, 0, last_section)
-        length = local_lengths[slot_index]
-        valid_rows = (jnp.arange(row_count) < length)[:, None]
-        seeded = jnp.where(valid_rows, take_slot(seed_all, slot_index).astype(jnp.float32), 0.0)
-        grad_now = jnp.where(section_index == last_section, seeded, back_in.astype(jnp.float32))
-        grad_shared = back_values.astype(jnp.float32)
-        section_entry = take_slot(stash_in, slot_index).astype(jnp.float32)
-        attended = take_slot(stash_attended, slot_index)
-        log_sums = take_slot(stash_sums, slot_index)
-        shared = take_slot(stash_values, slot_index)
-
-        def back_first(running):
-            grad_in, fresh_grads = first_backward(
-                section_entry, length, attended, log_sums, grad_now, grad_shared, *part_one
-            )
-            return (grad_in, zero_values, add_up(running, fresh_grads))
-
-        def back_second(running):
-            grad_in, fresh_grads = feed_backward(section_entry, grad_now, *part_two)
-            return (grad_in, back_values, add_up(running, fresh_grads))
-
-        def back_third(running):
-            grad_in, shared_grad, fresh_grads = third_backward(
-                section_entry, length, shared, attended, log_sums, grad_now, *part_three
-            )
-            return (grad_in, shared_grad, add_up(running, fresh_grads))
-
-        def back_fourth(running):
-            grad_in, fresh_grads = feed_backward(section_entry, grad_now, *part_four)
-            return (grad_in, zero_values, add_up(running, fresh_grads))
-
-        def skip_section(running):
-            return (zero_rows, zero_values, running)
-
-        entry_one, values_one, grads_one = lax.cond(
-            active & (section_index == 0), back_first, skip_section, grads_one
-        )
-        entry_two, values_two, grads_two = lax.cond(
-            active & (section_index == 1), back_second, skip_section, grads_two
-        )
-        entry_three, values_three, grads_three = lax.cond(
-            active & (section_index == 2), back_third, skip_section, grads_three
-        )
-        entry_four, values_four, grads_four = lax.cond(
-            active & (section_index == 3), back_fourth, skip_section, grads_four
-        )
-        grad_entry = entry_one + entry_two + entry_three + entry_four
-        value_grad = values_one + values_two + values_three + values_four
-        grad_results = keep_slot(
-            grad_results, grad_entry, slot_index, active & (section_index == 0)
-        )
-        outgoing = grad_entry.astype(jnp.bfloat16)
-        back_in, back_values = from_behind((outgoing, value_grad), "section", -1)
-    output, input_grad = (
-        lax.psum_scatter(
-            results.reshape(section_count * row_count, D).astype(jnp.bfloat16),
-            "section",
-            scatter_dimension=0,
-            tiled=True,
-        ).astype(jnp.float32),
-        lax.psum_scatter(
-            grad_results.reshape(section_count * row_count, D).astype(jnp.bfloat16),
-            "section",
-            scatter_dimension=0,
-            tiled=True,
-        ).astype(jnp.float32),
-    )
-    local_grads = grads_one + grads_two + grads_three + grads_four
-    totals = lax.psum(local_grads, ("section", "dp"))
-    return (output, input_grad) + tuple(totals)
+    length = lengths[section_index, 0]
+    gains = lax.all_gather(
+        jnp.stack([gain_one, gain_two, gain_three, gain_four]), "section", axis=1, tiled=True
+    ).astype(jnp.float32)
+    part_one = (gains[0], gathered(mixing_one, 1), gathered(output_one, 1))
+    part_two = (gains[1], gathered(up_two, 1), gathered(down_two, 0))
+    part_three = (
+        gains[2],
+        gathered(pair_three, 1),
+        gathered(fresh_three, 1),
+        gathered(output_three, 1),
+    )
+    part_four = (gains[3], gathered(up_four, 1), gathered(down_four, 0))
+
+    entry = tokens.astype(jnp.float32)
+    h1, shared, attended_one, sums_one = first_forward(entry, length, *part_one)
+    h1 = h1.astype(jnp.bfloat16).astype(jnp.float32)
+    h2 = feed_forward(h1, *part_two).astype(jnp.bfloat16).astype(jnp.float32)
+    h3, _, attended_three, sums_three = third_forward(h2, length, shared, *part_three)
+    h3 = h3.astype(jnp.bfloat16).astype(jnp.float32)
+    output = feed_forward(h3, *part_four)
+
+    valid_rows = (jnp.arange(tokens.shape[0]) < length)[:, None]
+    seeded = jnp.where(valid_rows, cotangent.astype(jnp.float32), 0.0)
+    grad_h3, grads_four = feed_backward(h3, seeded, *part_four)
+    grad_h3 = grad_h3.astype(jnp.bfloat16).astype(jnp.float32)
+    grad_h2, shared_grad, grads_three = third_backward(
+        h2, length, shared, attended_three, sums_three, grad_h3, *part_three
+    )
+    grad_h2 = grad_h2.astype(jnp.bfloat16).astype(jnp.float32)
+    grad_h1, grads_two = feed_backward(h1, grad_h2, *part_two)
+    grad_h1 = grad_h1.astype(jnp.bfloat16).astype(jnp.float32)
+    input_grad, grads_one = first_backward(
+        entry,
+        length,
+        attended_one,
+        sums_one,
+        grad_h1,
+        shared_grad.astype(jnp.float32),
+        *part_one,
+    )
+    local = shortened(grads_one + grads_two + grads_three + grads_four)
+    totals = lax.psum(local, ("section", "dp"))
+    return (output, input_grad) + tuple(total.astype(jnp.float32) for total in totals)
 
 
 def solution(mesh):

time: 944 us -> 358 us (0.38); the launches traced: 931 us -> 357 us
  local copies, waits for them, and re-layouts: 195 us -> 13.6 us
  waiting for transfers between devices: 338 us -> 158 us
  other arithmetic: 109 us -> 25.1 us
  starting transfers between devices: 44.3 us -> 0.19 us
  loops' own time: 37.3 us -> 0 us
  blocking collectives: 131 us -> 104 us
  matrix products: 59.7 us -> 41.9 us
    psum x1, waiting for transfers between devices: 246 us -> 120 us  [shards(): totals = lax.psum(local, ('section', 'dp'))]
    ppermute x24 -> x0, waiting for transfers between devices: 66.5 us -> none  [from_behind(): lax.ppermute(value, axis, [(source, source + steps) for source in range(l...]
    dynamic_update_slice x41 -> x0, other arithmetic: 55.8 us -> none  [keep_slot(): lax.dynamic_update_index_in_dim(buffer, jnp.where(active, fresh_value, pr...]
    dynamic_slice x31 -> x1, local copies, waits for them, and re-layouts: 46.2 us -> 0.63 us  [shards(): length = lengths[section_index, 0]]
    ppermute x24 -> x0, starting transfers between devices: 44.1 us -> none  [from_behind(): lax.ppermute(value, axis, [(source, source + steps) for source in range(l...]
    another operation x35 -> x0, loops' own time: 37.3 us -> none  [the longest x7 34.1 us: shards(): lax.cond(active & (section_index == 0), back_first, skip_section, grads_one)]
    slice x24 -> x4, local copies, waits for them, and re-layouts: 36 us -> 0.94 us  [the longest x1 0.6 us: shards(): part_four = (gains[3], gathered(up_four, 1), gathered(down_four, 0))]
    broadcast_in_dim x49 -> x0, local copies, waits for them, and re-layouts: 27.1 us -> none  [the longest x27 17.3 us: shards(): zero_rows = jnp.zeros((row_count, D), jnp.float32)]
  transfers between devices with their start and end apart: 31 -> 5, of which waited for: 8 -> 3; matrix products, arithmetic and copies ran while one was open for 19% -> 8% of each run, Pallas kernels for 0% -> 0%
where the time goes in v1:
time: 358 us; the launch traced here: 357 us
  waiting for transfers between devices  158 us (44%)
  blocking collectives  104 us (29%)
  matrix products  41.9 us (12%)
  other arithmetic  25.1 us (7%)
  between operations  15 us (4%)
  local copies, waits for them, and re-layouts  13.6 us (4%)
    psum x1, waiting for transfers between devices, shards(): totals = lax.psum(local, ('section', 'dp'))  120 us
    all_gather x5, blocking collectives, gathered(): return lax.all_gather(shard, 'section', axis=axis, tiled=True)  53.4 us
    psum x1, blocking collectives, shards(): totals = lax.psum(local, ('section', 'dp'))  40.9 us
    all_gather x4, waiting for transfers between devices, gathered(): return lax.all_gather(shard, 'section', axis=axis, tiled=True)  35.2 us
    convert_element_type x13, other arithmetic, shards(): total.astype(jnp.float32)  16.6 us
    dot_general x9, matrix products, inner_rows(): lax.dot_general(left, right, (((0,), (0,)), ((), ())), preferred_element_...  12.5 us
    dot_general x9, matrix products, product(): return jnp.dot(left, right, preferred_element_type=jnp.float32)  12.3 us
    dot_general x9, matrix products, inner_cols(): lax.dot_general(left, right, (((1,), (1,)), ((), ())), preferred_element_...  10.5 us
  transfers between devices with their start and end apart: 5, of which 3 were waited for; matrix products, arithmetic and copies ran while one was open for 8% of the time, Pallas kernels for 0%

profile of v1, /device:TPU:0, one launch (start us, length us, event | category | flops | bytes accessed | tf_op | source)
XLA Modules:
  0.0 357.3 jit_solution(11732790444954760615)
XLA Ops:
  12.9 9.5 %all-gather = bf16[4,96,4]{1,2,0:T(4,128)(2,1)S(1)} all-gather(bf16[1,96,4]{1,2,0:T(4,128)(2,1)S(1)} %maximum_bitcast_fusion), channel_id=1, replica_groups=mesh['section'=4,'dp'=8] {'section'}, dimensions={0}, use_global_device_ids=true | all-gather | bytes 3840 | tf_op jit(solution)/shard_map/all_gather | solution.py:267
  23.1 14.0 %all_gather.31 = bf16[384,1152]{0,1:T(8,128)(2,1)S(1)} all-gather(bf16[384,288]{0,1:T(8,128)(2,1)S(1)} %copy-done.54), channel_id=1, replica_groups=mesh['section'=4,'dp'=8] {'section'}, dimensions={1}, use_global_device_ids=true | all-gather | bytes 1105920 | tf_op jit(solution)/shard_map/all_gather | solution.py:244
  39.9 7.1 %all_gather.35 = bf16[384,192]{0,1:T(8,128)(2,1)S(1)} all-gather(bf16[384,48]{0,1:T(8,128)(2,1)S(1)} %copy-done.65), channel_id=1, replica_groups=mesh['section'=4,'dp'=8] {'section'}, dimensions={1}, use_global_device_ids=true | all-gather | bytes 184320 | tf_op jit(solution)/shard_map/all_gather | solution.py:244
  46.9 11.9 %all_gather.32 = bf16[384,384]{0,1:T(8,128)(2,1)S(1)} all-gather(bf16[384,96]{0,1:T(8,128)(2,1)S(1)} %copy-done.63), channel_id=1, replica_groups=mesh['section'=4,'dp'=8] {'section'}, dimensions={1}, use_global_device_ids=true | all-gather | bytes 368640 | tf_op jit(solution)/shard_map/all_gather | solution.py:244
  58.9 9.6 %all_gather.37 = bf16[384,384]{0,1:T(8,128)(2,1)} all-gather(bf16[384,96]{0,1:T(8,128)(2,1)S(1)} %copy-done.64), channel_id=1, replica_groups=mesh['section'=4,'dp'=8] {'section'}, dimensions={1}, use_global_device_ids=true | all-gather | bytes 368640 | tf_op jit(solution)/shard_map/all_gather | solution.py:244
  68.5 10.9 %all_gather.36 = bf16[384,768]{0,1:T(8,128)(2,1)S(1)} all-gather(bf16[384,192]{0,1:T(8,128)(2,1)S(1)} %copy-done.57), channel_id=1, replica_groups=mesh['section'=4,'dp'=8] {'section'}, dimensions={1}, use_global_device_ids=true | all-gather | bytes 737280 | tf_op jit(solution)/shard_map/all_gather | solution.py:244
  81.6 3.0 fusion.66
  84.7 2.6 fusion.75
  89.2 1.4 fusion.76
  94.9 10.6 %all-gather.10.cloned.1.call-done = bf16[384,1536]{1,0:T(8,128)(2,1)} async-done(((bf16[384,384]{1,0:T(8,128)(2,1)}), bf16[384,1536]{1,0:T(8,128)(2,1)}) %all-gather.10.cloned.1.call-update) | async-done | bytes 1179664 | tf_op jit(solution)/shard_map/all_gather | solution.py:244
  105.5 2.0 fusion.67
  108.7 1.8 convolution_convert_fusion.1
  110.5 24.5 %all-gather.12.cloned.1.call-done = bf16[1536,384]{1,0:T(8,128)(2,1)} async-done(((bf16[384,384]{1,0:T(8,128)(2,1)}), bf16[1536,384]{1,0:T(8,128)(2,1)}) %all-gather.12.cloned.1.call-update) | async-done | bytes 1179664 | tf_op jit(solution)/shard_map/all_gather | solution.py:244
  135.0 3.5 fusion.7
  138.5 1.6 convolution_convert_fusion.2
  144.2 1.7 copy.98
  146.0 1.4 convolution_convert_fusion.12
  153.9 1.8 convolution_convert_fusion.3
  155.7 1.6 fusion.3
  157.4 1.6 convolution_convert_fusion.4
  165.7 1.5 convolution_convert_fusion
  169.4 40.9 %all-reduce = (bf16[384]{0:T(512)(128)(2,1)S(1)}, bf16[384]{0:T(512)(128)(2,1)S(1)}, bf16[384]{0:T(512)(128)(2,1)S(1)}, bf16[384]{0:T(512)(128)(2,1)S(1)}) all-reduce(bf16[384]{0:T(512)(128)(2,1)S(1)} %get-tuple-element.101, bf16[384]{0:T(512)(128)(2,1)S(1)} %copy-done.99, ...), channel_id=1, replica_groups=mesh['section'=4,'dp'=8] {'section','dp'}, use_global_device_ids=true, to_apply=%region_23.24 | all-reduce | flops 1536 | bytes 6144 | tf_op jit(solution)/shard_map/psum | solution.py:308
  213.6 2.7 convolution_add_fusion.1
  216.3 120.0 %all-reduce.4.cloned.1.call-done = (bf16[384,1152]{1,0:T(8,128)(2,1)}, bf16[384,384]{1,0:T(8,128)(2,1)}, bf16[384,1536]{1,0:T(8,128)(2,1)}, bf16[1536,384]{1,0:T...) async-done(((bf16[384,1152]{1,0:T(8,128)(2,1)}, ...) | async-done | bytes 6930448 | tf_op jit(solution)/shard_map/psum | solution.py:308
  336.3 1.7 convert_element_type.279
  338.0 1.8 convert_element_type.267
  339.8 1.9 convert_element_type.281
  341.7 1.3 convert_element_type.265
  344.1 1.7 convert_element_type.271
  345.8 1.6 convert_element_type.273
  347.6 1.7 convert_element_type.285
  349.3 1.6 convert_element_type.287
  (306 shorter events, 41.9 us)
Async XLA Ops:
  7.2 31.2 %copy-start = (s32[4,1]{0,1:T(1,128)S(1)}, s32[4,1]{0,1:T(1,128)}, u32[]{:S(2)}) copy-start(s32[4,1]{0,1:T(1,128)} %param.34) | copy-start | bytes 52
  7.2 29.9 %copy-start.6 = (bf16[256,384]{1,0:T(8,128)(2,1)S(1)}, bf16[256,384]{1,0:T(8,128)(2,1)}, u32[]{:S(2)}) copy-start(bf16[256,384]{1,0:T(8,128)(2,1)} %param.32) | copy-start | bytes 589828
  7.2 5.6 %copy-start.100 = (bf16[96]{0:T(256)(128)(2,1)S(1)}, bf16[96]{0:T(256)(128)(2,1)}, u32[]{:S(2)}) copy-start(bf16[96]{0:T(256)(128)(2,1)} %param.45) | copy-start | bytes 580
  7.2 5.6 %copy-start.101 = (bf16[96]{0:T(256)(128)(2,1)S(1)}, bf16[96]{0:T(256)(128)(2,1)}, u32[]{:S(2)}) copy-start(bf16[96]{0:T(256)(128)(2,1)} %param.41) | copy-start | bytes 580
  7.2 5.6 %copy-start.102 = (bf16[96]{0:T(256)(128)(2,1)S(1)}, bf16[96]{0:T(256)(128)(2,1)}, u32[]{:S(2)}) copy-start(bf16[96]{0:T(256)(128)(2,1)} %param.38) | copy-start | bytes 580
  7.2 5.6 %copy-start.103 = (bf16[96]{0:T(256)(128)(2,1)S(1)}, bf16[96]{0:T(256)(128)(2,1)}, u32[]{:S(2)}) copy-start(bf16[96]{0:T(256)(128)(2,1)} %param.35) | copy-start | bytes 580
  7.2 15.8 %copy-start.54 = (bf16[384,288]{0,1:T(8,128)(2,1)S(1)}, bf16[384,288]{0,1:T(8,128)(2,1)}, u32[]{:S(2)}) copy-start(bf16[384,288]{0,1:T(8,128)(2,1)} %param.36) | copy-start | bytes 663556
  7.3 74.3 %all-gather.6.cloned.1.call-start = ((), (), s32[]{:S(2)}) async-start(), calls=%async_computation | async-start | bytes 1474560 | tf_op jit(solution)/shard_map/all_gather | solution.py:244
  8.0 76.7 %all-gather.8.cloned.1.call-start = ((), (), s32[]{:S(2)}) async-start(), calls=%async_computation.1 | async-start | bytes 1474560 | tf_op jit(solution)/shard_map/all_gather | solution.py:244
  8.7 96.8 %all-gather.10.cloned.1.call-start = ((), (), s32[]{:S(2)}) async-start(), calls=%async_computation.2 | async-start | bytes 1474560 | tf_op jit(solution)/shard_map/all_gather | solution.py:244
  9.5 125.5 %all-gather.12.cloned.1.call-start = ((), (), s32[]{:S(2)}) async-start(), calls=%async_computation.3 | async-start | bytes 1474560 | tf_op jit(solution)/shard_map/all_gather | solution.py:244
  10.1 326.2 %all-reduce.4.cloned.1.call-start = ((), (), s32[]{:S(2)}) async-start(), calls=%async_computation.4 | async-start | bytes 13860864 | tf_op jit(solution)/shard_map/psum | solution.py:308
  11.2 26.5 %copy-start.71 = (f32[256]{0:T(256)}, f32[256]{0:T(256)S(1)}, u32[]{:S(2)}) copy-start(f32[256]{0:T(256)S(1)} %broadcast_multiply_fusion.3) | copy-start | bytes 3076
  12.3 26.1 %copy-start.79 = (f32[256]{0:T(256)}, f32[256]{0:T(256)S(1)}, u32[]{:S(2)}) copy-start(f32[256]{0:T(256)S(1)} %fusion.53) | copy-start | bytes 3076
  23.1 58.5 %copy-start.66 = (f32[384]{0:T(512)}, f32[384]{0:T(512)S(1)}, u32[]{:S(2)}) copy-start(f32[384]{0:T(512)S(1)} %get-tuple-element.105) | copy-start | bytes 4612
  23.1 64.4 %copy-start.68 = (f32[384]{0:T(512)}, f32[384]{0:T(512)S(1)}, u32[]{:S(2)}) copy-start(f32[384]{0:T(512)S(1)} %get-tuple-element.104) | copy-start | bytes 4612
  37.0 9.9 %copy-start.10 = (bf16[384,1152]{0,1:T(8,128)(2,1)}, bf16[384,1152]{0,1:T(8,128)(2,1)S(1)}, u32[]{:S(2)}) copy-start(bf16[384,1152]{0,1:T(8,128)(2,1)S(1)} %all_gather.31) | copy-start | bytes 2654212
  37.1 9.9 %copy-start.63 = (bf16[384,96]{0,1:T(8,128)(2,1)S(1)}, bf16[384,96]{0,1:T(8,128)(2,1)}, u32[]{:S(2)}) copy-start(bf16[384,96]{0,1:T(8,128)(2,1)} %param.37) | copy-start | bytes 221188
  37.1 21.8 %copy-start.64 = (bf16[384,96]{0,1:T(8,128)(2,1)S(1)}, bf16[384,96]{0,1:T(8,128)(2,1)}, u32[]{:S(2)}) copy-start(bf16[384,96]{0,1:T(8,128)(2,1)} %param.44) | copy-start | bytes 221188
  37.7 42.1 %copy-start.14 = (bf16[256,1152]{0,1:T(8,128)(2,1)}, bf16[256,1152]{0,1:T(8,128)(2,1)S(1)}, u32[]{:S(2)}) copy-start(bf16[256,1152]{0,1:T(8,128)(2,1)S(1)} %convolution_convert_fusion.5) | copy-start | bytes 1769476
  37.7 30.8 %copy-start.57 = (bf16[384,192]{0,1:T(8,128)(2,1)S(1)}, bf16[384,192]{0,1:T(8,128)(2,1)}, u32[]{:S(2)}) copy-start(bf16[384,192]{0,1:T(8,128)(2,1)} %param.42) | copy-start | bytes 442372
  38.4 41.4 %copy-start.21 = (bf16[256,384]{0,1:T(8,128)(2,1)}, bf16[256,384]{0,1:T(8,128)(2,1)S(1)}, u32[]{:S(2)}) copy-start(bf16[256,384]{0,1:T(8,128)(2,1)S(1)} %get-tuple-element.126) | copy-start | bytes 589828
  38.4 41.4 %copy-start.23 = (bf16[256,384]{0,1:T(8,128)(2,1)}, bf16[256,384]{0,1:T(8,128)(2,1)S(1)}, u32[]{:S(2)}) copy-start(bf16[256,384]{0,1:T(8,128)(2,1)S(1)} %get-tuple-element.127) | copy-start | bytes 589828
  39.7 40.1 %copy-start.95 = (pred[256]{0:T(512)(128)(4,1)}, pred[256]{0:T(512)(128)(4,1)S(1)}, u32[]{:S(2)}) copy-start(pred[256]{0:T(512)(128)(4,1)S(1)} %iota_compare_fusion.1) | copy-start | bytes 772
  39.8 40.0 %copy-start.53 = (pred[256,256]{0,1:T(8,128)(4,1)}, pred[256,256]{0,1:T(8,128)(4,1)S(1)}, u32[]{:S(2)}) copy-start(pred[256,256]{0,1:T(8,128)(4,1)S(1)} %fusion.42) | copy-start | bytes 196612
  46.9 40.7 %copy-start.33 = (bf16[384,192]{0,1:T(8,128)(2,1)}, bf16[384,192]{0,1:T(8,128)(2,1)S(1)}, u32[]{:S(2)}) copy-start(bf16[384,192]{0,1:T(8,128)(2,1)S(1)} %all_gather.35) | copy-start | bytes 442372
  58.9 22.0 %copy-start.15 = (bf16[384,384]{0,1:T(8,128)(2,1)}, bf16[384,384]{0,1:T(8,128)(2,1)S(1)}, u32[]{:S(2)}) copy-start(bf16[384,384]{0,1:T(8,128)(2,1)S(1)} %all_gather.32) | copy-start | bytes 884740
  79.3 8.6 %copy-start.19 = (bf16[384,768]{0,1:T(8,128)(2,1)}, bf16[384,768]{0,1:T(8,128)(2,1)S(1)}, u32[]{:S(2)}) copy-start(bf16[384,768]{0,1:T(8,128)(2,1)S(1)} %all_gather.36) | copy-start | bytes 1769476
  80.9 3.8 %copy-start.48 = (bf16[6,64,256]{2,1,0:T(8,128)(2,1)}, bf16[6,64,256]{2,1,0:T(8,128)(2,1)S(1)}, u32[]{:S(2)}) copy-start(bf16[6,64,256]{2,1,0:T(8,128)(2,1)S(1)} %convolution_convert_fusion.14) | copy-start | bytes 589828
  147.4 5.0 %copy-start.35 = (bf16[6,64,256]{2,1,0:T(8,128)(2,1)}, bf16[6,64,256]{2,1,0:T(8,128)(2,1)S(1)}, u32[]{:S(2)}) copy-start(bf16[6,64,256]{2,1,0:T(8,128)(2,1)S(1)} %convolution_convert_fusion.12) | copy-start | bytes 589828
  169.1 44.6 %copy-start.31 = (f32[256,1536]{1,0:T(8,128)S(1)}, f32[256,1536]{1,0:T(8,128)}, u32[]{:S(2)}) copy-start(f32[256,1536]{1,0:T(8,128)} %copy-done.30) | copy-start | bytes 4718596
  336.3 5.4 %copy-start.43 = (bf16[384,1152]{1,0:T(8,128)(2,1)S(1)}, bf16[384,1152]{1,0:T(8,128)(2,1)}, u32[]{:S(2)}) copy-start(bf16[384,1152]{1,0:T(8,128)(2,1)} %get-tuple-element.111) | copy-start | bytes 2654212
  (79 other events, 133.3 us)
Sparse Core Ops, SparseCore 0:
  9.9 32.0 all-gather.5
  43.8 30.6 all-gather.7
  76.3 29.1 all-gather.9
  107.2 27.7 all-gather.11
  167.4 168.8 all-reduce.3

commit v2 on v1

v2 whole, which is shorter than its diff:
```python
import functools

import jax
import jax.numpy as jnp
from jax import lax
from jax.experimental import pallas as pl
from jax.experimental.pallas import tpu as pltpu
from jax.sharding import PartitionSpec as P

D = 384
HEADS = 6
HEAD = 64
SHARED = 3
QUARTERS = 4

EPSILON = 1e-05
MASKED = -1e30
GELU_SCALE = 0.7978845608028654
GELU_CUBE = 0.044715

f32 = jnp.float32
bf16 = jnp.bfloat16
VMEM_BYTES = 32 * 1024 * 1024


def nn(left, right):
    return jnp.dot(left, right, preferred_element_type=f32)


def nt(left, right):
    return lax.dot_general(left, right, (((1,), (1,)), ((), ())), preferred_element_type=f32)


def centre(hidden):
    centred = hidden - jnp.mean(hidden, -1, keepdims=True)
    spread = jnp.mean(centred * centred, -1, keepdims=True)
    rstd = lax.rsqrt(spread + EPSILON)
    return centred * rstd, rstd


def norm_back(scaled, rstd, gain, grad):
    grad_gain = jnp.sum(grad * scaled, 0, keepdims=True)
    c = grad * gain
    along = jnp.mean(c * scaled, -1, keepdims=True)
    return rstd * (c - jnp.mean(c, -1, keepdims=True) - scaled * along), grad_gain


def swapped(rank):
    return ((rank & 1) << 1) | (rank >> 1)


def place_pieces(info, pieces, held):
    own0, own1, near, far, both, other_near, other_far, other_both = pieces
    section, core = info[0], info[1]
    held[0, section] = own0[...]
    held[1, section] = own1[...]
    one, two, three = section ^ 1, section ^ 2, section ^ 3

    @pl.when(core == 0)
    def _():
        held[0, one] = near[...]
        held[0, two] = far[...]
        held[0, three] = both[...]
        held[1, two] = other_near[...]
        held[1, one] = other_far[...]
        held[1, three] = other_both[...]

    @pl.when(core != 0)
    def _():
        held[1, two] = near[...]
        held[1, one] = far[...]
        held[1, three] = both[...]
        held[0, one] = other_near[...]
        held[0, two] = other_far[...]
        held[0, three] = other_both[...]


def put(info, keep, send, half, quarter, value, rows=None):
    section, core = info[0], info[1]
    rank = quarter ^ section
    if half == 1:
        rank = swapped(rank)
    where = (rank,) if rows is None else (rank, pl.ds(*rows))

    @pl.when(core == half)
    def _():
        keep[where] = value

    @pl.when(core != half)
    def _():
        send[where] = value


def usable(rows, length):
    key_index = lax.broadcasted_iota(jnp.int32, (rows, rows), 0)
    query_index = lax.broadcasted_iota(jnp.int32, (rows, rows), 1)
    return (key_index <= query_index) & (key_index < length)


def head_lanes(rows, side):
    lane = lax.broadcasted_iota(jnp.int32, (rows, 2 * HEAD), 1)
    return (lane < HEAD) if side == 0 else (lane >= HEAD)


def attend(mixed, length, stats):
    rows = mixed.shape[0]
    allowed = usable(rows, length)
    values_across = mixed[:, 2 * D :].T
    outs = []
    for pair in range(HEADS // 2):
        at = 2 * HEAD * pair
        queries = mixed[:, at : at + 2 * HEAD]
        key_rows = mixed[:, D + at : D + at + 2 * HEAD]
        for side in range(2):
            head = 2 * pair + side
            one_head = jnp.where(head_lanes(rows, side), queries, 0)
            scores = jnp.where(allowed, nt(key_rows, one_head) * HEAD ** (-0.5), MASKED)
            peak = jnp.max(scores, 0, keepdims=True)
            raised = jnp.exp(scores - peak)
            inverse = 1.0 / jnp.sum(raised, 0, keepdims=True)
            stats[head : head + 1, :] = peak
            stats[8 + head : 9 + head, :] = inverse
            probability = (raised * inverse).astype(bf16)
            outs.append(nn(values_across[HEAD * head : HEAD * head + HEAD], probability))
    return jnp.concatenate(outs, 0).T.astype(bf16)


def attend_back(mixed, grad_heads, length, stats, grad_mixed):
    rows = mixed.shape[0]
    allowed = usable(rows, length)
    keys_across = mixed[:, D : 2 * D].T
    query_parts = []
    for pair in range(HEADS // 2):
        at = 2 * HEAD * pair
        queries = mixed[:, at : at + 2 * HEAD]
        key_rows = mixed[:, D + at : D + at + 2 * HEAD]
        values = mixed[:, 2 * D + at : 2 * D + at + 2 * HEAD]
        grads = grad_heads[:, at : at + 2 * HEAD]
        key_grad = jnp.zeros((rows, 2 * HEAD), f32)
        value_grad = jnp.zeros((rows, 2 * HEAD), f32)
        for side in range(2):
            head = 2 * pair + side
            lanes = head_lanes(rows, side)
            one_head = jnp.where(lanes, queries, 0)
            one_grad = jnp.where(lanes, grads, 0)
            scores = jnp.where(allowed, nt(key_rows, one_head) * HEAD ** (-0.5), MASKED)
            probability = jnp.exp(scores - stats[head : head + 1, :]) * stats[8 + head : 9 + head, :]
            grad_prob = nt(values, one_grad)
            middle = jnp.sum(probability * grad_prob, 0, keepdims=True)
            grad_scores = (probability * (grad_prob - middle)).astype(bf16)
            key_grad += nn(grad_scores, one_head)
            value_grad += nn(probability.astype(bf16), one_grad)
            query_parts.append(nn(keys_across[HEAD * head : HEAD * head + HEAD], grad_scores))
        grad_mixed[:, D + at : D + at + 2 * HEAD] = (key_grad * HEAD ** (-0.5)).astype(bf16)
        grad_mixed[:, 2 * D + at : 2 * D + at + 2 * HEAD] = value_grad.astype(bf16)
    grad_mixed[:, :D] = (jnp.concatenate(query_parts, 0).T * HEAD ** (-0.5)).astype(bf16)


def first_kernel(
    info, tokens, *rest
):
    pieces = rest[:8]
    h1, mixed, attended, stats, mixing, output, mixing_three, output_three, gains, held = rest[8:]
    place_pieces(info, pieces, held)
    mixing_three[:, 2 * D : 2 * D + SHARED * HEAD] = jnp.zeros((D, SHARED * HEAD), bf16)
    for j in range(QUARTERS):
        one = held[0, j]
        mixing[:, 288 * j : 288 * j + 288] = one[:, :288]
        output[:, 96 * j : 96 * j + 96] = one[:, 288:]
        three = held[1, j]
        mixing_three[:, 192 * j : 192 * j + 192] = three[:, :192]
        mixing_three[:, 960 + 48 * j : 960 + 48 * j + 48] = three[:, 192:240]
        output_three[:, 96 * j : 96 * j + 96] = three[:, 240:336]
        edge = held[1, j, 0:16, 256:384].astype(f32)[:, 80:]
        for k in range(4):
            for i in range(2):
                gains[k : k + 1, 96 * j + 48 * i : 96 * j + 48 * i + 48] = edge[2 * k + i : 2 * k + i + 1]
    hidden = tokens[...].astype(f32)
    scaled, _ = centre(hidden)
    normed = (scaled * gains[0:1, :]).astype(bf16)
    mixed[...] = nn(normed, mixing[...]).astype(bf16)
    attended[...] = attend(mixed, info[2], stats)
    h1[...] = (hidden + nn(attended[...], output[...])).astype(bf16)


def middle_kernel(info, h1, gains, mixing_three, output_three, mixed_one, *rest):
    pieces = rest[:8]
    h2, held, h3, mixed, attended, stats = rest[8:]
    place_pieces(info, pieces, held)
    hidden = h1[...].astype(f32)
    scaled, _ = centre(hidden)
    normed = (scaled * gains[1:2, :]).astype(bf16)
    total = hidden
    for j in range(QUARTERS):
        upward = nn(normed, held[0, j])
        bent = jnp.tanh(GELU_SCALE * (upward + GELU_CUBE * upward * upward * upward))
        total += nn((0.5 * upward * (1.0 + bent)).astype(bf16), held[1, j])
    h2[...] = total.astype(bf16)
    hidden = h2[...].astype(f32)
    scaled, _ = centre(hidden)
    normed = (scaled * gains[2:3, :]).astype(bf16)
    mixed[...] = nn(normed, mixing_three[...]).astype(bf16)
    shared_width = SHARED * HEAD
    mixed[:, 2 * D : 2 * D + shared_width] = mixed_one[:, 2 * D : 2 * D + shared_width]
    attended[...] = attend(mixed, info[2], stats)
    h3[...] = (hidden + nn(attended[...], output_three[...])).astype(bf16)


def feed_parts(upward):
    square = upward * upward
    bent = jnp.tanh(GELU_SCALE * (upward + GELU_CUBE * square * upward))
    active = 0.5 * upward * (1.0 + bent)
    slope = 0.5 * (1.0 + bent) + 0.5 * upward * (1.0 - bent * bent) * (
        GELU_SCALE * (1.0 + 3.0 * GELU_CUBE * square)
    )
    return active.astype(bf16), slope


def feed_back(info, held, normed, grad_out, actives, slopes, keep, send):
    grad_normed = jnp.zeros(normed.shape, f32)
    normed_across = normed.T
    for j in range(QUARTERS):
        up, down = held[0, j], held[1, j]
        if slopes is None:
            active, slope = feed_parts(nn(normed, up))
        else:
            active, slope = actives[j], slopes[j]
        grad_upward = (nt(grad_out, down) * slope).astype(bf16)
        put(info, keep, send, 1, j, nn(active.T, grad_out).astype(bf16))
        put(info, keep, send, 0, j, nn(normed_across, grad_upward).astype(bf16))
        grad_normed += nt(grad_upward, up)
    return grad_normed


def last_kernel(info, h3, gains, cotangent, *rest):
    pieces = rest[:8]
    out, grad_h3, keep, send, grad_gain, held, actives, slopes = rest[8:]
    place_pieces(info, pieces, held)
    hidden = h3[...].astype(f32)
    scaled, rstd = centre(hidden)
    gain = gains[3:4, :]
    normed = (scaled * gain).astype(bf16)
    total = hidden
    for j in range(QUARTERS):
        active, slope = feed_parts(nn(normed, held[0, j]))
        actives[j] = active
        slopes[j] = slope
        total += nn(active, held[1, j])
    out[...] = total
    row = lax.broadcasted_iota(jnp.int32, hidden.shape, 0)
    grad_out = jnp.where(row < info[2], cotangent[...].astype(f32), 0.0)
    grad_normed = feed_back(
        info, held, normed, grad_out.astype(bf16), actives, slopes, keep, send
    )
    grad_hidden, one_gain = norm_back(scaled, rstd, gain, grad_normed)
    grad_gain[0:1, :] = one_gain
    grad_h3[...] = (grad_out + grad_hidden).astype(bf16)


def attention_back(info, hidden, grad_out, mixed, attended, stats, mixing, output, gain, grad_mixed, shared):
    scaled, rstd = centre(hidden)
    normed_across = (scaled * gain).astype(bf16).T
    grad_heads = nt(grad_out, output[...]).astype(bf16)
    grad_output = nn(attended[...].T, grad_out).astype(bf16)
    attend_back(mixed, grad_heads, info[2], stats, grad_mixed)
    shared(grad_mixed)
    grad_mixing = nn(normed_across, grad_mixed[...]).astype(bf16)
    grad_hidden, grad_gain = norm_back(scaled, rstd, gain, nt(grad_mixed[...], mixing[...]))
    return grad_hidden, grad_gain, grad_mixing, grad_output


def third_back_kernel(
    info, h2, gains, grad_h3, mixed, attended, stats, mixing, output,
    grad_h2, grad_weights, grad_shared, grad_gain, grad_mixed,
):
    shared_width = SHARED * HEAD

    def hand_over(grads):
        grad_shared[...] = grads[:, 2 * D : 2 * D + shared_width]
        grads[:, 2 * D : 2 * D + shared_width] = jnp.zeros((grads.shape[0], shared_width), bf16)

    grad_hidden, one_gain, grad_mixing, grad_output = attention_back(
        info, h2[...].astype(f32), grad_h3[...], mixed, attended, stats, mixing, output,
        gains[2:3, :], grad_mixed, hand_over,
    )
    grad_weights[0, :D] = grad_mixing[:, :D]
    grad_weights[0, D:] = grad_mixing[:, D : 2 * D]
    grad_weights[1, :D] = grad_mixing[:, 2 * D :]
    grad_weights[1, D:] = grad_output
    grad_gain[0:1, :] = one_gain
    grad_h2[...] = (grad_h3[...].astype(f32) + grad_hidden).astype(bf16)


def second_back_kernel(info, h1, gains, grad_h2, held, grad_h1, keep, send, grad_gain):
    scaled, rstd = centre(h1[...].astype(f32))
    gain = gains[1:2, :]
    normed = (scaled * gain).astype(bf16)
    grad_normed = feed_back(info, held, normed, grad_h2[...], None, None, keep, send)
    grad_hidden, one_gain = norm_back(scaled, rstd, gain, grad_normed)
    grad_gain[0:1, :] = one_gain
    grad_h1[...] = (grad_h2[...].astype(f32) + grad_hidden).astype(bf16)


def first_back_kernel(
    info, tokens, gains, grad_h1, mixed, attended, stats, mixing, output,
    grad_shared, third_weights, gain_two, gain_three, gain_four,
    input_grad, keep, send, grad_mixed, grad_weights,
):
    shared_width = SHARED * HEAD

    def take_over(grads):
        at = slice(2 * D, 2 * D + shared_width)
        grads[:, at] = (grads[:, at].astype(f32) + grad_shared[...].astype(f32)).astype(bf16)

    grad_hidden, gain_one, grad_mixing, grad_output = attention_back(
        info, tokens[...].astype(f32), grad_h1[...], mixed, attended, stats, mixing, output,
        gains[0:1, :], grad_mixed, take_over,
    )
    input_grad[...] = grad_h1[...].astype(f32) + grad_hidden
    grad_weights[0, :D] = grad_mixing[:, :D]
    grad_weights[0, D:] = grad_mixing[:, D : 2 * D]
    grad_weights[1, :D] = grad_mixing[:, 2 * D :]
    grad_weights[1, D:] = grad_output
    part = 2 * D // QUARTERS
    for half in range(2):
        for j in range(QUARTERS):
            put(info, keep, send, half, j, grad_weights[half, part * j : part * (j + 1)], (0, part))
            put(info, keep, send, half, j, third_weights[half, part * j : part * (j + 1)], (part, part))
    rows = []
    for grad in (gain_one, gain_two[0:1, :], gain_three[0:1, :], gain_four[0:1, :]):
        rows += [grad[:, :shared_width], grad[:, shared_width:]]
    rows.append(jnp.zeros((8, shared_width), f32))
    block = jnp.concatenate(rows, 0).astype(bf16)
    section, core = info[0], info[1]
    rank = swapped(section)

    @pl.when(core == 1)
    def _():
        keep[rank, part : part + 16, :shared_width] = block

    @pl.when(core != 1)
    def _():
        send[rank, part : part + 16, :shared_width] = block


def unpack_feed_kernel(info, *rest):
    pieces, (up, down, wide, sems) = rest[:8], rest[8:]
    section, core = info[0], info[1]

    def copies(slot, rank):
        own = slot < 4
        half_zero = (core == 0) if own else (core != 0)
        at0 = pl.multiple_of((section ^ rank) * D, D)
        at1 = pl.multiple_of((section ^ ((rank & 1) << 1 | rank >> 1)) * D, D)
        return half_zero, pltpu.make_async_copy(
            wide.at[slot], up.at[:, pl.ds(at0, D)], sems.at[slot]
        ), pltpu.make_async_copy(wide.at[slot], down.at[pl.ds(at1, D), :], sems.at[slot])

    for slot in range(8):
        wide[slot] = pieces[slot][...].astype(f32)
        half_zero, to_up, to_down = copies(slot, slot % 4)
        pl.when(half_zero)(to_up.start)
        pl.when(jnp.logical_not(half_zero))(to_down.start)
    for slot in range(8):
        half_zero, to_up, to_down = copies(slot, slot % 4)
        pl.when(half_zero)(to_up.wait)
        pl.when(jnp.logical_not(half_zero))(to_down.wait)


def unpack_attention_kernel(info, *rest):
    pieces = rest[:8]
    mixing, output, pair, fresh, output_three, g1, g2, g3, g4, wide, narrow, sems = rest[8:]
    section, core = info[0], info[1]
    part = 2 * D // QUARTERS
    shared_width = SHARED * HEAD

    def plan(slot):
        rank = slot % 4
        half_zero = (core == 0) if slot < 4 else (core != 0)
        j0, j1 = section ^ rank, section ^ swapped(rank)
        col0 = pl.multiple_of((j0 >> 1) * D, D)
        row0 = pl.multiple_of((j0 & 1) * part, part)
        row1 = pl.multiple_of((j1 & 1) * part, part)
        top, low = wide.at[slot, :part], wide.at[slot, part:]
        st, sl = sems.at[slot, 0], sems.at[slot, 1]
        copy = pltpu.make_async_copy
        is_v = j1 < 2
        not_zero = jnp.logical_not(half_zero)
        return [
            (half_zero, copy(top, mixing.at[pl.ds(row0, part), pl.ds(col0, D)], st)),
            (half_zero, copy(low, pair.at[pl.ds(row0, part), pl.ds(col0, D)], sl)),
            (not_zero & is_v, copy(top, mixing.at[pl.ds(row1, part), 2 * D :], st)),
            (not_zero & is_v, copy(narrow.at[slot], fresh.at[pl.ds(row1, part), :], sl)),
            (not_zero & (j1 >= 2), copy(top, output.at[pl.ds(row1, part), :], st)),
            (not_zero & (j1 >= 2), copy(low, output_three.at[pl.ds(row1, part), :], sl)),
        ], not_zero & is_v, not_zero & (j1 == 0)

    for slot in range(8):
        wide[slot] = pieces[slot][...].astype(f32)
        steps, is_fresh, has_gains = plan(slot)

        @pl.when(is_fresh)
        def _():
            narrow[slot] = wide[slot, part:, shared_width:]

        @pl.when(has_gains)
        def _():
            block = wide[slot, part : part + 8, :shared_width]
            for k, ref in enumerate((g1, g2, g3, g4)):
                ref[...] = jnp.concatenate([block[2 * k : 2 * k + 1], block[2 * k + 1 : 2 * k + 2]], 1)

        for flag, copy in steps:
            pl.when(flag)(copy.start)
    for slot in range(8):
        for flag, copy in plan(slot)[0]:
            pl.when(flag)(copy.wait)


def call(body, name, outs, scratch, args, flops=10**9, any_outs=()):
    vmem = pl.BlockSpec(memory_space=pltpu.VMEM)
    return pl.pallas_call(
        body,
        name=name,
        out_shape=[jax.ShapeDtypeStruct(shape, dtype) for shape, dtype in outs],
        in_specs=[pl.BlockSpec(memory_space=pltpu.SMEM)] + [vmem] * (len(args) - 1),
        out_specs=[
            pl.BlockSpec(memory_space=pl.ANY) if i in any_outs else vmem for i in range(len(outs))
        ],
        scratch_shapes=scratch,
        compiler_params=pltpu.CompilerParams(vmem_limit_bytes=VMEM_BYTES),
        cost_estimate=pl.CostEstimate(flops=flops, bytes_accessed=10**6, transcendentals=10**6),
    )(*args)


def partner_pairs(sections, groups, kind):
    found = []
    for section in range(sections):
        for group in range(groups):
            core = group & 1
            to_section, to_group = section, group
            if kind == "near":
                to_section = section ^ (1 if core == 0 else 2)
            elif kind == "far":
                to_section = section ^ (2 if core == 0 else 1)
            else:
                to_group = group ^ kind
            found.append((section * groups + group, to_section * groups + to_group))
    return found


def partner(value, kind):
    sections, groups = lax.axis_size("section"), lax.axis_size("dp")
    return lax.ppermute(value, ("section", "dp"), partner_pairs(sections, groups, kind))


def gather_chunk(own0, own1, core):
    mine = jnp.where(core == 0, own0, own1)
    near = partner(mine, "near")
    far = partner(mine, "far")
    both = partner(near, "far")
    return (own0, own1, near, far, both) + tuple(partner(v, 1) for v in (near, far, both))


def add(left, right):
    return (left.astype(f32) + right.astype(f32)).astype(bf16)


def reduce_chunk(keep, send):
    groups = lax.axis_size("dp")
    from_core = partner(send, 1)
    p3 = add(keep[3], from_core[3])
    p1 = add(keep[1], from_core[1])
    r3 = partner(p3, "near")
    r1 = partner(p1, "near")
    p2 = (keep[2].astype(f32) + from_core[2].astype(f32) + r3.astype(f32)).astype(bf16)
    r2 = partner(p2, "far")
    own = (
        keep[0].astype(f32) + from_core[0].astype(f32) + r1.astype(f32) + r2.astype(f32)
    ).astype(bf16)
    if groups > 2:
        rows = own.shape[0] // 2
        bit = (lax.axis_index("dp") >> 1) & 1
        low, high = own[:rows], own[rows:]
        kept = add(jnp.where(bit == 0, low, high), partner(jnp.where(bit == 0, high, low), 2))
        step = 4
        while step < groups:
            kept = add(kept, partner(kept, step))
            step *= 2
        back = partner(kept, 2)
        own = jnp.concatenate(
            [jnp.where(bit == 0, kept, back), jnp.where(bit == 0, back, kept)], 0
        )
    g2 = partner(own, "far")
    g1 = partner(own, "near")
    g3 = partner(g2, "near")
    mine = (own, g1, g2, g3)
    return mine + tuple(partner(v, 1) for v in mine)


def shards(
    tokens,
    cotangent,
    lengths,
    gain_one,
    mixing_one,
    output_one,
    gain_two,
    up_two,
    down_two,
    gain_three,
    pair_three,
    fresh_three,
    output_three,
    gain_four,
    up_four,
    down_four,
):
    rows = tokens.shape[0]
    section = lax.axis_index("section")
    core = lax.axis_index("dp") & 1
    info = jnp.stack([section, core, lengths[section, 0]]).astype(jnp.int32)

    edge = jnp.stack([gain_one, gain_two, gain_three, gain_four]).reshape(8, 48)
    edge = jnp.concatenate([edge, jnp.zeros((D - 8, 48), bf16)], 0)
    one = jnp.concatenate([mixing_one, output_one], 1)
    three = jnp.concatenate([pair_three, fresh_three, output_three, edge], 1)
    chunk_one = gather_chunk(one, three, core)
    chunk_two = gather_chunk(up_two, down_two, core)
    chunk_four = gather_chunk(up_four, down_four, core)

    row = (rows, D)
    wide_row = (rows, 3 * D)
    square = (D, D)
    held = (2, QUARTERS, D, D)
    stat = ((16, rows), f32)
    gain_row = ((8, D), f32)
    h1, mixed_one, attended_one, stats_one, mixing, output, mixing_three, out_three, gains = call(
        first_kernel, "first_forward",
        [(row, bf16), (wide_row, bf16), (row, bf16), stat, ((D, 3 * D), bf16), (square, bf16),
         ((D, 3 * D), bf16), (square, bf16), gain_row],
        [pltpu.VMEM(held, bf16)],
        (info, tokens) + chunk_one,
    )
    h2, held_two, h3, mixed_three, attended_three, stats_three = call(
        middle_kernel, "second_third_forward",
        [(row, bf16), (held, bf16), (row, bf16), (wide_row, bf16), (row, bf16), stat],
        [],
        (info, h1, gains, mixing_three, out_three, mixed_one) + chunk_two,
    )
    packed = ((QUARTERS, D, D), bf16)
    out, grad_h3, keep_four, send_four, gain_grad_four = call(
        last_kernel, "fourth_both",
        [(row, f32), (row, bf16), packed, packed, gain_row],
        [pltpu.VMEM(held, bf16), pltpu.VMEM((QUARTERS,) + row, bf16), pltpu.VMEM((QUARTERS,) + row, f32)],
        (info, h3, gains, cotangent) + chunk_four,
    )
    grad_h2, third_weights, grad_shared, gain_grad_three = call(
        third_back_kernel, "third_backward",
        [(row, bf16), ((2, 2 * D, D), bf16), ((rows, SHARED * HEAD), bf16), gain_row],
        [pltpu.VMEM(wide_row, bf16)],
        (info, h2, gains, grad_h3, mixed_three, attended_three, stats_three, mixing_three, out_three),
    )
    grad_h1, keep_two, send_two, gain_grad_two = call(
        second_back_kernel, "second_backward",
        [(row, bf16), packed, packed, gain_row],
        [],
        (info, h1, gains, grad_h2, held_two),
    )
    input_grad, keep_one, send_one = call(
        first_back_kernel, "first_backward",
        [(row, f32), packed, packed],
        [pltpu.VMEM(wide_row, bf16), pltpu.VMEM((2, 2 * D, D), bf16)],
        (info, tokens, gains, grad_h1, mixed_one, attended_one, stats_one, mixing, output,
         grad_shared, third_weights, gain_grad_two, gain_grad_three, gain_grad_four),
    )

    feed_outs = [((D, 4 * D), f32), ((4 * D, D), f32)]
    feed_scratch = [pltpu.VMEM((8, D, D), f32), pltpu.SemaphoreType.DMA((8,))]
    grad_up_four, grad_down_four = call(
        unpack_feed_kernel, "unpack_four", feed_outs, feed_scratch,
        (info,) + reduce_chunk(keep_four, send_four), any_outs=(0, 1),
    )
    grad_up_two, grad_down_two = call(
        unpack_feed_kernel, "unpack_two", feed_outs, feed_scratch,
        (info,) + reduce_chunk(keep_two, send_two), any_outs=(0, 1),
    )
    part = 2 * D // QUARTERS
    gain_out = ((1, D), f32)
    mixing_g, output_g, pair_g, fresh_g, output_three_g, g1, g2, g3, g4 = call(
        unpack_attention_kernel, "unpack_attention",
        [((D, 3 * D), f32), (square, f32), ((D, 2 * D), f32), ((D, D // 2), f32), (square, f32)]
        + [gain_out] * 4,
        [pltpu.VMEM((8, D, D), f32), pltpu.VMEM((8, part, part), f32),
         pltpu.SemaphoreType.DMA((8, 2))],
        (info,) + reduce_chunk(keep_one, send_one), any_outs=(0, 1, 2, 3, 4),
    )
    g1, g2, g3, g4 = (g.reshape(D) for g in (g1, g2, g3, g4))
    return (
        out, input_grad, g1, mixing_g, output_g, g2, grad_up_two, grad_down_two,
        g3, pair_g, fresh_g, output_three_g, g4, grad_up_four, grad_down_four,
    )


def solution(mesh):
    return jax.shard_map(
        shards,
        mesh=mesh,
        in_specs=(
            P(("section", "dp"), None),
            P(("section", "dp"), None),
            P(None, "dp"),
            P("section"),
            P(None, "section"),
            P(None, "section"),
            P("section"),
            P(None, "section"),
            P("section", None),
            P("section"),
            P(None, "section"),
            P(None, "section"),
            P(None, "section"),
            P("section"),
            P(None, "section"),
            P("section", None),
        ),
        out_specs=(P(("section", "dp"), None), P(("section", "dp"), None)) + (P(),) * 13,
        check_vma=False,
    )
```

time: 358 us -> 198 us (0.55)
  blocking collectives: 104 us -> 0 us
  waiting for transfers between devices: 158 us -> 71 us
  starting transfers between devices: 0.19 us -> 50.6 us
  Pallas kernels: 0 us -> 43.4 us
  matrix products: 41.9 us -> 0 us
  between operations: 15 us -> 1.3 us
  other arithmetic: 25.1 us -> 15.1 us
    psum x1 -> x0, waiting for transfers between devices: 120 us -> none  [shards(): totals = lax.psum(local, ('section', 'dp'))]
    ppermute x0 -> x60, waiting for transfers between devices: none -> 71 us  [partner(): lax.ppermute(value, ('section', 'dp'), partner_pairs(sections, groups, ki...]
    all_gather x6 -> x0, blocking collectives: 62.9 us -> none  [the longest x5 53.4 us: gathered(): return lax.all_gather(shard, 'section', axis=axis, tiled=True)]
    ppermute x0 -> x60, starting transfers between devices: none -> 50.6 us  [partner(): lax.ppermute(value, ('section', 'dp'), partner_pairs(sections, groups, ki...]
    pallas_call x0 -> x9, Pallas kernels: none -> 43.4 us  [call(): pl.pallas_call(body, name=name, out_shape=[jax.ShapeDtypeStruct(shape, dt...]
    dot_general x39 -> x0, matrix products: 41.9 us -> none  [the longest x9 12.5 us: inner_rows(): lax.dot_general(left, right, (((0,), (0,)), ((), ())), preferred_element_...]
    psum x1 -> x0, blocking collectives: 40.9 us -> none  [shards(): totals = lax.psum(local, ('section', 'dp'))]
    all_gather x4 -> x0, waiting for transfers between devices: 35.2 us -> none  [gathered(): return lax.all_gather(shard, 'section', axis=axis, tiled=True)]
  transfers between devices with their start and end apart: 5 -> 60, of which waited for: 3 -> 29; matrix products, arithmetic and copies ran while one was open for 8% -> 8% of each run, Pallas kernels for 0% -> 8%
where the time goes in v2:
time: 198 us; the launch traced here: 197 us
  waiting for transfers between devices  71 us (36%)
  starting transfers between devices  50.6 us (26%)
  Pallas kernels  43.4 us (22%)
  local copies, waits for them, and re-layouts  15.3 us (8%)
  other arithmetic  15.1 us (8%)
    ppermute x60, waiting for transfers between devices, partner(): lax.ppermute(value, ('section', 'dp'), partner_pairs(sections, groups, ki...  71 us
    ppermute x60, starting transfers between devices, partner(): lax.ppermute(value, ('section', 'dp'), partner_pairs(sections, groups, ki...  50.6 us
    pallas_call x9, Pallas kernels, call(): pl.pallas_call(body, name=name, out_shape=[jax.ShapeDtypeStruct(shape, dt...  43.4 us
    unnamed x46, local copies, waits for them, and re-layouts  14.6 us
    convert_element_type x9, other arithmetic, add(): return (left.astype(f32) + right.astype(f32)).astype(bf16)  3.98 us
  transfers between devices with their start and end apart: 60, of which 29 were waited for; matrix products, arithmetic and copies ran while one was open for 8% of the time, Pallas kernels for 8%

profile of v2, /device:TPU:0, one launch (start us, length us, event | category | flops | bytes accessed | tf_op | source)
XLA Modules:
  0.0 196.7 jit_solution(5665194367517663893)
XLA Ops:
  6.9 3.0 %collective-permute-start.1 = (bf16[384,384]{1,0:T(8,128)(2,1)S(1)}, bf16[384,384]{1,0:T(8,128)(2,1)S(1)}, u32[]{:S(2)}, u32[]{:S(2)}) collective-permute-start(bf16[384,384]{1,0:T(8,128)(2,1)S(1)} %get-tuple-element.118), channel_id=1, source_target_pairs={{0,16},{1,9},{2,18},{3,11},{4,20},{5,13},{6,22},{7,15},{8,24},{9,1... | collective-permute-start | bytes 884744 | tf_op jit(solution)/shard_map/ppermute | solution.py:453
  14.2 3.1 %collective-permute-done.1.rest_3_ = bf16[384,384]{1,0:T(8,128)(2,1)S(1)} collective-permute-done((bf16[384,384]{1,0:T(8,128)(2,1)S(1)}, bf16[384,384]{1,0:T(8,128)(2,1)S(1)}, u32[]{:S(2)}, u32[]{:S(2)}) %collective-permute-start.1) | collective-permute-done | bytes 294944 | tf_op jit(solution)/shard_map/ppermute | solution.py:453
  17.3 2.5 %collective-permute-start.7 = (bf16[384,384]{1,0:T(8,128)(2,1)S(1)}, bf16[384,384]{1,0:T(8,128)(2,1)S(1)}, u32[]{:S(2)}, u32[]{:S(2)}) collective-permute-start(bf16[384,384]{1,0:T(8,128)(2,1)S(1)} %broadcast_select_fusion.1), channel_id=1, source_target_pairs={{0,16},{1,9},{2,18},{3,11},{4,20},{5,13},{6,22},{7,15},{8,24},{9,1... | collective-permute-start | bytes 884744 | tf_op jit(solution)/shard_map/ppermute | solution.py:453
  20.6 3.0 %collective-permute-done.13.rest_3_ = bf16[384,384]{1,0:T(8,128)(2,1)S(1)} collective-permute-done((bf16[384,384]{1,0:T(8,128)(2,1)S(1)}, bf16[384,384]{1,0:T(8,128)(2,1)S(1)}, u32[]{:S(2)}, u32[]{:S(2)}) %collective-permute-start.13) | collective-permute-done | bytes 294944 | tf_op jit(solution)/shard_map/ppermute | solution.py:453
  23.6 2.5 %collective-permute-start.2 = (bf16[384,384]{1,0:T(8,128)(2,1)S(1)}, bf16[384,384]{1,0:T(8,128)(2,1)}, u32[]{:S(2)}, u32[]{:S(2)}) collective-permute-start(bf16[384,384]{1,0:T(8,128)(2,1)S(1)} %collective-permute-done.rest_2_), channel_id=1, source_target_pairs={{0,16},{1,9},{2,18},{3,11},{4,20},{5,13},{6,22},{7,15},{8,24},{9,1... | collective-permute-start | bytes 884744 | tf_op jit(solution)/shard_map/ppermute | solution.py:453
  27.1 5.5 %collective-permute-done.6.rest_2_ = bf16[384,384]{1,0:T(8,128)(2,1)S(1)} collective-permute-done((bf16[384,384]{1,0:T(8,128)(2,1)S(1)}, bf16[384,384]{1,0:T(8,128)(2,1)S(1)}, u32[]{:S(2)}, u32[]{:S(2)}) %collective-permute-start.6) | collective-permute-done | bytes 294944 | tf_op jit(solution)/shard_map/ppermute | solution.py:453
  36.6 2.7 %collective-permute-done.8.rest_4_ = bf16[384,384]{1,0:T(8,128)(2,1)S(1)} collective-permute-done((bf16[384,384]{1,0:T(8,128)(2,1)S(1)}, bf16[384,384]{1,0:T(8,128)(2,1)S(1)}, u32[]{:S(2)}, u32[]{:S(2)}) %collective-permute-start.8) | collective-permute-done | bytes 294944 | tf_op jit(solution)/shard_map/ppermute | solution.py:453
  39.9 2.7 %collective-permute-done.14.rest_4_ = bf16[384,384]{1,0:T(8,128)(2,1)} collective-permute-done((bf16[384,384]{1,0:T(8,128)(2,1)}, bf16[384,384]{1,0:T(8,128)(2,1)}, u32[]{:S(2)}, u32[]{:S(2)}) %collective-permute-start.14) | collective-permute-done | bytes 294944 | tf_op jit(solution)/shard_map/ppermute | solution.py:453
  48.6 4.6 %first_forward.1 = (bf16[256,384]{1,0:T(8,128)(2,1)S(1)}, bf16[256,1152]{1,0:T(8,128)(2,1)S(1)}, bf16[256,384]{1,0:T(8,128)(2,1)S(1)}, f32[16,256]{1,0:T(8,128)S...) custom-call(s32[3]{0:T(128)S(1)} %pad_add_fusion.info, ...), custom_call_target="tpu_custom_call" | custom-call | flops 1000000000 | bytes 1000000 | tf_op jit(solution)/shard_map/first_forward/pallas_call | solution.py:421
  53.3 5.5 %second_third_forward.1 = (bf16[256,384]{1,0:T(8,128)(2,1)S(1)}, bf16[2,4,384,384]{3,2,1,0:T(8,128)(2,1)S(1)}, bf16[256,384]{1,0:T(8,128)(2,1)S(1)}, bf16[256,11...) custom-call(s32[3]{0:T(128)S(1)} %pad_add_fusion.info, ...), custom_call_target="tpu_custom_call" | custom-call | flops 1000000000 | bytes 1000000 | tf_op jit(solution)/shard_map/second_third_forward/pallas_call | solution.py:421
  58.9 8.0 %fourth_both.1 = (f32[256,384]{1,0:T(8,128)}, bf16[256,384]{1,0:T(8,128)(2,1)S(1)}, bf16[4,384,384]{2,1,0:T(8,128)(2,1)S(1)}, bf16[4,384,384]{2,1,0:T(8,128)(2,1)}, f32[8,384]{1,0:T(8,128)S(1)}) custom-call(s32[3]{0:T(128)S(1)} %pad_add_fusion.info, bf16[256,384]{1,0:T(8,128)(2,1)S(1)} %get-tuple-element.64.h3, f32[8,384]{1,0:T(8,128)S(1)} %get-tuple-element.60.gains, ...), custom_call_target="tpu_custom_call" | custom-call | flops 1000000000 | bytes 1000000 | tf_op jit(solution)/shard_map/fourth_both/pallas_call | solution.py:421
  66.8 4.0 %third_backward.1 = (bf16[256,384]{1,0:T(8,128)(2,1)S(1)}, bf16[2,768,384]{2,1,0:T(8,128)(2,1)S(1)}, bf16[256,192]{1,0:T(8,128)(2,1)S(1)}, f32[8,384]{1,0:T(8,128)S(1)}) custom-call(s32[3]{0:T(128)S(1)} %pad_add_fusion.info, bf16[256,384]{1,0:T(8,128)(2,1)S(1)} %get-tuple-element.66.h2, f32[8,384]{1,0:T(8,128)S(1)} %get-tuple-element.60.gains, ...), custom_call_target="tpu_custom_call" | custom-call | flops 1000000000 | bytes 1000000 | tf_op jit(solution)/shard_map/third_backward/pallas_call | solution.py:421
  70.8 6.2 %second_backward.1 = (bf16[256,384]{1,0:T(8,128)(2,1)S(1)}, bf16[4,384,384]{2,1,0:T(8,128)(2,1)S(1)}, bf16[4,384,384]{2,1,0:T(8,128)(2,1)}, f32[8,384]{1,0:T(8,128)S(1)}) custom-call(s32[3]{0:T(128)S(1)} %pad_add_fusion.info, bf16[256,384]{1,0:T(8,128)(2,1)S(1)} %get-tuple-element.59.h1, f32[8,384]{1,0:T(8,128)S(1)} %get-tuple-element.60.gains, ...), custom_call_target="tpu_custom_call" | custom-call | flops 1000000000 | bytes 1000000 | tf_op jit(solution)/shard_map/second_backward/pallas_call | solution.py:421
  77.1 5.6 %first_backward.1 = (f32[256,384]{1,0:T(8,128)}, bf16[4,384,384]{2,1,0:T(8,128)(2,1)S(1)}, bf16[4,384,384]{2,1,0:T(8,128)(2,1)}) custom-call(s32[3]{0:T(128)S(1)} %pad_add_fusion.info, bf16[256,384]{1,0:T(8,128)(2,1)S(1)} %copy-done.6, f32[8,384]{1,0:T(8,128)S(1)} %get-tuple-element.60.gains, bf16[256,384]{1,0:T(8,128)(2,1)S(1)} %get-tuple-element.73.grad_h1, ...), custom_call_target="tpu_custom_call" | custom-call | flops 1000000000 | bytes 1000000 | tf_op jit(solution)/shard_map/first_backward/pallas_call | solution.py:421
  83.6 2.3 %collective-permute-done.18 = bf16[4,384,384]{2,1,0:T(8,128)(2,1)} collective-permute-done((bf16[4,384,384]{2,1,0:T(8,128)(2,1)}, bf16[4,384,384]{2,1,0:T(8,128)(2,1)}, u32[]{:S(2)}, u32[]{:S(2)}) %collective-permute-start.18) | collective-permute-done | bytes 1179680 | tf_op jit(solution)/shard_map/ppermute | solution.py:453
  99.7 3.7 %collective-permute-done.34 = bf16[384,384]{1,0:T(8,128)(2,1)S(1)} collective-permute-done((bf16[384,384]{1,0:T(8,128)(2,1)S(1)}, bf16[384,384]{1,0:T(8,128)(2,1)S(1)}, u32[]{:S(2)}, u32[]{:S(2)}) %collective-permute-start.34) | collective-permute-done | bytes 294944 | tf_op jit(solution)/shard_map/ppermute | solution.py:453
  104.6 8.3 %collective-permute-done.48 = bf16[384,384]{1,0:T(8,128)(2,1)S(1)} collective-permute-done((bf16[384,384]{1,0:T(8,128)(2,1)S(1)}, bf16[384,384]{1,0:T(8,128)(2,1)S(1)}, u32[]{:S(2)}, u32[]{:S(2)}) %collective-permute-start.48) | collective-permute-done | bytes 294944 | tf_op jit(solution)/shard_map/ppermute | solution.py:453
  114.1 2.0 %collective-permute-start.49 = (bf16[384,384]{1,0:T(8,128)(2,1)S(1)}, bf16[384,384]{1,0:T(8,128)(2,1)S(1)}, u32[]{:S(2)}, u32[]{:S(2)}) collective-permute-start(bf16[384,384]{1,0:T(8,128)(2,1)S(1)} %fusion), channel_id=1, source_target_pairs={{0,16},{1,9},{2,18},{3,11},{4,20},{5,13},{6,22},{7,15},{8,24},{9,1... | collective-permute-start | bytes 884744 | tf_op jit(solution)/shard_map/ppermute | solution.py:453
  125.7 2.6 %collective-permute-start.23 = (bf16[192,384]{1,0:T(8,128)(2,1)S(1)}, bf16[192,384]{1,0:T(8,128)(2,1)S(1)}, u32[]{:S(2)}, u32[]{:S(2)}) collective-permute-start(bf16[192,384]{1,0:T(8,128)(2,1)S(1)} %add_convert_fusion.11), channel_id=1, source_target_pairs={{0,4},{1,5},{2,6},{3,7},{4,0},{5,1},{6,2},{7,3},{8,12},{9,13},{10,... | collective-permute-start | bytes 442376 | tf_op jit(solution)/shard_map/ppermute | solution.py:453
  129.0 2.9 %collective-permute-start.37 = (bf16[192,384]{1,0:T(8,128)(2,1)S(1)}, bf16[192,384]{1,0:T(8,128)(2,1)S(1)}, u32[]{:S(2)}, u32[]{:S(2)}) collective-permute-start(bf16[192,384]{1,0:T(8,128)(2,1)S(1)} %add_convert_fusion.9), channel_id=1, source_target_pairs={{0,4},{1,5},{2,6},{3,7},{4,0},{5,1},{6,2},{7,3},{8,12},{9,13},{10,... | collective-permute-start | bytes 442376 | tf_op jit(solution)/shard_map/ppermute | solution.py:453
  133.9 8.4 %collective-permute-done.23 = bf16[192,384]{1,0:T(8,128)(2,1)S(1)} collective-permute-done((bf16[192,384]{1,0:T(8,128)(2,1)S(1)}, bf16[192,384]{1,0:T(8,128)(2,1)S(1)}, u32[]{:S(2)}, u32[]{:S(2)}) %collective-permute-start.23) | collective-permute-done | bytes 147488 | tf_op jit(solution)/shard_map/ppermute | solution.py:453
  142.5 2.4 %collective-permute-done.37 = bf16[192,384]{1,0:T(8,128)(2,1)S(1)} collective-permute-done((bf16[192,384]{1,0:T(8,128)(2,1)S(1)}, bf16[192,384]{1,0:T(8,128)(2,1)S(1)}, u32[]{:S(2)}, u32[]{:S(2)}) %collective-permute-start.37) | collective-permute-done | bytes 147488 | tf_op jit(solution)/shard_map/ppermute | solution.py:453
  147.1 2.5 %collective-permute-done.24 = bf16[192,384]{1,0:T(8,128)(2,1)S(1)} collective-permute-done((bf16[192,384]{1,0:T(8,128)(2,1)S(1)}, bf16[192,384]{1,0:T(8,128)(2,1)S(1)}, u32[]{:S(2)}, u32[]{:S(2)}) %collective-permute-start.24) | collective-permute-done | bytes 147488 | tf_op jit(solution)/shard_map/ppermute | solution.py:453
  155.9 3.2 %collective-permute-done.26.rest_2_ = bf16[384,384]{1,0:T(8,128)(2,1)S(1)} collective-permute-done((bf16[384,384]{1,0:T(8,128)(2,1)S(1)}, bf16[384,384]{1,0:T(8,128)(2,1)S(1)}, u32[]{:S(2)}, u32[]{:S(2)}) %collective-permute-start.26) | collective-permute-done | bytes 294944 | tf_op jit(solution)/shard_map/ppermute | solution.py:453
  161.7 3.7 %collective-permute-done.40.rest_2_ = bf16[384,384]{1,0:T(8,128)(2,1)S(1)} collective-permute-done((bf16[384,384]{1,0:T(8,128)(2,1)S(1)}, bf16[384,384]{1,0:T(8,128)(2,1)S(1)}, u32[]{:S(2)}, u32[]{:S(2)}) %collective-permute-start.40) | collective-permute-done | bytes 294944 | tf_op jit(solution)/shard_map/ppermute | solution.py:453
  168.1 3.7 %collective-permute-done.54.rest_2_ = bf16[384,384]{1,0:T(8,128)(2,1)S(1)} collective-permute-done((bf16[384,384]{1,0:T(8,128)(2,1)S(1)}, bf16[384,384]{1,0:T(8,128)(2,1)S(1)}, u32[]{:S(2)}, u32[]{:S(2)}) %collective-permute-start.54) | collective-permute-done | bytes 294944 | tf_op jit(solution)/shard_map/ppermute | solution.py:453
  171.7 2.1 %collective-permute-start.55 = (bf16[384,384]{1,0:T(8,128)(2,1)S(1)}, bf16[384,384]{1,0:T(8,128)(2,1)S(1)}, u32[]{:S(2)}, u32[]{:S(2)}) collective-permute-start(bf16[384,384]{1,0:T(8,128)(2,1)S(1)} %collective-permute-done.54.rest_2_), channel_id=1, source_target_pairs={{0,8},{1,17},{2,10},{3,19},{4,12},{5,21},{6,14},{7,23},{8,0},{9,25... | collective-permute-start | bytes 884744 | tf_op jit(solution)/shard_map/ppermute | solution.py:453
  175.7 2.9 %collective-permute-done.55.rest_3_ = bf16[384,384]{1,0:T(8,128)(2,1)S(1)} collective-permute-done((bf16[384,384]{1,0:T(8,128)(2,1)S(1)}, bf16[384,384]{1,0:T(8,128)(2,1)S(1)}, u32[]{:S(2)}, u32[]{:S(2)}) %collective-permute-start.55) | collective-permute-done | bytes 294944 | tf_op jit(solution)/shard_map/ppermute | solution.py:453
  178.8 2.9 %collective-permute-done.41.rest_3_ = bf16[384,384]{1,0:T(8,128)(2,1)S(1)} collective-permute-done((bf16[384,384]{1,0:T(8,128)(2,1)S(1)}, bf16[384,384]{1,0:T(8,128)(2,1)S(1)}, u32[]{:S(2)}, u32[]{:S(2)}) %collective-permute-start.41) | collective-permute-done | bytes 294944 | tf_op jit(solution)/shard_map/ppermute | solution.py:453
  182.8 2.7 %unpack_attention.1 = (f32[384,1152]{1,0:T(8,128)}, f32[384,384]{1,0:T(8,128)}, f32[384,768]{1,0:T(8,128)}, f32[384,192]{1,0:T(8,128)S(1)}, f32[384,384]{1,0:T(8...) custom-call(s32[3]{0:T(128)S(1)} %pad_add_fusion.info, ...), custom_call_target="tpu_custom_call" | custom-call | flops 1000000000 | bytes 1000000 | tf_op jit(solution)/shard_map/unpack_attention/pallas_call | solution.py:421
  189.7 3.2 %unpack_four.1 = (f32[384,1536]{1,0:T(8,128)}, f32[1536,384]{1,0:T(8,128)}) custom-call(s32[3]{0:T(128)S(1)} %pad_add_fusion.info, bf16[384,384]{1,0:T(8,128)(2,1)S(1)} %pad_maximum_fusion.3.rest_0_, bf16[384,384]{1,0:T(8,128)(2,1)S(1)} %collective-permute-done.53.rest_1_, bf16[384,384]{1,0:T(8,128)(2,1)S(1)} %collective-permute-done.54.rest_2_, ...), custom_call_target="tpu_custom_call" | custom-call | flops 1000000000 | bytes 1000000 | tf_op jit(solution)/shard_map/unpack_four/pallas_call | solution.py:421
  193.0 3.5 %unpack_two.1 = (f32[384,1536]{1,0:T(8,128)}, f32[1536,384]{1,0:T(8,128)}) custom-call(s32[3]{0:T(128)S(1)} %pad_add_fusion.info, bf16[384,384]{1,0:T(8,128)(2,1)S(1)} %pad_maximum_fusion.2.rest_0_, bf16[384,384]{1,0:T(8,128)(2,1)S(1)} %collective-permute-done.39.rest_1_, bf16[384,384]{1,0:T(8,128)(2,1)S(1)} %collective-permute-done.40.rest_2_, ...), custom_call_target="tpu_custom_call" | custom-call | flops 1000000000 | bytes 1000000 | tf_op jit(solution)/shard_map/unpack_two/pallas_call | solution.py:421
  (178 shorter events, 73.3 us)
Async XLA Ops:
  6.9 10.4 %collective-permute-start.1 = (bf16[384,384]{1,0:T(8,128)(2,1)S(1)}, bf16[384,384]{1,0:T(8,128)(2,1)S(1)}, u32[]{:S(2)}, u32[]{:S(2)}) collective-permute-start(bf16[384,384]{1,0:T(8,128)(2,1)S(1)} %get-tuple-element.118), channel_id=1, source_target_pairs={{0,16},{1,9},{2,18},{3,11},{4,20},{5,13},{6,22},{7,15},{8,24},{9,1... | collective-permute-start | bytes 884744 | tf_op jit(solution)/shard_map/ppermute | solution.py:453
  10.0 9.9 %collective-permute-start = (bf16[384,384]{1,0:T(8,128)(2,1)S(1)}, bf16[384,384]{1,0:T(8,128)(2,1)S(1)}, u32[]{:S(2)}, u32[]{:S(2)}) collective-permute-start(bf16[384,384]{1,0:T(8,128)(2,1)S(1)} %get-tuple-element.118), channel_id=1, source_target_pairs={{0,8},{1,17},{2,10},{3,19},{4,12},{5,21},{6,14},{7,23},{8,0},{9,25... | collective-permute-start | bytes 884744 | tf_op jit(solution)/shard_map/ppermute | solution.py:453
  11.5 12.1 %collective-permute-start.13 = (bf16[384,384]{1,0:T(8,128)(2,1)S(1)}, bf16[384,384]{1,0:T(8,128)(2,1)S(1)}, u32[]{:S(2)}, u32[]{:S(2)}) collective-permute-start(bf16[384,384]{1,0:T(8,128)(2,1)S(1)} %broadcast_select_fusion), channel_id=1, source_target_pairs={{0,16},{1,9},{2,18},{3,11},{4,20},{5,13},{6,22},{7,15},{8,24},{9,1... | collective-permute-start | bytes 884744 | tf_op jit(solution)/shard_map/ppermute | solution.py:453
  12.1 14.3 %collective-permute-start.12 = (bf16[384,384]{1,0:T(8,128)(2,1)S(1)}, bf16[384,384]{1,0:T(8,128)(2,1)}, u32[]{:S(2)}, u32[]{:S(2)}) collective-permute-start(bf16[384,384]{1,0:T(8,128)(2,1)S(1)} %broadcast_select_fusion), channel_id=1, source_target_pairs={{0,8},{1,17},{2,10},{3,19},{4,12},{5,21},{6,14},{7,23},{8,0},{9,25... | collective-permute-start | bytes 884744 | tf_op jit(solution)/shard_map/ppermute | solution.py:453
  12.2 20.3 %collective-permute-start.6 = (bf16[384,384]{1,0:T(8,128)(2,1)S(1)}, bf16[384,384]{1,0:T(8,128)(2,1)S(1)}, u32[]{:S(2)}, u32[]{:S(2)}) collective-permute-start(bf16[384,384]{1,0:T(8,128)(2,1)S(1)} %broadcast_select_fusion.1), channel_id=1, source_target_pairs={{0,8},{1,17},{2,10},{3,19},{4,12},{5,21},{6,14},{7,23},{8,0},{9,25... | collective-permute-start | bytes 884744 | tf_op jit(solution)/shard_map/ppermute | solution.py:453
  17.3 15.3 %collective-permute-start.7 = (bf16[384,384]{1,0:T(8,128)(2,1)S(1)}, bf16[384,384]{1,0:T(8,128)(2,1)S(1)}, u32[]{:S(2)}, u32[]{:S(2)}) collective-permute-start(bf16[384,384]{1,0:T(8,128)(2,1)S(1)} %broadcast_select_fusion.1), channel_id=1, source_target_pairs={{0,16},{1,9},{2,18},{3,11},{4,20},{5,13},{6,22},{7,15},{8,24},{9,1... | collective-permute-start | bytes 884744 | tf_op jit(solution)/shard_map/ppermute | solution.py:453
  19.9 14.7 %collective-permute-start.4 = (bf16[384,384]{1,0:T(8,128)(2,1)S(1)}, bf16[384,384]{1,0:T(8,128)(2,1)S(1)}, u32[]{:S(2)}, u32[]{:S(2)}) collective-permute-start(bf16[384,384]{1,0:T(8,128)(2,1)S(1)} %collective-permute-done.1.rest_3_), channel_id=1, source_target_pairs={{0,1},{1,0},{2,3},{3,2},{4,5},{5,4},{6,7},{7,6},{8,9},{9,8},{10,11... | collective-permute-start | bytes 884744 | tf_op jit(solution)/shard_map/ppermute | solution.py:453
  23.6 11.7 %collective-permute-start.2 = (bf16[384,384]{1,0:T(8,128)(2,1)S(1)}, bf16[384,384]{1,0:T(8,128)(2,1)}, u32[]{:S(2)}, u32[]{:S(2)}) collective-permute-start(bf16[384,384]{1,0:T(8,128)(2,1)S(1)} %collective-permute-done.rest_2_), channel_id=1, source_target_pairs={{0,16},{1,9},{2,18},{3,11},{4,20},{5,13},{6,22},{7,15},{8,24},{9,1... | collective-permute-start | bytes 884744 | tf_op jit(solution)/shard_map/ppermute | solution.py:453
  36.6 16.8 %collective-permute-start.9 = (bf16[384,384]{1,0:T(8,128)(2,1)S(1)}, bf16[384,384]{1,0:T(8,128)(2,1)S(1)}, u32[]{:S(2)}, u32[]{:S(2)}) collective-permute-start(bf16[384,384]{1,0:T(8,128)(2,1)S(1)} %collective-permute-done.6.rest_2_), channel_id=1, source_target_pairs={{0,1},{1,0},{2,3},{3,2},{4,5},{5,4},{6,7},{7,6},{8,9},{9,8},{10,11... | collective-permute-start | bytes 884744 | tf_op jit(solution)/shard_map/ppermute | solution.py:453
  39.3 14.0 %collective-permute-start.11 = (bf16[384,384]{1,0:T(8,128)(2,1)S(1)}, bf16[384,384]{1,0:T(8,128)(2,1)S(1)}, u32[]{:S(2)}, u32[]{:S(2)}) collective-permute-start(bf16[384,384]{1,0:T(8,128)(2,1)S(1)} %collective-permute-done.8.rest_4_), channel_id=1, source_target_pairs={{0,1},{1,0},{2,3},{3,2},{4,5},{5,4},{6,7},{7,6},{8,9},{9,8},{10,11... | collective-permute-start | bytes 884744 | tf_op jit(solution)/shard_map/ppermute | solution.py:453
  42.6 16.3 %collective-permute-start.15 = (bf16[384,384]{1,0:T(8,128)(2,1)}, bf16[384,384]{1,0:T(8,128)(2,1)S(1)}, u32[]{:S(2)}, u32[]{:S(2)}) collective-permute-start(bf16[384,384]{1,0:T(8,128)(2,1)} %collective-permute-done.12.rest_2_), channel_id=1, source_target_pairs={{0,1},{1,0},{2,3},{3,2},{4,5},{5,4},{6,7},{7,6},{8,9},{9,8},{10,11... | collective-permute-start | bytes 884744 | tf_op jit(solution)/shard_map/ppermute | solution.py:453
  42.6 16.2 %collective-permute-start.16 = (bf16[384,384]{1,0:T(8,128)(2,1)}, bf16[384,384]{1,0:T(8,128)(2,1)S(1)}, u32[]{:S(2)}, u32[]{:S(2)}) collective-permute-start(bf16[384,384]{1,0:T(8,128)(2,1)} %copy-done.7), channel_id=1, source_target_pairs={{0,1},{1,0},{2,3},{3,2},{4,5},{5,4},{6,7},{7,6},{8,9},{9,8},{10,11... | collective-permute-start | bytes 884744 | tf_op jit(solution)/shard_map/ppermute | solution.py:453
  43.1 15.8 %collective-permute-start.17 = (bf16[384,384]{1,0:T(8,128)(2,1)}, bf16[384,384]{1,0:T(8,128)(2,1)S(1)}, u32[]{:S(2)}, u32[]{:S(2)}) collective-permute-start(bf16[384,384]{1,0:T(8,128)(2,1)} %collective-permute-done.14.rest_4_), channel_id=1, source_target_pairs={{0,1},{1,0},{2,3},{3,2},{4,5},{5,4},{6,7},{7,6},{8,9},{9,8},{10,11... | collective-permute-start | bytes 884744 | tf_op jit(solution)/shard_map/ppermute | solution.py:453
  87.2 26.9 %collective-permute-start.19 = (bf16[384,384]{1,0:T(8,128)(2,1)S(1)}, bf16[384,384]{1,0:T(8,128)(2,1)S(1)}, u32[]{:S(2)}, u32[]{:S(2)}) collective-permute-start(bf16[384,384]{1,0:T(8,128)(2,1)S(1)} %get-tuple-element.125), channel_id=1, source_target_pairs={{0,8},{1,17},{2,10},{3,19},{4,12},{5,21},{6,14},{7,23},{8,0},{9,25... | collective-permute-start | bytes 884744 | tf_op jit(solution)/shard_map/ppermute | solution.py:453
  90.5 28.4 %collective-permute-start.33 = (bf16[384,384]{1,0:T(8,128)(2,1)S(1)}, bf16[384,384]{1,0:T(8,128)(2,1)S(1)}, u32[]{:S(2)}, u32[]{:S(2)}) collective-permute-start(bf16[384,384]{1,0:T(8,128)(2,1)S(1)} %get-tuple-element.123), channel_id=1, source_target_pairs={{0,8},{1,17},{2,10},{3,19},{4,12},{5,21},{6,14},{7,23},{8,0},{9,25... | collective-permute-start | bytes 884744 | tf_op jit(solution)/shard_map/ppermute | solution.py:453
  92.1 11.4 %collective-permute-start.34 = (bf16[384,384]{1,0:T(8,128)(2,1)S(1)}, bf16[384,384]{1,0:T(8,128)(2,1)S(1)}, u32[]{:S(2)}, u32[]{:S(2)}) collective-permute-start(bf16[384,384]{1,0:T(8,128)(2,1)S(1)} %get-tuple-element.124), channel_id=1, source_target_pairs={{0,8},{1,17},{2,10},{3,19},{4,12},{5,21},{6,14},{7,23},{8,0},{9,25... | collective-permute-start | bytes 884744 | tf_op jit(solution)/shard_map/ppermute | solution.py:453
  93.8 28.6 %collective-permute-start.47 = (bf16[384,384]{1,0:T(8,128)(2,1)S(1)}, bf16[384,384]{1,0:T(8,128)(2,1)S(1)}, u32[]{:S(2)}, u32[]{:S(2)}) collective-permute-start(bf16[384,384]{1,0:T(8,128)(2,1)S(1)} %get-tuple-element.121), channel_id=1, source_target_pairs={{0,8},{1,17},{2,10},{3,19},{4,12},{5,21},{6,14},{7,23},{8,0},{9,25... | collective-permute-start | bytes 884744 | tf_op jit(solution)/shard_map/ppermute | solution.py:453
  97.1 15.8 %collective-permute-start.48 = (bf16[384,384]{1,0:T(8,128)(2,1)S(1)}, bf16[384,384]{1,0:T(8,128)(2,1)S(1)}, u32[]{:S(2)}, u32[]{:S(2)}) collective-permute-start(bf16[384,384]{1,0:T(8,128)(2,1)S(1)} %get-tuple-element.122), channel_id=1, source_target_pairs={{0,8},{1,17},{2,10},{3,19},{4,12},{5,21},{6,14},{7,23},{8,0},{9,25... | collective-permute-start | bytes 884744 | tf_op jit(solution)/shard_map/ppermute | solution.py:453
  103.4 12.7 %collective-permute-start.21 = (bf16[384,384]{1,0:T(8,128)(2,1)S(1)}, bf16[384,384]{1,0:T(8,128)(2,1)S(1)}, u32[]{:S(2)}, u32[]{:S(2)}) collective-permute-start(bf16[384,384]{1,0:T(8,128)(2,1)S(1)} %fusion.6), channel_id=1, source_target_pairs={{0,16},{1,9},{2,18},{3,11},{4,20},{5,13},{6,22},{7,15},{8,24},{9,1... | collective-permute-start | bytes 884744 | tf_op jit(solution)/shard_map/ppermute | solution.py:453
  125.7 16.6 %collective-permute-start.23 = (bf16[192,384]{1,0:T(8,128)(2,1)S(1)}, bf16[192,384]{1,0:T(8,128)(2,1)S(1)}, u32[]{:S(2)}, u32[]{:S(2)}) collective-permute-start(bf16[192,384]{1,0:T(8,128)(2,1)S(1)} %add_convert_fusion.11), channel_id=1, source_target_pairs={{0,4},{1,5},{2,6},{3,7},{4,0},{5,1},{6,2},{7,3},{8,12},{9,13},{10,... | collective-permute-start | bytes 442376 | tf_op jit(solution)/shard_map/ppermute | solution.py:453
  129.0 15.9 %collective-permute-start.37 = (bf16[192,384]{1,0:T(8,128)(2,1)S(1)}, bf16[192,384]{1,0:T(8,128)(2,1)S(1)}, u32[]{:S(2)}, u32[]{:S(2)}) collective-permute-start(bf16[192,384]{1,0:T(8,128)(2,1)S(1)} %add_convert_fusion.9), channel_id=1, source_target_pairs={{0,4},{1,5},{2,6},{3,7},{4,0},{5,1},{6,2},{7,3},{8,12},{9,13},{10,... | collective-permute-start | bytes 442376 | tf_op jit(solution)/shard_map/ppermute | solution.py:453
  132.3 14.2 %collective-permute-start.51 = (bf16[192,384]{1,0:T(8,128)(2,1)S(1)}, bf16[192,384]{1,0:T(8,128)(2,1)S(1)}, u32[]{:S(2)}, u32[]{:S(2)}) collective-permute-start(bf16[192,384]{1,0:T(8,128)(2,1)S(1)} %add_convert_fusion.7), channel_id=1, source_target_pairs={{0,4},{1,5},{2,6},{3,7},{4,0},{5,1},{6,2},{7,3},{8,12},{9,13},{10,... | collective-permute-start | bytes 442376 | tf_op jit(solution)/shard_map/ppermute | solution.py:453
  152.8 12.6 %collective-permute-start.40 = (bf16[384,384]{1,0:T(8,128)(2,1)S(1)}, bf16[384,384]{1,0:T(8,128)(2,1)S(1)}, u32[]{:S(2)}, u32[]{:S(2)}) collective-permute-start(bf16[384,384]{1,0:T(8,128)(2,1)S(1)} %pad_maximum_fusion.2.rest_0_), channel_id=1, source_target_pairs={{0,16},{1,9},{2,18},{3,11},{4,20},{5,13},{6,22},{7,15},{8,24},{9,1... | collective-permute-start | bytes 884744 | tf_op jit(solution)/shard_map/ppermute | solution.py:453
  154.3 12.3 %collective-permute-start.39 = (bf16[384,384]{1,0:T(8,128)(2,1)S(1)}, bf16[384,384]{1,0:T(8,128)(2,1)S(1)}, u32[]{:S(2)}, u32[]{:S(2)}) collective-permute-start(bf16[384,384]{1,0:T(8,128)(2,1)S(1)} %pad_maximum_fusion.2.rest_0_), channel_id=1, source_target_pairs={{0,8},{1,17},{2,10},{3,19},{4,12},{5,21},{6,14},{7,23},{8,0},{9,25... | collective-permute-start | bytes 884744 | tf_op jit(solution)/shard_map/ppermute | solution.py:453
  155.9 12.2 %collective-permute-start.56 = (bf16[384,384]{1,0:T(8,128)(2,1)S(1)}, bf16[384,384]{1,0:T(8,128)(2,1)S(1)}, u32[]{:S(2)}, u32[]{:S(2)}) collective-permute-start(bf16[384,384]{1,0:T(8,128)(2,1)S(1)} %pad_maximum_fusion.3.rest_0_), channel_id=1, source_target_pairs={{0,1},{1,0},{2,3},{3,2},{4,5},{5,4},{6,7},{7,6},{8,9},{9,8},{10,11... | collective-permute-start | bytes 884744 | tf_op jit(solution)/shard_map/ppermute | solution.py:453
  159.1 12.6 %collective-permute-start.54 = (bf16[384,384]{1,0:T(8,128)(2,1)S(1)}, bf16[384,384]{1,0:T(8,128)(2,1)S(1)}, u32[]{:S(2)}, u32[]{:S(2)}) collective-permute-start(bf16[384,384]{1,0:T(8,128)(2,1)S(1)} %pad_maximum_fusion.3.rest_0_), channel_id=1, source_target_pairs={{0,16},{1,9},{2,18},{3,11},{4,20},{5,13},{6,22},{7,15},{8,24},{9,1... | collective-permute-start | bytes 884744 | tf_op jit(solution)/shard_map/ppermute | solution.py:453
  160.2 13.6 %collective-permute-start.53 = (bf16[384,384]{1,0:T(8,128)(2,1)S(1)}, bf16[384,384]{1,0:T(8,128)(2,1)S(1)}, u32[]{:S(2)}, u32[]{:S(2)}) collective-permute-start(bf16[384,384]{1,0:T(8,128)(2,1)S(1)} %pad_maximum_fusion.3.rest_0_), channel_id=1, source_target_pairs={{0,8},{1,17},{2,10},{3,19},{4,12},{5,21},{6,14},{7,23},{8,0},{9,25... | collective-permute-start | bytes 884744 | tf_op jit(solution)/shard_map/ppermute | solution.py:453
  178.6 10.2 %collective-permute-start.59 = (bf16[384,384]{1,0:T(8,128)(2,1)S(1)}, bf16[384,384]{1,0:T(8,128)(2,1)}, u32[]{:S(2)}, u32[]{:S(2)}) collective-permute-start(bf16[384,384]{1,0:T(8,128)(2,1)S(1)} %collective-permute-done.55.rest_3_), channel_id=1, source_target_pairs={{0,1},{1,0},{2,3},{3,2},{4,5},{5,4},{6,7},{7,6},{8,9},{9,8},{10,11... | collective-permute-start | bytes 884744 | tf_op jit(solution)/shard_map/ppermute | solution.py:453
  181.7 11.2 %collective-permute-start.42 = (bf16[384,384]{1,0:T(8,128)(2,1)S(1)}, bf16[384,384]{1,0:T(8,128)(2,1)}, u32[]{:S(2)}, u32[]{:S(2)}) collective-permute-start(bf16[384,384]{1,0:T(8,128)(2,1)S(1)} %pad_maximum_fusion.2.rest_0_), channel_id=1, source_target_pairs={{0,1},{1,0},{2,3},{3,2},{4,5},{5,4},{6,7},{7,6},{8,9},{9,8},{10,11... | collective-permute-start | bytes 884744 | tf_op jit(solution)/shard_map/ppermute | solution.py:453
  181.8 11.1 %collective-permute-start.44 = (bf16[384,384]{1,0:T(8,128)(2,1)S(1)}, bf16[384,384]{1,0:T(8,128)(2,1)}, u32[]{:S(2)}, u32[]{:S(2)}) collective-permute-start(bf16[384,384]{1,0:T(8,128)(2,1)S(1)} %collective-permute-done.40.rest_2_), channel_id=1, source_target_pairs={{0,1},{1,0},{2,3},{3,2},{4,5},{5,4},{6,7},{7,6},{8,9},{9,8},{10,11... | collective-permute-start | bytes 884744 | tf_op jit(solution)/shard_map/ppermute | solution.py:453
  182.2 10.7 %collective-permute-start.43 = (bf16[384,384]{1,0:T(8,128)(2,1)S(1)}, bf16[384,384]{1,0:T(8,128)(2,1)}, u32[]{:S(2)}, u32[]{:S(2)}) collective-permute-start(bf16[384,384]{1,0:T(8,128)(2,1)S(1)} %collective-permute-done.39.rest_1_), channel_id=1, source_target_pairs={{0,1},{1,0},{2,3},{3,2},{4,5},{5,4},{6,7},{7,6},{8,9},{9,8},{10,11... | collective-permute-start | bytes 884744 | tf_op jit(solution)/shard_map/ppermute | solution.py:453
  182.4 10.6 %collective-permute-start.45 = (bf16[384,384]{1,0:T(8,128)(2,1)S(1)}, bf16[384,384]{1,0:T(8,128)(2,1)}, u32[]{:S(2)}, u32[]{:S(2)}) collective-permute-start(bf16[384,384]{1,0:T(8,128)(2,1)S(1)} %collective-permute-done.41.rest_3_), channel_id=1, source_target_pairs={{0,1},{1,0},{2,3},{3,2},{4,5},{5,4},{6,7},{7,6},{8,9},{9,8},{10,11... | collective-permute-start | bytes 884744 | tf_op jit(solution)/shard_map/ppermute | solution.py:453
  (48 other events, 324.4 us)

commit v3 on v2

v3 whole, which is shorter than its diff:
```python
import functools

import jax
import jax.numpy as jnp
from jax import lax
from jax.experimental import pallas as pl
from jax.experimental.pallas import tpu as pltpu
from jax.sharding import PartitionSpec as P

D = 384
HEADS = 6
HEAD = 64
SHARED = 3
QUARTERS = 4

EPSILON = 1e-05
MASKED = -1e30
GELU_SCALE = 0.7978845608028654
GELU_CUBE = 0.044715

f32 = jnp.float32
bf16 = jnp.bfloat16


def nn(left, right):
    return jnp.dot(left, right, preferred_element_type=f32)


def nt(left, right):
    return lax.dot_general(left, right, (((1,), (1,)), ((), ())), preferred_element_type=f32)


def centre(hidden):
    centred = hidden - jnp.mean(hidden, -1, keepdims=True)
    spread = jnp.mean(centred * centred, -1, keepdims=True)
    rstd = lax.rsqrt(spread + EPSILON)
    return centred * rstd, rstd


def norm_back(scaled, rstd, gain, grad):
    grad_gain = jnp.sum(grad * scaled, 0, keepdims=True)
    c = grad * gain
    along = jnp.mean(c * scaled, -1, keepdims=True)
    return rstd * (c - jnp.mean(c, -1, keepdims=True) - scaled * along), grad_gain


def swapped(rank):
    return ((rank & 1) << 1) | (rank >> 1)


def place():
    return lax.axis_index("section"), lax.axis_index("dp") & 1


def select_pieces(pieces):
    near, far, both, other_near, other_far, other_both = pieces
    first = place()[1] == 0

    def pick(left, right):
        return jnp.where(first, left[...], right[...])

    return (
        (pick(near, other_near), pick(far, other_far), pick(both, other_both)),
        (pick(other_far, far), pick(other_near, near), pick(other_both, both)),
    )


def put(keep, send, rank, half_zero, half_one, rows=None):
    first = place()[1] == 0
    zero, one = rank, swapped(rank)
    kept, sent = jnp.where(first, zero, one), jnp.where(first, one, zero)
    if rows is None:
        keep[kept] = jnp.where(first, half_zero, half_one)
        send[sent] = jnp.where(first, half_one, half_zero)
    else:
        keep[kept, pl.ds(*rows)] = jnp.where(first, half_zero, half_one)
        send[sent, pl.ds(*rows)] = jnp.where(first, half_one, half_zero)


def usable(rows, limits):
    key_index = lax.broadcasted_iota(jnp.int32, (rows, rows), 0)
    query_index = lax.broadcasted_iota(jnp.int32, (rows, rows), 1)
    return (key_index <= query_index) & (key_index < limits[0:1, :rows])


def head_lanes(rows, side):
    lane = lax.broadcasted_iota(jnp.int32, (rows, 2 * HEAD), 1)
    return (lane < HEAD) if side == 0 else (lane >= HEAD)


def attend(mixed, limits, probabilities):
    rows = mixed.shape[0]
    allowed = usable(rows, limits)
    values_across = mixed[:, 2 * D :].T
    outs = []
    for pair in range(HEADS // 2):
        at = 2 * HEAD * pair
        queries = mixed[:, at : at + 2 * HEAD]
        key_rows = mixed[:, D + at : D + at + 2 * HEAD]
        for side in range(2):
            head = 2 * pair + side
            one_head = jnp.where(head_lanes(rows, side), queries, 0)
            scores = jnp.where(allowed, nt(key_rows, one_head) * HEAD ** (-0.5), MASKED)
            peak = jnp.max(scores, 0, keepdims=True)
            raised = jnp.exp(scores - peak)
            inverse = 1.0 / jnp.sum(raised, 0, keepdims=True)
            probability = raised * inverse
            probabilities[head] = probability
            outs.append(nn(values_across[HEAD * head : HEAD * head + HEAD], probability.astype(bf16)))
    return jnp.concatenate(outs, 0).T.astype(bf16)


def attend_back(mixed, grad_heads, probabilities, grad_mixed):
    rows = mixed.shape[0]
    keys_across = mixed[:, D : 2 * D].T
    query_parts = []
    for pair in range(HEADS // 2):
        at = 2 * HEAD * pair
        queries = mixed[:, at : at + 2 * HEAD]
        values = mixed[:, 2 * D + at : 2 * D + at + 2 * HEAD]
        grads = grad_heads[:, at : at + 2 * HEAD]
        key_grad = jnp.zeros((rows, 2 * HEAD), f32)
        value_grad = jnp.zeros((rows, 2 * HEAD), f32)
        for side in range(2):
            head = 2 * pair + side
            lanes = head_lanes(rows, side)
            one_head = jnp.where(lanes, queries, 0)
            one_grad = jnp.where(lanes, grads, 0)
            probability = probabilities[head]
            grad_prob = nt(values, one_grad)
            middle = jnp.sum(probability * grad_prob, 0, keepdims=True)
            grad_scores = (probability * (grad_prob - middle)).astype(bf16)
            key_grad += nn(grad_scores, one_head)
            value_grad += nn(probability.astype(bf16), one_grad)
            query_parts.append(nn(keys_across[HEAD * head : HEAD * head + HEAD], grad_scores))
        grad_mixed[:, D + at : D + at + 2 * HEAD] = (key_grad * HEAD ** (-0.5)).astype(bf16)
        grad_mixed[:, 2 * D + at : 2 * D + at + 2 * HEAD] = value_grad.astype(bf16)
    grad_mixed[:, :D] = (jnp.concatenate(query_parts, 0).T * HEAD ** (-0.5)).astype(bf16)


def prepare_kernel(
    mixing, output, pair, fresh, output_three, gain_one, gain_two, gain_three, gain_four,
    up_two, down_two, up_four, down_four, lengths,
    one, three, mine_one, mine_two, mine_four, limits, edge, narrow_one, narrow_two, narrow_three, narrow_four, sems,
):
    core = place()[1]
    count = mixing.shape[0]
    wide, small = output.shape[0], fresh.shape[0]
    halves = [[(mixing, 0), (output, count)],
              [(pair, 0), (fresh, 2 * wide), (output_three, 2 * wide + small)]]
    last = 3 * wide + small
    copies = []
    for half, target in ((0, one), (1, three)):
        for source, row in halves[half]:
            rows = source.shape[0]
            copies.append((None, source, target.at[pl.ds(row, rows)]))
            copies.append((half, source, mine_one.at[pl.ds(row, rows)]))
    copies += [(0, up_two, mine_two), (1, down_two, mine_two)]
    copies += [(0, up_four, mine_four), (1, down_four, mine_four)]
    made = [
        (half, pltpu.make_async_copy(source, target, sems.at[i]))
        for i, (half, source, target) in enumerate(copies)
    ]
    for half, copy in made:
        if half is None:
            copy.start()
        else:
            pl.when(core == half)(copy.start)
    gains = [
        pltpu.make_async_copy(gain, narrow, sems.at[len(copies) + k])
        for k, (gain, narrow) in enumerate(
            ((gain_one, narrow_one), (gain_two, narrow_two), (gain_three, narrow_three), (gain_four, narrow_four))
        )
    ]
    for copy in gains:
        copy.start()
    limits[...] = jnp.full(limits.shape, lengths[0, place()[0]], jnp.int32)
    edge[...] = jnp.zeros_like(edge)
    for k, narrow in enumerate((narrow_one, narrow_two, narrow_three, narrow_four)):
        gains[k].wait()
        edge[k : k + 1, : narrow.shape[0]] = narrow[...].astype(f32).reshape(1, narrow.shape[0])
    rows = D - last
    block = jnp.concatenate([edge[...], jnp.zeros((rows - 8, D), f32)], 0).astype(bf16)
    three[last:] = block

    @pl.when(core != 0)
    def _():
        mine_one[last:] = block

    for half, copy in made:
        if half is None:
            copy.wait()
        else:
            pl.when(core == half)(copy.wait)


def first_kernel(limits, tokens, own0, own1, *rest):
    h1, mixed, attended, probabilities, mixing, output, mixing_three, output_three, gains, held = rest[6:]
    section = place()[0]
    for half, (own, came) in enumerate(zip((own0, own1), select_pieces(rest[:6]))):
        held[half, section] = own[...]
        for rank in (1, 2, 3):
            held[half, section ^ rank] = came[rank - 1]
    shared_width = SHARED * HEAD
    mixing_three[2 * D : 2 * D + shared_width, :] = jnp.zeros((shared_width, D), bf16)
    for j in range(QUARTERS):
        mixing[288 * j : 288 * j + 288, :] = held[0, j, :288]
        output[96 * j : 96 * j + 96, :] = held[0, j, 288:]
        mixing_three[192 * j : 192 * j + 192, :] = held[1, j, :192]
        mixing_three[960 + 48 * j : 960 + 48 * j + 48, :] = held[1, j, 192:240]
        output_three[96 * j : 96 * j + 96, :] = held[1, j, 240:336]
        gains[0:8, 96 * j : 96 * j + 96] = held[1, j, 336:352, :96].astype(f32)[:8]
    hidden = tokens[...].astype(f32)
    scaled, _ = centre(hidden)
    normed = (scaled * gains[0:1, :]).astype(bf16)
    mixed[...] = nt(normed, mixing[...]).astype(bf16)
    attended[...] = attend(mixed, limits, probabilities)
    h1[...] = (hidden + nt(attended[...], output[...])).astype(bf16)


def bring(own0, own1, held, sems):
    copies = [
        pltpu.make_async_copy(own0, held.at[0, 0], sems.at[0]),
        pltpu.make_async_copy(own1, held.at[1, 0], sems.at[1]),
    ]
    for copy in copies:
        copy.start()
    return copies


def middle_kernel(limits, h1, gains, mixing_three, output_three, mixed_one, own0, own1, *rest):
    h2, held, h3, mixed, attended, probabilities, actives, slopes, sems = rest[6:]
    copies = bring(own0, own1, held, sems)
    hidden = h1[...].astype(f32)
    scaled, _ = centre(hidden)
    normed = (scaled * gains[1:2, :]).astype(bf16)
    ups, downs = select_pieces(rest[:6])
    total = hidden
    for rank in (1, 2, 3, 0):
        if rank:
            held[0, rank], held[1, rank] = ups[rank - 1], downs[rank - 1]
        else:
            for copy in copies:
                copy.wait()
        active, slope = feed_parts(nn(normed, held[0, rank]))
        actives[rank] = active
        slopes[rank] = slope
        total += nn(active, held[1, rank])
    h2[...] = total.astype(bf16)
    hidden = h2[...].astype(f32)
    scaled, _ = centre(hidden)
    normed = (scaled * gains[2:3, :]).astype(bf16)
    mixed[...] = nt(normed, mixing_three[...]).astype(bf16)
    shared_width = SHARED * HEAD
    mixed[:, 2 * D : 2 * D + shared_width] = mixed_one[:, 2 * D : 2 * D + shared_width]
    attended[...] = attend(mixed, limits, probabilities)
    h3[...] = (hidden + nt(attended[...], output_three[...])).astype(bf16)


def feed_parts(upward):
    square = upward * upward
    rising = 0.5 + 0.5 * jnp.tanh(upward * (GELU_SCALE + (GELU_SCALE * GELU_CUBE) * square))
    active = upward * rising
    steep = 2.0 * GELU_SCALE + (6.0 * GELU_SCALE * GELU_CUBE) * square
    return active.astype(bf16), rising + active * (1.0 - rising) * steep


def quarter_back(up, down, normed_across, grad_out, active, slope):
    grad_upward = (nt(grad_out, down) * slope).astype(bf16)
    grad_down = nn(active.T, grad_out).astype(bf16)
    return nn(normed_across, grad_upward).astype(bf16), grad_down, nt(grad_upward, up)


def seeded(limits, cotangent):
    row = lax.broadcasted_iota(jnp.int32, cotangent.shape, 0)
    return jnp.where(row < limits[0:1, :1], cotangent[...].astype(f32), 0.0)


def fourth_kernel(limits, h3, gains, cotangent, own0, own1, near, far, other_near, other_far, *rest):
    total, grad_normed, keep, send, held, sems = rest
    copies = bring(own0, own1, held, sems)
    hidden = h3[...].astype(f32)
    scaled, _ = centre(hidden)
    normed = (scaled * gains[3:4, :]).astype(bf16)
    normed_across = normed.T
    grad_out = seeded(limits, cotangent).astype(bf16)
    first = place()[1] == 0
    after, grads = hidden, jnp.zeros(hidden.shape, f32)
    for rank in (1, 2, 0):
        if rank == 1:
            up = jnp.where(first, near[...], other_near[...])
            down = jnp.where(first, other_far[...], far[...])
        elif rank == 2:
            up = jnp.where(first, far[...], other_far[...])
            down = jnp.where(first, other_near[...], near[...])
        else:
            for copy in copies:
                copy.wait()
            up, down = held[0, 0], held[1, 0]
        active, slope = feed_parts(nn(normed, up))
        after += nn(active, down)
        grad_up, grad_down, grad = quarter_back(up, down, normed_across, grad_out, active, slope)
        put(keep, send, rank, grad_up, grad_down)
        grads += grad
    total[...] = after
    grad_normed[...] = grads


def fourth_end_kernel(
    limits, h3, gains, cotangent, total, grads, both, other_both, out, grad_h3, keep, send, grad_gain
):
    scaled, rstd = centre(h3[...].astype(f32))
    gain = gains[3:4, :]
    normed = (scaled * gain).astype(bf16)
    grad_out = seeded(limits, cotangent)
    first = place()[1] == 0
    up = jnp.where(first, both[...], other_both[...])
    down = jnp.where(first, other_both[...], both[...])
    active, slope = feed_parts(nn(normed, up))
    out[...] = total[...] + nn(active, down)
    grad_up, grad_down, grad = quarter_back(up, down, normed.T, grad_out.astype(bf16), active, slope)
    keep[...] = jnp.where(first, grad_up, grad_down)
    send[...] = jnp.where(first, grad_down, grad_up)
    grad_hidden, one_gain = norm_back(scaled, rstd, gain, grads[...] + grad)
    grad_gain[0:1, :] = one_gain
    grad_h3[...] = (grad_out + grad_hidden).astype(bf16)


def attention_back(hidden, grad_out, mixed, attended, probabilities, mixing, output, gain, grad_mixed, shared, value_grad):
    scaled, rstd = centre(hidden)
    normed_across = (scaled * gain).astype(bf16).T
    grad_heads = nn(grad_out, output[...]).astype(bf16)
    grad_output = nn(attended[...].T, grad_out).astype(bf16)
    attend_back(mixed, grad_heads, probabilities, grad_mixed)
    shared(grad_mixed)
    grad_pair = nn(normed_across, grad_mixed[:, : 2 * D]).astype(bf16)
    grad_values = value_grad(scaled, gain, normed_across, grad_mixed)
    grad_hidden, grad_gain = norm_back(scaled, rstd, gain, nn(grad_mixed[...], mixing[...]))
    return grad_hidden, grad_gain, grad_pair, grad_values, grad_output


def third_back_kernel(
    h2, gains, grad_h3, mixed, attended, probabilities, mixing, output,
    grad_h2, grad_weights, grad_shared, grad_gain, grad_mixed,
):
    shared_width = SHARED * HEAD

    def hand_over(grads):
        grad_shared[...] = grads[:, 2 * D : 2 * D + shared_width]
        grads[:, 2 * D : 2 * D + shared_width] = jnp.zeros((grads.shape[0], shared_width), bf16)

    def fresh_grad(scaled, gain, normed_across, grads):
        across = grads[:, 2 * D + 2 * HEAD :].T
        return nn(across[HEAD:], (scaled * gain).astype(bf16)).astype(bf16)

    grad_hidden, one_gain, grad_pair, grad_fresh, grad_output = attention_back(
        h2[...].astype(f32), grad_h3[...], mixed, attended, probabilities, mixing, output,
        gains[2:3, :], grad_mixed, hand_over, fresh_grad,
    )
    grad_weights[0, :D] = grad_pair[:, :D]
    grad_weights[0, D:] = grad_pair[:, D:]
    grad_weights[1, :shared_width] = jnp.zeros((shared_width, D), bf16)
    grad_weights[1, shared_width:D] = grad_fresh
    grad_weights[1, D:] = grad_output
    grad_gain[0:1, :] = one_gain
    grad_h2[...] = (grad_h3[...].astype(f32) + grad_hidden).astype(bf16)


def second_back_kernel(h1, gains, grad_h2, held, actives, slopes, grad_h1, keep, send, grad_gain):
    scaled, rstd = centre(h1[...].astype(f32))
    gain = gains[1:2, :]
    normed_across = (scaled * gain).astype(bf16).T
    grads = jnp.zeros(scaled.shape, f32)
    for rank in range(QUARTERS):
        grad_up, grad_down, grad = quarter_back(
            held[0, rank], held[1, rank], normed_across, grad_h2[...], actives[rank], slopes[rank]
        )
        put(keep, send, rank, grad_up, grad_down)
        grads += grad
    grad_hidden, one_gain = norm_back(scaled, rstd, gain, grads)
    grad_gain[0:1, :] = one_gain
    grad_h1[...] = (grad_h2[...].astype(f32) + grad_hidden).astype(bf16)


def first_back_kernel(
    tokens, gains, grad_h1, mixed, attended, probabilities, mixing, output,
    grad_shared, third_weights, gain_two, gain_three, gain_four,
    input_grad, keep, send, grad_mixed,
):
    shared_width = SHARED * HEAD

    def take_over(grads):
        at = slice(2 * D, 2 * D + shared_width)
        grads[:, at] = (grads[:, at].astype(f32) + grad_shared[...].astype(f32)).astype(bf16)

    def value_grad(scaled, gain, normed_across, grads):
        return nn(normed_across, grads[:, 2 * D :]).astype(bf16)

    grad_hidden, gain_one, grad_pair, grad_values, grad_output = attention_back(
        tokens[...].astype(f32), grad_h1[...], mixed, attended, probabilities, mixing, output,
        gains[0:1, :], grad_mixed, take_over, value_grad,
    )
    input_grad[...] = grad_h1[...].astype(f32) + grad_hidden
    section, part = place()[0], D // 2
    gain_rows = jnp.concatenate(
        [gain_one, gain_two[0:1, :], gain_three[0:1, :], gain_four[0:1, :], jnp.zeros((12, D), f32)], 0
    ).astype(bf16)
    for j in range(QUARTERS):
        at = slice(part * (j % 2), part * (j % 2) + part)
        zero = (grad_pair[:, :D], grad_pair[:, D:])[j // 2][at]
        one = (grad_values, grad_output)[j // 2][at]
        put(keep, send, section ^ j, zero, one, (0, part))
        below = third_weights[1, part * j : part * j + part]
        if j == 0:
            below = jnp.concatenate([gain_rows, below[16:]], 0)
        put(keep, send, section ^ j, third_weights[0, part * j : part * j + part], below, (part, part))


def pieces_of(refs):
    for own, (mine, far, pair) in ((True, refs[:3]), (False, refs[3:])):
        yield own, 0, mine[...]
        yield own, 2, far[...]
        yield own, 1, pair[0]
        yield own, 3, pair[1]


def unpack_feed_kernel(*rest):
    up, down, wide, sems = rest[6:]
    section, core = place()
    steps = []
    for slot, (own, rank, value) in enumerate(pieces_of(rest[:6])):
        wide[slot] = value.astype(f32)
        zero = (core == 0) if own else (core != 0)
        column = pl.ds(pl.multiple_of((section ^ rank) * D, D), D)
        below = pl.ds(pl.multiple_of((section ^ swapped(rank)) * D, D), D)
        steps += [
            (zero, pltpu.make_async_copy(wide.at[slot], up.at[:, column], sems.at[slot])),
            (jnp.logical_not(zero), pltpu.make_async_copy(wide.at[slot], down.at[below, :], sems.at[slot])),
        ]
        for flag, copy in steps[-2:]:
            pl.when(flag)(copy.start)
    for flag, copy in steps:
        pl.when(flag)(copy.wait)


def unpack_attention_kernel(*rest):
    mixing, output, pair, fresh, output_three, g1, g2, g3, g4, wide, sems = rest[6:]
    section, core = place()
    part = D // 2
    steps = []
    for slot, (own, rank, value) in enumerate(pieces_of(rest[:6])):
        wide[slot] = value.astype(f32)
        zero = (core == 0) if own else (core != 0)
        j0, j1 = section ^ rank, section ^ swapped(rank)
        column = pl.ds(pl.multiple_of((j0 >> 1) * D, D), D)
        row0 = pl.ds(pl.multiple_of((j0 & 1) * part, part), part)
        row1 = pl.ds(pl.multiple_of((j1 & 1) * part, part), part)
        one = jnp.logical_not(zero)

        @pl.when(one & (j1 == 0))
        def _():
            for k, ref in enumerate((g1, g2, g3, g4)):
                ref[...] = wide[slot, part + k]

        for low, flag, target in (
            (0, zero, mixing.at[row0, column]),
            (1, zero, pair.at[row0, column]),
            (0, one & (j1 < 2), mixing.at[row1, 2 * D :]),
            (1, one & (j1 == 1), fresh),
            (0, one & (j1 >= 2), output.at[row1, :]),
            (1, one & (j1 >= 2), output_three.at[row1, :]),
        ):
            copy = pltpu.make_async_copy(
                wide.at[slot, part * low : part * low + part], target, sems.at[slot, low]
            )
            steps.append((flag, copy))
            pl.when(flag)(copy.start)
    for flag, copy in steps:
        pl.when(flag)(copy.wait)


SMEM, VMEM, HBM = pltpu.SMEM, pltpu.VMEM, pltpu.HBM


def call(body, name, args, outs, scratch=(), spaces=None, limit=12, hint=20):
    spaces = spaces or {}
    args = [
        pltpu.with_memory_space_constraint(arg, HBM) if spaces.get(i) is HBM else arg
        for i, arg in enumerate(args)
    ]
    places = {"vmem": VMEM, "hbm": HBM}
    return pl.pallas_call(
        body,
        name=name,
        out_shape=[
            places[where](shape, dtype) if where in places else jax.ShapeDtypeStruct(shape, dtype)
            for shape, dtype, where in outs
        ],
        in_specs=[pl.BlockSpec(memory_space=spaces.get(i, VMEM)) for i in range(len(args))],
        out_specs=[pl.BlockSpec(memory_space=places.get(where, VMEM)) for _, _, where in outs],
        scratch_shapes=list(scratch),
        compiler_params=pltpu.CompilerParams(vmem_limit_bytes=limit * 1024 * 1024),
        cost_estimate=pl.CostEstimate(flops=hint * 10**9, bytes_accessed=1, transcendentals=1),
    )(*args)


def partner_pairs(sections, groups, kind):
    found = []
    for section in range(sections):
        for group in range(groups):
            core = group & 1
            to_section, to_group = section, group
            if kind == "near":
                to_section = section ^ (1 if core == 0 else 2)
            elif kind == "far":
                to_section = section ^ (2 if core == 0 else 1)
            else:
                to_group = group ^ kind
            found.append((section * groups + group, to_section * groups + to_group))
    return found


def partner(value, kind):
    sections, groups = lax.axis_size("section"), lax.axis_size("dp")
    return lax.ppermute(value, ("section", "dp"), partner_pairs(sections, groups, kind))


def total(*parts):
    return sum(part.astype(f32) for part in parts).astype(bf16)


def chip_bit():
    return (lax.axis_index("dp") >> 1) & 1


def one_sum_kernel(index, keep, came, out):
    out[...] = total(keep[index], came[index])


def begin_kernel(keep, came, both, near):
    both[...] = total(keep[3], came[3])
    near[...] = total(keep[1], came[1])


def turn_kernel(keep, came, both, far):
    far[...] = total(keep[2], came[2], both[...])


def own_kernel(keep, came, near, far, away, kept, halves):
    rows = kept.shape[0]
    own = total(keep[0], came[0], near[...], far[...])
    halves[0] = own[:rows]
    halves[1] = own[rows:]
    bit = chip_bit()
    kept[...] = halves[bit]
    away[...] = halves[1 - bit]


def copy_kernel(value, out):
    out[...] = value[...]


def pair_kernel(left, right, out):
    out[0] = left[...]
    out[1] = right[...]


def sum_kernel(left, right, out):
    out[...] = total(left[...], right[...])


def join_kernel(kept, back, own):
    rows = kept.shape[0]
    bit = chip_bit()
    own[pl.ds(pl.multiple_of(bit * rows, rows), rows)] = kept[...]
    own[pl.ds(pl.multiple_of((1 - bit) * rows, rows), rows)] = back[...]


class Line:
    def __init__(self):
        self.last = ()

    def tied(self, *values):
        if not self.last:
            return values
        return lax.optimization_barrier(values + self.last)[: len(values)]

    def step(self, made, *values):
        made = made(*self.tied(*values))
        self.last = (jax.tree.leaves(made)[0],)
        return made

    def hop(self, value, kind):
        return partner(self.tied(value)[0], kind)

    def gate(self, value, hint):
        copy = [(value.shape, value.dtype, "vmem")]
        return self.step(lambda v: call(copy_kernel, "gate", (v,), copy, limit=4, hint=hint)[0], value)


class Chunk:
    def __init__(self, line, keep, send):
        self.line, self.keep = line, keep
        self.came = partner(send, 1)
        self.groups = lax.axis_size("dp")

    def made(self, hint, body, name, outs, *args, scratch=()):
        return self.line.step(
            lambda *tied: call(
                body, name, tied, [(shape, bf16, "vmem") for shape in outs], scratch, limit=4, hint=hint
            ),
            *args,
        )

    def begin(self, hint):
        block = self.keep.shape[1:]
        both, near = self.made(hint, begin_kernel, "sum_begin", [block] * 2, self.keep, self.came)
        self.both, self.near = partner(both, "near"), partner(near, "near")

    def begin_near(self, hint):
        body = functools.partial(one_sum_kernel, 1)
        (near,) = self.made(hint, body, "sum_near", [self.keep.shape[1:]], self.keep, self.came)
        self.near = partner(near, "near")

    def begin_both(self, keep, send, hint):
        (both,) = self.made(hint, sum_kernel, "sum_both", [keep.shape], keep, partner(send, 1))
        self.both = partner(both, "near")

    def turn(self, hint):
        (far,) = self.made(
            hint, turn_kernel, "sum_turn", [self.keep.shape[1:]], self.keep, self.came, self.both
        )
        self.far = partner(far, "far")

    def own(self, hint):
        rows, width = self.keep.shape[1:]
        half = (rows // 2, width)
        away, self.kept = self.made(
            hint, own_kernel, "sum_own", [half] * 2, self.keep, self.came, self.near, self.far,
            scratch=[VMEM((2,) + half, bf16)],
        )
        self.back = partner(away, 2)

    def plus(self, came, hint):
        (self.kept,) = self.made(hint, sum_kernel, "sum_chips", [self.kept.shape], self.kept, came)

    def along(self, hint):
        self.plus(self.back, hint)
        step = 4
        while step < self.groups:
            self.back = partner(self.kept, step)
            step *= 2
            if step < self.groups:
                self.plus(self.back, hint)

    def across(self, hint):
        if self.groups > 4:
            self.plus(self.back, hint)
        self.back = partner(self.kept, 2)

    def share(self, hint):
        rows, width = self.kept.shape
        (own,) = self.made(hint, join_kernel, "sum_join", [(2 * rows, width)], self.kept, self.back)
        self.mine, self.far, self.near = own, partner(own, "far"), partner(own, "near")
        self.others = [partner(own, 1)]

    def pass_on(self, hint):
        self.far = self.line.gate(self.far, hint)
        self.both = partner(self.far, "near")
        self.others.append(partner(self.far, 1))

    def end(self, hint):
        shape = (2,) + self.far.shape
        (pair,) = self.made(hint, pair_kernel, "sum_pair", [shape], self.near, self.both)
        self.pieces = [self.mine, self.far, pair] + self.others + [partner(pair, 1)]


def shards(
    tokens,
    cotangent,
    lengths,
    gain_one,
    mixing_one,
    output_one,
    gain_two,
    up_two,
    down_two,
    gain_three,
    pair_three,
    fresh_three,
    output_three,
    gain_four,
    up_four,
    down_four,
):
    rows = tokens.shape[0]
    square = (D, D)
    row, wide_row, held = (rows, D), (rows, 3 * D), (2, QUARTERS, D, D)
    gain_row, packed, chances = (8, D), (QUARTERS, D, D), (HEADS, rows, rows)
    hidden_row = (QUARTERS,) + row
    shared_width = SHARED * HEAD
    line = Line()

    half_one, half_three, mine_one, mine_two, mine_four, limits = call(
        prepare_kernel, "prepare",
        (mixing_one.T, output_one.T, pair_three.T, fresh_three.T, output_three.T,
         gain_one, gain_two, gain_three, gain_four, up_two, down_two, up_four, down_four, lengths.T),
        [(square, bf16, "vmem")] * 5 + [((8, rows), jnp.int32, "vmem")],
        [VMEM((8, D), f32)] + [VMEM(gain_one.shape, bf16)] * 4 + [pltpu.SemaphoreType.DMA((18,))],
        {i: HBM for i in range(13)} | {13: SMEM},
    )
    near_one, far_one = partner(mine_one, "near"), partner(mine_one, "far")
    near_two, far_two = partner(mine_two, "near"), partner(mine_two, "far")
    near_one = line.gate(near_one, 20)
    other_near_one = partner(near_one, 1)
    both_one = partner(near_one, "far")
    near_two = line.gate(near_two, 20)
    other_near_two = partner(near_two, 1)
    both_two = partner(near_two, "far")
    far_one = line.gate(far_one, 20)
    other_far_one = partner(far_one, 1)
    limits = line.gate(limits, 20)
    both_two = line.gate(both_two, 20)
    other_both_two = partner(both_two, 1)
    far_two = line.gate(far_two, 20)
    other_far_two = partner(far_two, 1)
    mine_four = line.gate(mine_four, 20)
    near_four, far_four = partner(mine_four, "near"), partner(mine_four, "far")
    both_one = line.gate(both_one, 20)
    other_both_one = partner(both_one, 1)
    h1, mixed_one, attended_one, chances_one, mixing, output, mixing_three, out_three, gains = line.step(
        lambda *args: call(
            first_kernel, "first_forward", args,
            [(row, bf16, "vmem"), (wide_row, bf16, "vmem"), (row, bf16, "vmem"), (chances, f32, "vmem"),
             ((3 * D, D), bf16, "vmem"), (square, bf16, "vmem"), ((3 * D, D), bf16, "vmem"),
             (square, bf16, "vmem"), (gain_row, f32, "vmem")],
            [VMEM(held, bf16)], hint=20,
        ),
        limits, tokens, half_one, half_three,
        near_one, far_one, both_one, other_near_one, other_far_one, other_both_one,
    )
    h2, held_two, h3, mixed_three, attended_three, chances_three, actives, slopes = line.step(
        lambda *args: call(
            middle_kernel, "second_third_forward", args,
            [(row, bf16, "vmem"), (held, bf16, "vmem"), (row, bf16, "vmem"), (wide_row, bf16, "vmem"),
             (row, bf16, "vmem"), (chances, f32, "vmem"), (hidden_row, bf16, "vmem"),
             (hidden_row, f32, "vmem")],
            [pltpu.SemaphoreType.DMA((2,))], {6: HBM, 7: HBM}, hint=20,
        ),
        limits, h1, gains, mixing_three, out_three, mixed_one, up_two, down_two,
        near_two, far_two, both_two, other_near_two, other_far_two, other_both_two,
    )
    far_four = line.gate(far_four, 20)
    other_far_four = partner(far_four, 1)
    near_four = line.gate(near_four, 0)
    other_near_four = partner(near_four, 1)
    both_four = partner(near_four, "far")
    three_quarters = (QUARTERS - 1, D, D)
    after, grad_normed, keep, send = line.step(
        lambda *args: call(
            fourth_kernel, "fourth_both", args,
            [(row, f32, "vmem"), (row, f32, "vmem"), (three_quarters, bf16, "vmem"),
             (three_quarters, bf16, "vmem")],
            [VMEM((2, 1, D, D), bf16), pltpu.SemaphoreType.DMA((2,))], {4: HBM, 5: HBM}, hint=20,
        ),
        limits, h3, gains, cotangent, up_four, down_four,
        near_four, far_four, other_near_four, other_far_four,
    )
    four = Chunk(line, keep, send)
    both_four = line.gate(both_four, 20)
    other_both_four = partner(both_four, 1)
    out, grad_h3, last_keep, last_send, gain_grad_four = line.step(
        lambda *args: call(
            fourth_end_kernel, "fourth_end", args,
            [(row, f32, "plain"), (row, bf16, "vmem"), (square, bf16, "vmem"), (square, bf16, "vmem"),
             (gain_row, f32, "vmem")], hint=20,
        ),
        limits, h3, gains, cotangent, after, grad_normed, both_four, other_both_four,
    )
    four.begin_near(20)
    four.begin_both(last_keep, last_send, 20)
    grad_h2, third_weights, grad_shared, gain_grad_three = line.step(
        lambda *args: call(
            third_back_kernel, "third_backward", args,
            [(row, bf16, "vmem"), ((2, 2 * D, D), bf16, "vmem"), ((rows, shared_width), bf16, "vmem"),
             (gain_row, f32, "vmem")],
            [VMEM(wide_row, bf16)], hint=3,
        ),
        h2, gains, grad_h3, mixed_three, attended_three, chances_three, mixing_three, out_three,
    )
    grad_h1, keep, send, gain_grad_two = line.step(
        lambda *args: call(
            second_back_kernel, "second_backward", args,
            [(row, bf16, "vmem"), (packed, bf16, "vmem"), (packed, bf16, "vmem"), (gain_row, f32, "vmem")], hint=20,
        ),
        h1, gains, grad_h2, held_two, actives, slopes,
    )
    two = Chunk(line, keep, send)
    four.turn(20)
    input_grad, keep, send = line.step(
        lambda *args: call(
            first_back_kernel, "first_backward", args,
            [(row, f32, "plain"), (packed, bf16, "vmem"), (packed, bf16, "vmem")],
            [VMEM(wide_row, bf16)], hint=20,
        ),
        tokens, gains, grad_h1, mixed_one, attended_one, chances_one, mixing, output,
        grad_shared, third_weights, gain_grad_two, gain_grad_three, gain_grad_four,
    )
    first = Chunk(line, keep, send)
    two.begin(20)
    four.own(3)
    two.turn(20)
    four.along(20)
    first.begin(20)
    two.own(20)
    four.across(20)
    first.turn(20)
    two.along(20)
    four.share(20)
    first.own(20)
    two.across(20)
    four.pass_on(20)
    first.along(20)
    two.share(20)
    four.end(20)
    first.across(20)
    two.pass_on(20)
    first.share(20)
    two.end(3)
    first.pass_on(2)
    feed_outs = [((D, 4 * D), f32, "hbm"), ((4 * D, D), f32, "hbm")]
    feed_scratch = [VMEM((8, D, D), f32), pltpu.SemaphoreType.DMA((8,))]
    grad_up_two, grad_down_two = line.step(
        lambda *args: call(unpack_feed_kernel, "unpack_two", args, feed_outs, feed_scratch, hint=1),
        *two.pieces,
    )
    first.end(20)
    grad_up_four, grad_down_four = line.step(
        lambda *args: call(unpack_feed_kernel, "unpack_four", args, feed_outs, feed_scratch, hint=20),
        *four.pieces,
    )
    mixing_g, output_g, pair_g, fresh_g, output_three_g, g1, g2, g3, g4 = line.step(
        lambda *args: call(
            unpack_attention_kernel, "unpack_attention", args,
            [((D, 3 * D), f32, "hbm"), (square, f32, "hbm"), ((D, 2 * D), f32, "hbm"),
             ((D // 2, D), f32, "hbm"), (square, f32, "hbm")] + [((D,), f32, "plain")] * 4,
            [VMEM((8, D, D), f32), pltpu.SemaphoreType.DMA((8, 2))], hint=20,
        ),
        *first.pieces,
    )
    return (
        out, input_grad, g1, mixing_g, output_g, g2, grad_up_two, grad_down_two,
        g3, pair_g, fresh_g.T, output_three_g, g4, grad_up_four, grad_down_four,
    )


def solution(mesh):
    return jax.shard_map(
        shards,
        mesh=mesh,
        in_specs=(
            P(("section", "dp"), None),
            P(("section", "dp"), None),
            P(None, "dp"),
            P("section"),
            P(None, "section"),
            P(None, "section"),
            P("section"),
            P(None, "section"),
            P("section", None),
            P("section"),
            P(None, "section"),
            P(None, "section"),
            P(None, "section"),
            P("section"),
            P(None, "section"),
            P("section", None),
        ),
        out_specs=(P(("section", "dp"), None), P(("section", "dp"), None)) + (P(),) * 13,
        check_vma=False,
    )
```

time: 198 us -> 139 us (0.70)
  waiting for transfers between devices: 71 us -> 49.1 us
  other arithmetic: 15.1 us -> 0 us
  local copies, waits for them, and re-layouts: 15.3 us -> 1.25 us
  Pallas kernels: 43.4 us -> 35.5 us
    ppermute x60 -> x58, waiting for transfers between devices: 71 us -> 49.1 us  [partner(): lax.ppermute(value, ('section', 'dp'), partner_pairs(sections, groups, ki...]
    unnamed x46 -> x16, local copies, waits for them, and re-layouts: 14.6 us -> 1.25 us
    convert_element_type x15 -> x0, other arithmetic: 10.7 us -> none  [the longest x9 3.98 us: add(): return (left.astype(f32) + right.astype(f32)).astype(bf16)]
    pallas_call x9 -> x47, Pallas kernels: 43.4 us -> 35.5 us  [call(): pl.pallas_call(body, name=name, out_shape=[places[where](shape, dtype) if...]
    pallas_call x4 -> x0, other arithmetic: 2.38 us -> none  [call(): pl.pallas_call(body, name=name, out_shape=[jax.ShapeDtypeStruct(shape, dt...]
    ppermute x60 -> x58, starting transfers between devices: 50.6 us -> 51.7 us  [partner(): lax.ppermute(value, ('section', 'dp'), partner_pairs(sections, groups, ki...]
  transfers between devices with their start and end apart: 60 -> 58, of which waited for: 29 -> 22; matrix products, arithmetic and copies ran while one was open for 8% -> 0% of each run, Pallas kernels for 8% -> 22%
where the time goes in v3:
time: 139 us
  starting transfers between devices  51.7 us (37%)
  waiting for transfers between devices  49.1 us (35%)
  Pallas kernels  35.5 us (26%)
    ppermute x58, starting transfers between devices, partner(): lax.ppermute(value, ('section', 'dp'), partner_pairs(sections, groups, ki...  51.7 us
    ppermute x58, waiting for transfers between devices, partner(): lax.ppermute(value, ('section', 'dp'), partner_pairs(sections, groups, ki...  49.1 us
    pallas_call x47, Pallas kernels, call(): pl.pallas_call(body, name=name, out_shape=[places[where](shape, dtype) if...  35.5 us
  transfers between devices with their start and end apart: 58, of which 22 were waited for; matrix products, arithmetic and copies ran while one was open for 0% of the time, Pallas kernels for 22%

profile of v3, /device:TPU:0, one launch (start us, length us, event | category | flops | bytes accessed | tf_op | source)
XLA Modules:
  0.0 138.9 jit_solution(5140840354470949003)
XLA Ops:
  1.3 2.1 %prepare.1 = (bf16[384,384]{1,0:T(8,128)(2,1)S(1)}, bf16[384,384]{1,0:T(8,128)(2,1)S(1)}, bf16[384,384]{1,0:T(8,128)(2,1)S(1)}, bf16[384,384]{1,0:T(8,128)(2,1)S...) custom-call(bf16[288,384]{1,0:T(8,128)(2,1)} %bitcast.8, bf16[96,384]{1,0:T(8,128)(2,1)} %bitcast.10, ...), custom_call_target="tpu_custom_call" | custom-call | flops 20000000000 | bytes 1 | tf_op jit(solution)/shard_map/prepare/pallas_call | solution.py:492
  3.4 3.0 %collective-permute-start.2 = (bf16[384,384]{1,0:T(8,128)(2,1)S(1)}, bf16[384,384]{1,0:T(8,128)(2,1)S(1)}, u32[]{:S(2)}, u32[]{:S(2)}) collective-permute-start(bf16[384,384]{1,0:T(8,128)(2,1)S(1)} %get-tuple-element.235), channel_id=1, source_target_pairs={{0,8},{1,17},{2,10},{3,19},{4,12},{5,21},{6,14},{7,23},{8,0},{9,25... | collective-permute-start | bytes 884744 | tf_op jit(solution)/shard_map/ppermute | solution.py:525
  8.6 5.2 %collective-permute-done.2.value = bf16[384,384]{1,0:T(8,128)(2,1)S(1)} collective-permute-done((bf16[384,384]{1,0:T(8,128)(2,1)S(1)}, bf16[384,384]{1,0:T(8,128)(2,1)S(1)}, u32[]{:S(2)}, u32[]{:S(2)}) %collective-permute-start.2) | collective-permute-done | bytes 294944 | tf_op jit(solution)/shard_map/ppermute | solution.py:525
  13.9 2.7 %collective-permute-start.3 = (bf16[384,384]{1,0:T(8,128)(2,1)S(1)}, bf16[384,384]{1,0:T(8,128)(2,1)S(1)}, u32[]{:S(2)}, u32[]{:S(2)}) collective-permute-start(bf16[384,384]{1,0:T(8,128)(2,1)S(1)} %gate.14.rest_0_), channel_id=1, source_target_pairs={{0,16},{1,9},{2,18},{3,11},{4,20},{5,13},{6,22},{7,15},{8,24},{9,1... | collective-permute-start | bytes 884744 | tf_op jit(solution)/shard_map/ppermute | solution.py:525
  16.5 3.5 %collective-permute-done.1.value = bf16[384,384]{1,0:T(8,128)(2,1)S(1)} collective-permute-done((bf16[384,384]{1,0:T(8,128)(2,1)S(1)}, bf16[384,384]{1,0:T(8,128)(2,1)S(1)}, u32[]{:S(2)}, u32[]{:S(2)}) %collective-permute-start.1) | collective-permute-done | bytes 294944 | tf_op jit(solution)/shard_map/ppermute | solution.py:525
  20.1 2.7 %collective-permute-start.5 = (bf16[384,384]{1,0:T(8,128)(2,1)S(1)}, bf16[384,384]{1,0:T(8,128)(2,1)S(1)}, u32[]{:S(2)}, u32[]{:S(2)}) collective-permute-start(bf16[384,384]{1,0:T(8,128)(2,1)S(1)} %gate.15.rest_0_), channel_id=1, source_target_pairs={{0,16},{1,9},{2,18},{3,11},{4,20},{5,13},{6,22},{7,15},{8,24},{9,1... | collective-permute-start | bytes 884744 | tf_op jit(solution)/shard_map/ppermute | solution.py:525
  22.9 4.6 %collective-permute-done.5.value = bf16[384,384]{1,0:T(8,128)(2,1)S(1)} collective-permute-done((bf16[384,384]{1,0:T(8,128)(2,1)S(1)}, bf16[384,384]{1,0:T(8,128)(2,1)S(1)}, u32[]{:S(2)}, u32[]{:S(2)}) %collective-permute-start.5) | collective-permute-done | bytes 294944 | tf_op jit(solution)/shard_map/ppermute | solution.py:525
  28.2 2.0 %collective-permute-start.13 = (bf16[384,384]{1,0:T(8,128)(2,1)S(1)}, bf16[384,384]{1,0:T(8,128)(2,1)S(1)}, u32[]{:S(2)}, u32[]{:S(2)}) collective-permute-start(bf16[384,384]{1,0:T(8,128)(2,1)S(1)} %gate.20), channel_id=1, source_target_pairs={{0,16},{1,9},{2,18},{3,11},{4,20},{5,13},{6,22},{7,15},{8,24},{9,1... | collective-permute-start | bytes 884744 | tf_op jit(solution)/shard_map/ppermute | solution.py:525
  32.3 3.5 %first_forward.1 = (bf16[256,384]{1,0:T(8,128)(2,1)S(1)}, bf16[256,1152]{1,0:T(8,128)(2,1)S(1)}, bf16[256,384]{1,0:T(8,128)(2,1)S(1)}, f32[6,256,256]{2,1,0:T(8,...) custom-call(s32[8,256]{1,0:T(8,128)S(1)} %gate.17.limits, ...), custom_call_target="tpu_custom_call" | custom-call | flops 20000000000 | bytes 1 | tf_op jit(solution)/shard_map/first_forward/pallas_call | solution.py:492
  35.8 5.2 %second_third_forward.1 = (bf16[256,384]{1,0:T(8,128)(2,1)S(1)}, bf16[2,4,384,384]{3,2,1,0:T(8,128)(2,1)S(1)}, bf16[256,384]{1,0:T(8,128)(2,1)S(1)}, bf16[256,11...) custom-call(s32[8,256]{1,0:T(8,128)S(1)} %gate.17.limits, ...), custom_call_target="tpu_custom_call" | custom-call | flops 20000000000 | bytes 1 | tf_op jit(solution)/shard_map/second_third_forward/pallas_call | solution.py:492
  43.2 3.1 %fourth_both.1 = (f32[256,384]{1,0:T(8,128)S(1)}, f32[256,384]{1,0:T(8,128)S(1)}, bf16[3,384,384]{2,1,0:T(8,128)(2,1)S(1)}, bf16[3,384,384]{2,1,0:T(8,128)(2,1)S(1)}) custom-call(s32[8,256]{1,0:T(8,128)S(1)} %gate.17.limits, bf16[256,384]{1,0:T(8,128)(2,1)S(1)} %get-tuple-element.294.h3, f32[8,384]{1,0:T(8,128)S(1)} %get-tuple-element.346.gains, ...), custom_call_target="tpu_custom_call" | custom-call | flops 20000000000 | bytes 1 | tf_op jit(solution)/shard_map/fourth_both/pallas_call | solution.py:492
  46.3 2.1 %collective-permute-done.16.value = bf16[384,384]{1,0:T(8,128)(2,1)S(1)} collective-permute-done((bf16[384,384]{1,0:T(8,128)(2,1)S(1)}, bf16[384,384]{1,0:T(8,128)(2,1)S(1)}, u32[]{:S(2)}, u32[]{:S(2)}) %collective-permute-start.16) | collective-permute-done | bytes 294944 | tf_op jit(solution)/shard_map/ppermute | solution.py:525
  50.1 2.0 %fourth_end.1 = (f32[256,384]{1,0:T(8,128)}, bf16[256,384]{1,0:T(8,128)(2,1)S(1)}, bf16[384,384]{1,0:T(8,128)(2,1)S(1)}, bf16[384,384]{1,0:T(8,128)(2,1)S(1)}, f32[8,384]{1,0:T(8,128)S(1)}) custom-call(s32[8,256]{1,0:T(8,128)S(1)} %gate.17.limits, bf16[256,384]{1,0:T(8,128)(2,1)S(1)} %get-tuple-element.294.h3, f32[8,384]{1,0:T(8,128)S(1)} %get-tuple-element.346.gains, ...), custom_call_target="tpu_custom_call" | custom-call | flops 20000000000 | bytes 1 | tf_op jit(solution)/shard_map/fourth_end/pallas_call | solution.py:492
  54.6 3.0 %third_backward.1 = (bf16[256,384]{1,0:T(8,128)(2,1)S(1)}, bf16[2,768,384]{2,1,0:T(8,128)(2,1)S(1)}, bf16[256,192]{1,0:T(8,128)(2,1)S(1)}, f32[8,384]{1,0:T(8,128)S(1)}) custom-call(bf16[256,384]{1,0:T(8,128)(2,1)S(1)} %get-tuple-element.314.h2, f32[8,384]{1,0:T(8,128)S(1)} %get-tuple-element.346.gains, bf16[256,384]{1,0:T(8,128)(2,1)S(1)} %get-tuple-element.316.grad_h3, ...), custom_call_target="tpu_custom_call" | custom-call | flops 3000000000 | bytes 1 | tf_op jit(solution)/shard_map/third_backward/pallas_call | solution.py:492
  57.6 2.4 %second_backward.1 = (bf16[256,384]{1,0:T(8,128)(2,1)S(1)}, bf16[4,384,384]{2,1,0:T(8,128)(2,1)S(1)}, bf16[4,384,384]{2,1,0:T(8,128)(2,1)S(1)}, f32[8,384]{1,0:T(8,128)S(1)}) custom-call(bf16[256,384]{1,0:T(8,128)(2,1)S(1)} %get-tuple-element.326.h1, f32[8,384]{1,0:T(8,128)S(1)} %get-tuple-element.346.gains, ...), custom_call_target="tpu_custom_call" | custom-call | flops 20000000000 | bytes 1 | tf_op jit(solution)/shard_map/second_backward/pallas_call | solution.py:492
  60.0 2.2 %collective-permute-done.20.both = bf16[384,384]{1,0:T(8,128)(2,1)S(1)} collective-permute-done((bf16[384,384]{1,0:T(8,128)(2,1)S(1)}, bf16[384,384]{1,0:T(8,128)(2,1)S(1)}, u32[]{:S(2)}, u32[]{:S(2)}) %collective-permute-start.20) | collective-permute-done | bytes 294944 | tf_op jit(solution)/shard_map/ppermute | solution.py:525
  63.5 4.1 %first_backward.1 = (f32[256,384]{1,0:T(8,128)}, bf16[4,384,384]{2,1,0:T(8,128)(2,1)S(1)}, bf16[4,384,384]{2,1,0:T(8,128)(2,1)S(1)}) custom-call(bf16[256,384]{1,0:T(8,128)(2,1)S(1)} %copy-done.4, f32[8,384]{1,0:T(8,128)S(1)} %get-tuple-element.346.gains, bf16[256,384]{1,0:T(8,128)(2,1)S(1)} %get-tuple-element.347.grad_h1, bf16[256,1152]{1,0:T(8,128)(2,1)S(1)} %copy-done.7, ...), custom_call_target="tpu_custom_call" | custom-call | flops 20000000000 | bytes 1 | tf_op jit(solution)/shard_map/first_backward/pallas_call | solution.py:492
  71.7 2.8 %collective-permute-done.26.both = bf16[384,384]{1,0:T(8,128)(2,1)S(1)} collective-permute-done((bf16[384,384]{1,0:T(8,128)(2,1)S(1)}, bf16[384,384]{1,0:T(8,128)(2,1)S(1)}, u32[]{:S(2)}, u32[]{:S(2)}) %collective-permute-start.26) | collective-permute-done | bytes 294944 | tf_op jit(solution)/shard_map/ppermute | solution.py:525
  75.8 2.6 %collective-permute-start.29 = (bf16[192,384]{1,0:T(8,128)(2,1)S(1)}, bf16[192,384]{1,0:T(8,128)(2,1)S(1)}, u32[]{:S(2)}, u32[]{:S(2)}) collective-permute-start(bf16[192,384]{1,0:T(8,128)(2,1)S(1)} %sum_chips.6.left), channel_id=1, source_target_pairs={{0,4},{1,5},{2,6},{3,7},{4,0},{5,1},{6,2},{7,3},{8,12},{9,13},{10,... | collective-permute-start | bytes 442376 | tf_op jit(solution)/shard_map/ppermute | solution.py:525
  80.7 3.1 %collective-permute-done.31.far = bf16[384,384]{1,0:T(8,128)(2,1)S(1)} collective-permute-done((bf16[384,384]{1,0:T(8,128)(2,1)S(1)}, bf16[384,384]{1,0:T(8,128)(2,1)S(1)}, u32[]{:S(2)}, u32[]{:S(2)}) %collective-permute-start.31) | collective-permute-done | bytes 294944 | tf_op jit(solution)/shard_map/ppermute | solution.py:525
  86.2 2.3 %collective-permute-done.28.both = bf16[384,384]{1,0:T(8,128)(2,1)S(1)} collective-permute-done((bf16[384,384]{1,0:T(8,128)(2,1)S(1)}, bf16[384,384]{1,0:T(8,128)(2,1)S(1)}, u32[]{:S(2)}, u32[]{:S(2)}) %collective-permute-start.28) | collective-permute-done | bytes 294944 | tf_op jit(solution)/shard_map/ppermute | solution.py:525
  89.7 3.1 %collective-permute-start.37 = (bf16[192,384]{1,0:T(8,128)(2,1)S(1)}, bf16[192,384]{1,0:T(8,128)(2,1)S(1)}, u32[]{:S(2)}, u32[]{:S(2)}) collective-permute-start(bf16[192,384]{1,0:T(8,128)(2,1)S(1)} %sum_chips.8.left), channel_id=1, source_target_pairs={{0,4},{1,5},{2,6},{3,7},{4,0},{5,1},{6,2},{7,3},{8,12},{9,13},{10,... | collective-permute-start | bytes 442376 | tf_op jit(solution)/shard_map/ppermute | solution.py:525
  95.5 2.2 %collective-permute-done.32.far = bf16[384,384]{1,0:T(8,128)(2,1)S(1)} collective-permute-done((bf16[384,384]{1,0:T(8,128)(2,1)S(1)}, bf16[384,384]{1,0:T(8,128)(2,1)S(1)}, u32[]{:S(2)}, u32[]{:S(2)}) %collective-permute-start.32) | collective-permute-done | bytes 294944 | tf_op jit(solution)/shard_map/ppermute | solution.py:525
  100.2 2.8 %collective-permute-done.36.value = bf16[384,384]{1,0:T(8,128)(2,1)S(1)} collective-permute-done((bf16[384,384]{1,0:T(8,128)(2,1)S(1)}, bf16[384,384]{1,0:T(8,128)(2,1)S(1)}, u32[]{:S(2)}, u32[]{:S(2)}) %collective-permute-start.36) | collective-permute-done | bytes 294944 | tf_op jit(solution)/shard_map/ppermute | solution.py:525
  103.6 3.0 %collective-permute-start.38 = (bf16[192,384]{1,0:T(8,128)(2,1)S(1)}, bf16[192,384]{1,0:T(8,128)(2,1)S(1)}, u32[]{:S(2)}, u32[]{:S(2)}) collective-permute-start(bf16[192,384]{1,0:T(8,128)(2,1)S(1)} %sum_chips.10.left), channel_id=1, source_target_pairs={{0,4},{1,5},{2,6},{3,7},{4,0},{5,1},{6,2},{7,3},{8,12},{9,13},{10,... | collective-permute-start | bytes 442376 | tf_op jit(solution)/shard_map/ppermute | solution.py:525
  108.2 3.1 %collective-permute-done.40.right = bf16[384,384]{1,0:T(8,128)(2,1)S(1)} collective-permute-done((bf16[384,384]{1,0:T(8,128)(2,1)S(1)}, bf16[384,384]{1,0:T(8,128)(2,1)S(1)}, u32[]{:S(2)}, u32[]{:S(2)}) %collective-permute-start.40) | collective-permute-done | bytes 294944 | tf_op jit(solution)/shard_map/ppermute | solution.py:525
  111.6 2.1 %collective-permute-start.42 = (bf16[192,384]{1,0:T(8,128)(2,1)S(1)}, bf16[192,384]{1,0:T(8,128)(2,1)S(1)}, u32[]{:S(2)}, u32[]{:S(2)}) collective-permute-start(bf16[192,384]{1,0:T(8,128)(2,1)S(1)} %sum_chips.11.kept), channel_id=1, source_target_pairs={{0,2},{1,3},{2,0},{3,1},{4,6},{5,7},{6,4},{7,5},{8,10},{9,11},{10,... | collective-permute-start | bytes 442376 | tf_op jit(solution)/shard_map/ppermute | solution.py:525
  118.1 4.2 %collective-permute-done.46.right = bf16[384,384]{1,0:T(8,128)(2,1)S(1)} collective-permute-done((bf16[384,384]{1,0:T(8,128)(2,1)S(1)}, bf16[384,384]{1,0:T(8,128)(2,1)S(1)}, u32[]{:S(2)}, u32[]{:S(2)}) %collective-permute-start.46) | collective-permute-done | bytes 294944 | tf_op jit(solution)/shard_map/ppermute | solution.py:525
  125.8 2.3 %unpack_two.1 = (f32[384,1536]{1,0:T(8,128)}, f32[1536,384]{1,0:T(8,128)}) custom-call(bf16[384,384]{1,0:T(8,128)(2,1)S(1)} %sum_join.4.rest_0_, bf16[384,384]{1,0:T(8,128)(2,1)S(1)} %gate.26.rest_1_, bf16[2,384,384]{2,1,0:T(8,128)(2,1)S(1)} %sum_pair.4.rest_2_, bf16[384,384]{1,0:T(8,128)(2,1)S(1)} %collective-permute-done.49.rest_3_, ...), custom_call_target="tpu_custom_call" | custom-call | flops 1000000000 | bytes 1 | tf_op jit(solution)/shard_map/unpack_two/pallas_call | solution.py:492
  129.7 3.2 %collective-permute-done.48.right = bf16[384,384]{1,0:T(8,128)(2,1)S(1)} collective-permute-done((bf16[384,384]{1,0:T(8,128)(2,1)S(1)}, bf16[384,384]{1,0:T(8,128)(2,1)S(1)}, u32[]{:S(2)}, u32[]{:S(2)}) %collective-permute-start.48) | collective-permute-done | bytes 294944 | tf_op jit(solution)/shard_map/ppermute | solution.py:525
  133.5 2.3 %unpack_four.1 = (f32[384,1536]{1,0:T(8,128)}, f32[1536,384]{1,0:T(8,128)}) custom-call(bf16[384,384]{1,0:T(8,128)(2,1)S(1)} %copy-done.1, bf16[384,384]{1,0:T(8,128)(2,1)S(1)} %gate.25.rest_1_, bf16[2,384,384]{2,1,0:T(8,128)(2,1)S(1)} %sum_pair.3.rest_2_, bf16[384,384]{1,0:T(8,128)(2,1)S(1)} %collective-permute-done.55.rest_3_, ...), custom_call_target="tpu_custom_call" | custom-call | flops 20000000000 | bytes 1 | tf_op jit(solution)/shard_map/unpack_four/pallas_call | solution.py:492
  135.9 2.8 %unpack_attention.1 = (f32[384,1152]{1,0:T(8,128)}, f32[384,384]{1,0:T(8,128)}, f32[384,768]{1,0:T(8,128)}, f32[192,384]{1,0:T(8,128)}, f32[384,384]{1,0:T(8,128...) custom-call(bf16[384,384]{1,0:T(8,128)(2,1)S(1)} %sum_join.5.rest_0_, ...), custom_call_target="tpu_custom_call" | custom-call | flops 20000000000 | bytes 1 | tf_op jit(solution)/shard_map/unpack_attention/pallas_call | solution.py:492
  (147 shorter events, 42.1 us)
Async XLA Ops:
  3.4 10.3 %collective-permute-start.2 = (bf16[384,384]{1,0:T(8,128)(2,1)S(1)}, bf16[384,384]{1,0:T(8,128)(2,1)S(1)}, u32[]{:S(2)}, u32[]{:S(2)}) collective-permute-start(bf16[384,384]{1,0:T(8,128)(2,1)S(1)} %get-tuple-element.235), channel_id=1, source_target_pairs={{0,8},{1,17},{2,10},{3,19},{4,12},{5,21},{6,14},{7,23},{8,0},{9,25... | collective-permute-start | bytes 884744 | tf_op jit(solution)/shard_map/ppermute | solution.py:525
  6.4 16.3 %collective-permute-start = (bf16[384,384]{1,0:T(8,128)(2,1)S(1)}, bf16[384,384]{1,0:T(8,128)(2,1)S(1)}, u32[]{:S(2)}, u32[]{:S(2)}) collective-permute-start(bf16[384,384]{1,0:T(8,128)(2,1)S(1)} %get-tuple-element.235), channel_id=1, source_target_pairs={{0,16},{1,9},{2,18},{3,11},{4,20},{5,13},{6,22},{7,15},{8,24},{9,1... | collective-permute-start | bytes 884744 | tf_op jit(solution)/shard_map/ppermute | solution.py:525
  8.0 19.5 %collective-permute-start.4 = (bf16[384,384]{1,0:T(8,128)(2,1)S(1)}, bf16[384,384]{1,0:T(8,128)(2,1)S(1)}, u32[]{:S(2)}, u32[]{:S(2)}) collective-permute-start(bf16[384,384]{1,0:T(8,128)(2,1)S(1)} %get-tuple-element.236), channel_id=1, source_target_pairs={{0,16},{1,9},{2,18},{3,11},{4,20},{5,13},{6,22},{7,15},{8,24},{9,1... | collective-permute-start | bytes 884744 | tf_op jit(solution)/shard_map/ppermute | solution.py:525
  8.5 11.6 %collective-permute-start.1 = (bf16[384,384]{1,0:T(8,128)(2,1)S(1)}, bf16[384,384]{1,0:T(8,128)(2,1)S(1)}, u32[]{:S(2)}, u32[]{:S(2)}) collective-permute-start(bf16[384,384]{1,0:T(8,128)(2,1)S(1)} %get-tuple-element.236), channel_id=1, source_target_pairs={{0,8},{1,17},{2,10},{3,19},{4,12},{5,21},{6,14},{7,23},{8,0},{9,25... | collective-permute-start | bytes 884744 | tf_op jit(solution)/shard_map/ppermute | solution.py:525
  13.8 16.5 %collective-permute-start.6 = (bf16[384,384]{1,0:T(8,128)(2,1)S(1)}, bf16[384,384]{1,0:T(8,128)(2,1)S(1)}, u32[]{:S(2)}, u32[]{:S(2)}) collective-permute-start(bf16[384,384]{1,0:T(8,128)(2,1)S(1)} %gate.14.rest_0_), channel_id=1, source_target_pairs={{0,1},{1,0},{2,3},{3,2},{4,5},{5,4},{6,7},{7,6},{8,9},{9,8},{10,11... | collective-permute-start | bytes 884744 | tf_op jit(solution)/shard_map/ppermute | solution.py:525
  13.9 13.7 %collective-permute-start.3 = (bf16[384,384]{1,0:T(8,128)(2,1)S(1)}, bf16[384,384]{1,0:T(8,128)(2,1)S(1)}, u32[]{:S(2)}, u32[]{:S(2)}) collective-permute-start(bf16[384,384]{1,0:T(8,128)(2,1)S(1)} %gate.14.rest_0_), channel_id=1, source_target_pairs={{0,16},{1,9},{2,18},{3,11},{4,20},{5,13},{6,22},{7,15},{8,24},{9,1... | collective-permute-start | bytes 884744 | tf_op jit(solution)/shard_map/ppermute | solution.py:525
  20.1 7.4 %collective-permute-start.5 = (bf16[384,384]{1,0:T(8,128)(2,1)S(1)}, bf16[384,384]{1,0:T(8,128)(2,1)S(1)}, u32[]{:S(2)}, u32[]{:S(2)}) collective-permute-start(bf16[384,384]{1,0:T(8,128)(2,1)S(1)} %gate.15.rest_0_), channel_id=1, source_target_pairs={{0,16},{1,9},{2,18},{3,11},{4,20},{5,13},{6,22},{7,15},{8,24},{9,1... | collective-permute-start | bytes 884744 | tf_op jit(solution)/shard_map/ppermute | solution.py:525
  22.8 8.9 %collective-permute-start.7 = (bf16[384,384]{1,0:T(8,128)(2,1)S(1)}, bf16[384,384]{1,0:T(8,128)(2,1)S(1)}, u32[]{:S(2)}, u32[]{:S(2)}) collective-permute-start(bf16[384,384]{1,0:T(8,128)(2,1)S(1)} %gate.16.rest_1_), channel_id=1, source_target_pairs={{0,1},{1,0},{2,3},{3,2},{4,5},{5,4},{6,7},{7,6},{8,9},{9,8},{10,11... | collective-permute-start | bytes 884744 | tf_op jit(solution)/shard_map/ppermute | solution.py:525
  27.7 8.0 %collective-permute-start.9 = (bf16[384,384]{1,0:T(8,128)(2,1)S(1)}, bf16[384,384]{1,0:T(8,128)(2,1)S(1)}, u32[]{:S(2)}, u32[]{:S(2)}) collective-permute-start(bf16[384,384]{1,0:T(8,128)(2,1)S(1)} %gate.15.rest_0_), channel_id=1, source_target_pairs={{0,1},{1,0},{2,3},{3,2},{4,5},{5,4},{6,7},{7,6},{8,9},{9,8},{10,11... | collective-permute-start | bytes 884744 | tf_op jit(solution)/shard_map/ppermute | solution.py:525
  28.2 12.8 %collective-permute-start.13 = (bf16[384,384]{1,0:T(8,128)(2,1)S(1)}, bf16[384,384]{1,0:T(8,128)(2,1)S(1)}, u32[]{:S(2)}, u32[]{:S(2)}) collective-permute-start(bf16[384,384]{1,0:T(8,128)(2,1)S(1)} %gate.20), channel_id=1, source_target_pairs={{0,16},{1,9},{2,18},{3,11},{4,20},{5,13},{6,22},{7,15},{8,24},{9,1... | collective-permute-start | bytes 884744 | tf_op jit(solution)/shard_map/ppermute | solution.py:525
  30.2 10.8 %collective-permute-start.12 = (bf16[384,384]{1,0:T(8,128)(2,1)S(1)}, bf16[384,384]{1,0:T(8,128)(2,1)S(1)}, u32[]{:S(2)}, u32[]{:S(2)}) collective-permute-start(bf16[384,384]{1,0:T(8,128)(2,1)S(1)} %gate.20), channel_id=1, source_target_pairs={{0,8},{1,17},{2,10},{3,19},{4,12},{5,21},{6,14},{7,23},{8,0},{9,25... | collective-permute-start | bytes 884744 | tf_op jit(solution)/shard_map/ppermute | solution.py:525
  52.3 16.0 %collective-permute-start.22 = (bf16[384,384]{1,0:T(8,128)(2,1)S(1)}, bf16[384,384]{1,0:T(8,128)(2,1)S(1)}, u32[]{:S(2)}, u32[]{:S(2)}) collective-permute-start(bf16[384,384]{1,0:T(8,128)(2,1)S(1)} %sum_near.1), channel_id=1, source_target_pairs={{0,8},{1,17},{2,10},{3,19},{4,12},{5,21},{6,14},{7,23},{8,0},{9,25... | collective-permute-start | bytes 884744 | tf_op jit(solution)/shard_map/ppermute | solution.py:525
  53.8 8.5 %collective-permute-start.20 = (bf16[384,384]{1,0:T(8,128)(2,1)S(1)}, bf16[384,384]{1,0:T(8,128)(2,1)S(1)}, u32[]{:S(2)}, u32[]{:S(2)}) collective-permute-start(bf16[384,384]{1,0:T(8,128)(2,1)S(1)} %sum_both.1), channel_id=1, source_target_pairs={{0,8},{1,17},{2,10},{3,19},{4,12},{5,21},{6,14},{7,23},{8,0},{9,25... | collective-permute-start | bytes 884744 | tf_op jit(solution)/shard_map/ppermute | solution.py:525
  60.0 7.6 %collective-permute-start.24 = (bf16[4,384,384]{2,1,0:T(8,128)(2,1)S(1)}, bf16[4,384,384]{2,1,0:T(8,128)(2,1)S(1)}, u32[]{:S(2)}, u32[]{:S(2)}) collective-permute-start(bf16[4,384,384]{2,1,0:T(8,128)(2,1)S(1)} %get-tuple-element.362), channel_id=1, source_target_pairs={{0,1},{1,0},{2,3},{3,2},{4,5},{5,4},{6,7},{7,6},{8,9},{9,8},{10,11... | collective-permute-start | bytes 3538952 | tf_op jit(solution)/shard_map/ppermute | solution.py:525
  68.3 10.1 %collective-permute-start.21 = (bf16[4,384,384]{2,1,0:T(8,128)(2,1)S(1)}, bf16[4,384,384]{2,1,0:T(8,128)(2,1)S(1)}, u32[]{:S(2)}, u32[]{:S(2)}) collective-permute-start(bf16[4,384,384]{2,1,0:T(8,128)(2,1)S(1)} %get-tuple-element.360), channel_id=1, source_target_pairs={{0,1},{1,0},{2,3},{3,2},{4,5},{5,4},{6,7},{7,6},{8,9},{9,8},{10,11... | collective-permute-start | bytes 3538952 | tf_op jit(solution)/shard_map/ppermute | solution.py:525
  71.1 9.6 %collective-permute-start.30 = (bf16[384,384]{1,0:T(8,128)(2,1)S(1)}, bf16[384,384]{1,0:T(8,128)(2,1)S(1)}, u32[]{:S(2)}, u32[]{:S(2)}) collective-permute-start(bf16[384,384]{1,0:T(8,128)(2,1)S(1)} %get-tuple-element.381), channel_id=1, source_target_pairs={{0,8},{1,17},{2,10},{3,19},{4,12},{5,21},{6,14},{7,23},{8,0},{9,25... | collective-permute-start | bytes 884744 | tf_op jit(solution)/shard_map/ppermute | solution.py:525
  74.6 9.2 %collective-permute-start.31 = (bf16[384,384]{1,0:T(8,128)(2,1)S(1)}, bf16[384,384]{1,0:T(8,128)(2,1)S(1)}, u32[]{:S(2)}, u32[]{:S(2)}) collective-permute-start(bf16[384,384]{1,0:T(8,128)(2,1)S(1)} %sum_turn.4), channel_id=1, source_target_pairs={{0,16},{1,9},{2,18},{3,11},{4,20},{5,13},{6,22},{7,15},{8,24},{9,1... | collective-permute-start | bytes 884744 | tf_op jit(solution)/shard_map/ppermute | solution.py:525
  75.8 9.9 %collective-permute-start.29 = (bf16[192,384]{1,0:T(8,128)(2,1)S(1)}, bf16[192,384]{1,0:T(8,128)(2,1)S(1)}, u32[]{:S(2)}, u32[]{:S(2)}) collective-permute-start(bf16[192,384]{1,0:T(8,128)(2,1)S(1)} %sum_chips.6.left), channel_id=1, source_target_pairs={{0,4},{1,5},{2,6},{3,7},{4,0},{5,1},{6,2},{7,3},{8,12},{9,13},{10,... | collective-permute-start | bytes 442376 | tf_op jit(solution)/shard_map/ppermute | solution.py:525
  78.6 17.0 %collective-permute-start.27 = (bf16[384,384]{1,0:T(8,128)(2,1)S(1)}, bf16[384,384]{1,0:T(8,128)(2,1)S(1)}, u32[]{:S(2)}, u32[]{:S(2)}) collective-permute-start(bf16[384,384]{1,0:T(8,128)(2,1)S(1)} %get-tuple-element.379), channel_id=1, source_target_pairs={{0,8},{1,17},{2,10},{3,19},{4,12},{5,21},{6,14},{7,23},{8,0},{9,25... | collective-permute-start | bytes 884744 | tf_op jit(solution)/shard_map/ppermute | solution.py:525
  79.3 9.2 %collective-permute-start.28 = (bf16[384,384]{1,0:T(8,128)(2,1)S(1)}, bf16[384,384]{1,0:T(8,128)(2,1)S(1)}, u32[]{:S(2)}, u32[]{:S(2)}) collective-permute-start(bf16[384,384]{1,0:T(8,128)(2,1)S(1)} %get-tuple-element.380), channel_id=1, source_target_pairs={{0,8},{1,17},{2,10},{3,19},{4,12},{5,21},{6,14},{7,23},{8,0},{9,25... | collective-permute-start | bytes 884744 | tf_op jit(solution)/shard_map/ppermute | solution.py:525
  88.6 9.1 %collective-permute-start.32 = (bf16[384,384]{1,0:T(8,128)(2,1)S(1)}, bf16[384,384]{1,0:T(8,128)(2,1)S(1)}, u32[]{:S(2)}, u32[]{:S(2)}) collective-permute-start(bf16[384,384]{1,0:T(8,128)(2,1)S(1)} %sum_turn.5), channel_id=1, source_target_pairs={{0,16},{1,9},{2,18},{3,11},{4,20},{5,13},{6,22},{7,15},{8,24},{9,1... | collective-permute-start | bytes 884744 | tf_op jit(solution)/shard_map/ppermute | solution.py:525
  89.7 10.0 %collective-permute-start.37 = (bf16[192,384]{1,0:T(8,128)(2,1)S(1)}, bf16[192,384]{1,0:T(8,128)(2,1)S(1)}, u32[]{:S(2)}, u32[]{:S(2)}) collective-permute-start(bf16[192,384]{1,0:T(8,128)(2,1)S(1)} %sum_chips.8.left), channel_id=1, source_target_pairs={{0,4},{1,5},{2,6},{3,7},{4,0},{5,1},{6,2},{7,3},{8,12},{9,13},{10,... | collective-permute-start | bytes 442376 | tf_op jit(solution)/shard_map/ppermute | solution.py:525
  92.8 15.3 %collective-permute-start.39 = (bf16[384,384]{1,0:T(8,128)(2,1)S(1)}, bf16[384,384]{1,0:T(8,128)(2,1)S(1)}, u32[]{:S(2)}, u32[]{:S(2)}) collective-permute-start(bf16[384,384]{1,0:T(8,128)(2,1)S(1)} %sum_join.3.rest_0_), channel_id=1, source_target_pairs={{0,8},{1,17},{2,10},{3,19},{4,12},{5,21},{6,14},{7,23},{8,0},{9,25... | collective-permute-start | bytes 884744 | tf_op jit(solution)/shard_map/ppermute | solution.py:525
  94.5 8.6 %collective-permute-start.36 = (bf16[384,384]{1,0:T(8,128)(2,1)S(1)}, bf16[384,384]{1,0:T(8,128)(2,1)S(1)}, u32[]{:S(2)}, u32[]{:S(2)}) collective-permute-start(bf16[384,384]{1,0:T(8,128)(2,1)S(1)} %sum_join.3.rest_0_), channel_id=1, source_target_pairs={{0,16},{1,9},{2,18},{3,11},{4,20},{5,13},{6,22},{7,15},{8,24},{9,1... | collective-permute-start | bytes 884744 | tf_op jit(solution)/shard_map/ppermute | solution.py:525
  103.1 8.2 %collective-permute-start.40 = (bf16[384,384]{1,0:T(8,128)(2,1)S(1)}, bf16[384,384]{1,0:T(8,128)(2,1)S(1)}, u32[]{:S(2)}, u32[]{:S(2)}) collective-permute-start(bf16[384,384]{1,0:T(8,128)(2,1)S(1)} %gate.25.rest_1_), channel_id=1, source_target_pairs={{0,8},{1,17},{2,10},{3,19},{4,12},{5,21},{6,14},{7,23},{8,0},{9,25... | collective-permute-start | bytes 884744 | tf_op jit(solution)/shard_map/ppermute | solution.py:525
  103.6 7.7 %collective-permute-start.38 = (bf16[192,384]{1,0:T(8,128)(2,1)S(1)}, bf16[192,384]{1,0:T(8,128)(2,1)S(1)}, u32[]{:S(2)}, u32[]{:S(2)}) collective-permute-start(bf16[192,384]{1,0:T(8,128)(2,1)S(1)} %sum_chips.10.left), channel_id=1, source_target_pairs={{0,4},{1,5},{2,6},{3,7},{4,0},{5,1},{6,2},{7,3},{8,12},{9,13},{10,... | collective-permute-start | bytes 442376 | tf_op jit(solution)/shard_map/ppermute | solution.py:525
  106.7 11.3 %collective-permute-start.45 = (bf16[384,384]{1,0:T(8,128)(2,1)S(1)}, bf16[384,384]{1,0:T(8,128)(2,1)S(1)}, u32[]{:S(2)}, u32[]{:S(2)}) collective-permute-start(bf16[384,384]{1,0:T(8,128)(2,1)S(1)} %sum_join.4.rest_0_), channel_id=1, source_target_pairs={{0,8},{1,17},{2,10},{3,19},{4,12},{5,21},{6,14},{7,23},{8,0},{9,25... | collective-permute-start | bytes 884744 | tf_op jit(solution)/shard_map/ppermute | solution.py:525
  107.2 8.3 %collective-permute-start.43 = (bf16[384,384]{1,0:T(8,128)(2,1)S(1)}, bf16[384,384]{1,0:T(8,128)(2,1)S(1)}, u32[]{:S(2)}, u32[]{:S(2)}) collective-permute-start(bf16[384,384]{1,0:T(8,128)(2,1)S(1)} %sum_join.4.rest_0_), channel_id=1, source_target_pairs={{0,16},{1,9},{2,18},{3,11},{4,20},{5,13},{6,22},{7,15},{8,24},{9,1... | collective-permute-start | bytes 884744 | tf_op jit(solution)/shard_map/ppermute | solution.py:525
  124.2 8.7 %collective-permute-start.48 = (bf16[384,384]{1,0:T(8,128)(2,1)S(1)}, bf16[384,384]{1,0:T(8,128)(2,1)S(1)}, u32[]{:S(2)}, u32[]{:S(2)}) collective-permute-start(bf16[384,384]{1,0:T(8,128)(2,1)S(1)} %gate.27.rest_1_), channel_id=1, source_target_pairs={{0,8},{1,17},{2,10},{3,19},{4,12},{5,21},{6,14},{7,23},{8,0},{9,25... | collective-permute-start | bytes 884744 | tf_op jit(solution)/shard_map/ppermute | solution.py:525
  125.2 7.7 %collective-permute-start.55 = (bf16[384,384]{1,0:T(8,128)(2,1)S(1)}, bf16[384,384]{1,0:T(8,128)(2,1)S(1)}, u32[]{:S(2)}, u32[]{:S(2)}) collective-permute-start(bf16[384,384]{1,0:T(8,128)(2,1)S(1)} %copy-done.1), channel_id=1, source_target_pairs={{0,1},{1,0},{2,3},{3,2},{4,5},{5,4},{6,7},{7,6},{8,9},{9,8},{10,11... | collective-permute-start | bytes 884744 | tf_op jit(solution)/shard_map/ppermute | solution.py:525
  125.3 8.3 %collective-permute-start.56 = (bf16[384,384]{1,0:T(8,128)(2,1)S(1)}, bf16[384,384]{1,0:T(8,128)(2,1)S(1)}, u32[]{:S(2)}, u32[]{:S(2)}) collective-permute-start(bf16[384,384]{1,0:T(8,128)(2,1)S(1)} %gate.25.rest_1_), channel_id=1, source_target_pairs={{0,1},{1,0},{2,3},{3,2},{4,5},{5,4},{6,7},{7,6},{8,9},{9,8},{10,11... | collective-permute-start | bytes 884744 | tf_op jit(solution)/shard_map/ppermute | solution.py:525
  125.8 7.8 %collective-permute-start.57 = (bf16[2,384,384]{2,1,0:T(8,128)(2,1)S(1)}, bf16[2,384,384]{2,1,0:T(8,128)(2,1)S(1)}, u32[]{:S(2)}, u32[]{:S(2)}) collective-permute-start(bf16[2,384,384]{2,1,0:T(8,128)(2,1)S(1)} %sum_pair.3.rest_2_), channel_id=1, source_target_pairs={{0,1},{1,0},{2,3},{3,2},{4,5},{5,4},{6,7},{7,6},{8,9},{9,8},{10,11... | collective-permute-start | bytes 1769480 | tf_op jit(solution)/shard_map/ppermute | solution.py:525
  (34 other events, 143.9 us)

commit v4 on v3

--- a/solution.py
+++ b/solution.py
@@ -77,62 +77,82 @@
         send[sent, pl.ds(*rows)] = jnp.where(first, half_one, half_zero)
 
 
-def usable(rows, limits):
-    key_index = lax.broadcasted_iota(jnp.int32, (rows, rows), 0)
-    query_index = lax.broadcasted_iota(jnp.int32, (rows, rows), 1)
-    return (key_index <= query_index) & (key_index < limits[0:1, :rows])
-
-
-def head_lanes(rows, side):
-    lane = lax.broadcasted_iota(jnp.int32, (rows, 2 * HEAD), 1)
-    return (lane < HEAD) if side == 0 else (lane >= HEAD)
+def query_blocks(rows):
+    step = min(rows, 128)
+    return [(first, first + step) for first in range(0, rows, step)]
+
+
+def usable(first, last, limits):
+    key_index = lax.broadcasted_iota(jnp.int32, (last, last - first), 0)
+    query_index = lax.broadcasted_iota(jnp.int32, (last, last - first), 1) + first
+    return (key_index <= query_index) & (key_index < limits[0:1, first:last])
+
+
+def one_head(block, side):
+    lane = lax.broadcasted_iota(jnp.int32, block.shape, 1)
+    return jnp.where((lane < HEAD) if side == 0 else (lane >= HEAD), block, 0)
+
+
+def pair_at(head):
+    return 2 * HEAD * (head // 2)
 
 
 def attend(mixed, limits, probabilities):
+    blocks = query_blocks(mixed.shape[0])
+    values_across = mixed[:, 2 * D :].T
+    allowed = [usable(first, last, limits) for first, last in blocks]
+    for head in range(HEADS):
+        at = pair_at(head)
+        for (first, last), mask in zip(blocks, allowed):
+            queries = one_head(mixed[first:last, at : at + 2 * HEAD], head % 2)
+            scores = nt(mixed[:last, D + at : D + at + 2 * HEAD], queries) * HEAD ** (-0.5)
+            probabilities[head, :last, first:last] = jnp.where(mask, scores, MASKED)
+    outs = []
+    for head in range(HEADS):
+        parts = []
+        for first, last in blocks:
+            scores = probabilities[head, :last, first:last]
+            raised = jnp.exp(scores - jnp.max(scores, 0, keepdims=True))
+            probability = raised * (1.0 / jnp.sum(raised, 0, keepdims=True))
+            probabilities[head, :last, first:last] = probability
+            values = values_across[HEAD * head : HEAD * head + HEAD, :last]
+            parts.append(nn(values, probability.astype(bf16)))
+        outs.append(jnp.concatenate(parts, 1))
+    return jnp.concatenate(outs, 0).T.astype(bf16)
+
+
+def attend_back(mixed, grad_heads, probabilities, grad_mixed, grad_probs, rounded):
     rows = mixed.shape[0]
-    allowed = usable(rows, limits)
-    values_across = mixed[:, 2 * D :].T
-    outs = []
-    for pair in range(HEADS // 2):
-        at = 2 * HEAD * pair
-        queries = mixed[:, at : at + 2 * HEAD]
-        key_rows = mixed[:, D + at : D + at + 2 * HEAD]
-        for side in range(2):
-            head = 2 * pair + side
-            one_head = jnp.where(head_lanes(rows, side), queries, 0)
-            scores = jnp.where(allowed, nt(key_rows, one_head) * HEAD ** (-0.5), MASKED)
-            peak = jnp.max(scores, 0, keepdims=True)
-            raised = jnp.exp(scores - peak)
-            inverse = 1.0 / jnp.sum(raised, 0, keepdims=True)
-            probability = raised * inverse
-            probabilities[head] = probability
-            outs.append(nn(values_across[HEAD * head : HEAD * head + HEAD], probability.astype(bf16)))
-    return jnp.concatenate(outs, 0).T.astype(bf16)
-
-
-def attend_back(mixed, grad_heads, probabilities, grad_mixed):
-    rows = mixed.shape[0]
+    blocks = query_blocks(rows)
     keys_across = mixed[:, D : 2 * D].T
+    for head in range(HEADS):
+        at = pair_at(head)
+        for first, last in blocks:
+            grads = one_head(grad_heads[first:last, at : at + 2 * HEAD], head % 2)
+            values = mixed[:last, 2 * D + at : 2 * D + at + 2 * HEAD]
+            grad_probs[head, :last, first:last] = nt(values, grads)
+    for head in range(HEADS):
+        for first, last in blocks:
+            probability = probabilities[head, :last, first:last]
+            grad_prob = grad_probs[head, :last, first:last]
+            middle = jnp.sum(probability * grad_prob, 0, keepdims=True)
+            rounded[0, head, :last, first:last] = (probability * (grad_prob - middle)).astype(bf16)
+            rounded[1, head, :last, first:last] = probability.astype(bf16)
+            if last < rows:
+                unused = jnp.zeros((rows - last, last - first), bf16)
+                rounded[0, head, last:, first:last] = unused
+                rounded[1, head, last:, first:last] = unused
     query_parts = []
     for pair in range(HEADS // 2):
         at = 2 * HEAD * pair
         queries = mixed[:, at : at + 2 * HEAD]
-        values = mixed[:, 2 * D + at : 2 * D + at + 2 * HEAD]
         grads = grad_heads[:, at : at + 2 * HEAD]
-        key_grad = jnp.zeros((rows, 2 * HEAD), f32)
-        value_grad = jnp.zeros((rows, 2 * HEAD), f32)
+        key_grad = value_grad = 0.0
         for side in range(2):
             head = 2 * pair + side
-            lanes = head_lanes(rows, side)
-            one_head = jnp.where(lanes, queries, 0)
-            one_grad = jnp.where(lanes, grads, 0)
-            probability = probabilities[head]
-            grad_prob = nt(values, one_grad)
-            middle = jnp.sum(probability * grad_prob, 0, keepdims=True)
-            grad_scores = (probability * (grad_prob - middle)).astype(bf16)
-            key_grad += nn(grad_scores, one_head)
-            value_grad += nn(probability.astype(bf16), one_grad)
-            query_parts.append(nn(keys_across[HEAD * head : HEAD * head + HEAD], grad_scores))
+            key_grad += nn(rounded[0, head], one_head(queries, side))
+            value_grad += nn(rounded[1, head], one_head(grads, side))
+            query_parts.append(nn(keys_across[HEAD * head : HEAD * head + HEAD], rounded[0, head]))
         grad_mixed[:, D + at : D + at + 2 * HEAD] = (key_grad * HEAD ** (-0.5)).astype(bf16)
         grad_mixed[:, 2 * D + at : 2 * D + at + 2 * HEAD] = value_grad.astype(bf16)
     grad_mixed[:, :D] = (jnp.concatenate(query_parts, 0).T * HEAD ** (-0.5)).astype(bf16)
@@ -141,7 +161,7 @@
 def prepare_kernel(
     mixing, output, pair, fresh, output_three, gain_one, gain_two, gain_three, gain_four,
     up_two, down_two, up_four, down_four, lengths,
-    one, three, mine_one, mine_two, mine_four, limits, edge, narrow_one, narrow_two, narrow_three, narrow_four, sems,
+    one, three, mine_one, mine_two, mine_four, limits, edge, narrow_one, narrow_two, narrow_three, narrow_four, counts, sems,
 ):
     core = place()[1]
     count = mixing.shape[0]
@@ -174,11 +194,14 @@
     ]
     for copy in gains:
         copy.start()
-    limits[...] = jnp.full(limits.shape, lengths[0, place()[0]], jnp.int32)
+    counted = pltpu.make_async_copy(lengths, counts, sems.at[len(copies) + len(gains)])
+    counted.start()
     edge[...] = jnp.zeros_like(edge)
     for k, narrow in enumerate((narrow_one, narrow_two, narrow_three, narrow_four)):
         gains[k].wait()
         edge[k : k + 1, : narrow.shape[0]] = narrow[...].astype(f32).reshape(1, narrow.shape[0])
+    counted.wait()
+    limits[...] = jnp.full(limits.shape, counts[0, place()[0]], jnp.int32)
     rows = D - last
     block = jnp.concatenate([edge[...], jnp.zeros((rows - 8, D), f32)], 0).astype(bf16)
     three[last:] = block
@@ -235,17 +258,17 @@
     scaled, _ = centre(hidden)
     normed = (scaled * gains[1:2, :]).astype(bf16)
     ups, downs = select_pieces(rest[:6])
+    for rank in (1, 2, 3):
+        held[0, rank], held[1, rank] = ups[rank - 1], downs[rank - 1]
+    for copy in copies:
+        copy.wait()
+    for rank in range(QUARTERS):
+        slopes[rank] = nn(normed, held[0, rank])
+    for rank in range(QUARTERS):
+        actives[rank], slopes[rank] = feed_parts(slopes[rank])
     total = hidden
-    for rank in (1, 2, 3, 0):
-        if rank:
-            held[0, rank], held[1, rank] = ups[rank - 1], downs[rank - 1]
-        else:
-            for copy in copies:
-                copy.wait()
-        active, slope = feed_parts(nn(normed, held[0, rank]))
-        actives[rank] = active
-        slopes[rank] = slope
-        total += nn(active, held[1, rank])
+    for rank in range(QUARTERS):
+        total += nn(actives[rank], held[1, rank])
     h2[...] = total.astype(bf16)
     hidden = h2[...].astype(f32)
     scaled, _ = centre(hidden)
@@ -271,19 +294,15 @@
     return nn(normed_across, grad_upward).astype(bf16), grad_down, nt(grad_upward, up)
 
 
-def seeded(limits, cotangent):
-    row = lax.broadcasted_iota(jnp.int32, cotangent.shape, 0)
-    return jnp.where(row < limits[0:1, :1], cotangent[...].astype(f32), 0.0)
-
-
 def fourth_kernel(limits, h3, gains, cotangent, own0, own1, near, far, other_near, other_far, *rest):
-    total, grad_normed, keep, send, held, sems = rest
+    total, grad_normed, keep, send, seed, held, brought, sems = rest
+    seeding = pltpu.make_async_copy(cotangent, brought, sems.at[2])
+    seeding.start()
     copies = bring(own0, own1, held, sems)
     hidden = h3[...].astype(f32)
     scaled, _ = centre(hidden)
     normed = (scaled * gains[3:4, :]).astype(bf16)
     normed_across = normed.T
-    grad_out = seeded(limits, cotangent).astype(bf16)
     first = place()[1] == 0
     after, grads = hidden, jnp.zeros(hidden.shape, f32)
     for rank in (1, 2, 0):
@@ -299,6 +318,11 @@
             up, down = held[0, 0], held[1, 0]
         active, slope = feed_parts(nn(normed, up))
         after += nn(active, down)
+        if rank == 1:
+            seeding.wait()
+            row = lax.broadcasted_iota(jnp.int32, hidden.shape, 0)
+            grad_out = jnp.where(row < limits[0:1, :1], brought[...], 0)
+            seed[...] = grad_out
         grad_up, grad_down, grad = quarter_back(up, down, normed_across, grad_out, active, slope)
         put(keep, send, rank, grad_up, grad_down)
         grads += grad
@@ -307,31 +331,31 @@
 
 
 def fourth_end_kernel(
-    limits, h3, gains, cotangent, total, grads, both, other_both, out, grad_h3, keep, send, grad_gain
+    h3, gains, seed, total, grads, both, other_both, out, grad_h3, keep, send, grad_gain
 ):
     scaled, rstd = centre(h3[...].astype(f32))
     gain = gains[3:4, :]
     normed = (scaled * gain).astype(bf16)
-    grad_out = seeded(limits, cotangent)
     first = place()[1] == 0
     up = jnp.where(first, both[...], other_both[...])
     down = jnp.where(first, other_both[...], both[...])
     active, slope = feed_parts(nn(normed, up))
     out[...] = total[...] + nn(active, down)
-    grad_up, grad_down, grad = quarter_back(up, down, normed.T, grad_out.astype(bf16), active, slope)
+    grad_up, grad_down, grad = quarter_back(up, down, normed.T, seed[...], active, slope)
     keep[...] = jnp.where(first, grad_up, grad_down)
     send[...] = jnp.where(first, grad_down, grad_up)
     grad_hidden, one_gain = norm_back(scaled, rstd, gain, grads[...] + grad)
     grad_gain[0:1, :] = one_gain
-    grad_h3[...] = (grad_out + grad_hidden).astype(bf16)
-
-
-def attention_back(hidden, grad_out, mixed, attended, probabilities, mixing, output, gain, grad_mixed, shared, value_grad):
+    grad_h3[...] = (seed[...].astype(f32) + grad_hidden).astype(bf16)
+
+
+def attention_back(hidden, grad_out, mixed, attended, probabilities, mixing, output, gain, scratch, shared, value_grad):
     scaled, rstd = centre(hidden)
     normed_across = (scaled * gain).astype(bf16).T
     grad_heads = nn(grad_out, output[...]).astype(bf16)
     grad_output = nn(attended[...].T, grad_out).astype(bf16)
-    attend_back(mixed, grad_heads, probabilities, grad_mixed)
+    grad_mixed = scratch[0]
+    attend_back(mixed, grad_heads, probabilities, *scratch)
     shared(grad_mixed)
     grad_pair = nn(normed_across, grad_mixed[:, : 2 * D]).astype(bf16)
     grad_values = value_grad(scaled, gain, normed_across, grad_mixed)
@@ -341,7 +365,7 @@
 
 def third_back_kernel(
     h2, gains, grad_h3, mixed, attended, probabilities, mixing, output,
-    grad_h2, grad_weights, grad_shared, grad_gain, grad_mixed,
+    grad_h2, grad_weights, grad_shared, grad_gain, *scratch,
 ):
     shared_width = SHARED * HEAD
 
@@ -355,7 +379,7 @@
 
     grad_hidden, one_gain, grad_pair, grad_fresh, grad_output = attention_back(
         h2[...].astype(f32), grad_h3[...], mixed, attended, probabilities, mixing, output,
-        gains[2:3, :], grad_mixed, hand_over, fresh_grad,
+        gains[2:3, :], scratch, hand_over, fresh_grad,
     )
     grad_weights[0, :D] = grad_pair[:, :D]
     grad_weights[0, D:] = grad_pair[:, D:]
@@ -385,7 +409,7 @@
 def first_back_kernel(
     tokens, gains, grad_h1, mixed, attended, probabilities, mixing, output,
     grad_shared, third_weights, gain_two, gain_three, gain_four,
-    input_grad, keep, send, grad_mixed,
+    input_grad, keep, send, *scratch,
 ):
     shared_width = SHARED * HEAD
 
@@ -398,7 +422,7 @@
 
     grad_hidden, gain_one, grad_pair, grad_values, grad_output = attention_back(
         tokens[...].astype(f32), grad_h1[...], mixed, attended, probabilities, mixing, output,
-        gains[0:1, :], grad_mixed, take_over, value_grad,
+        gains[0:1, :], scratch, take_over, value_grad,
     )
     input_grad[...] = grad_h1[...].astype(f32) + grad_hidden
     section, part = place()[0], D // 2
@@ -417,6 +441,13 @@
 
 
 def pieces_of(refs):
+    if len(refs) == 4:
+        for own, (mine, pair) in ((True, refs[:2]), (False, refs[2:])):
+            yield own, 0, mine[0]
+            yield own, 2, mine[1]
+            yield own, 1, pair[0]
+            yield own, 3, pair[1]
+        return
     for own, (mine, far, pair) in ((True, refs[:3]), (False, refs[3:])):
         yield own, 0, mine[...]
         yield own, 2, far[...]
@@ -425,10 +456,10 @@
 
 
 def unpack_feed_kernel(*rest):
-    up, down, wide, sems = rest[6:]
+    up, down, wide, sems = rest[-4:]
     section, core = place()
     steps = []
-    for slot, (own, rank, value) in enumerate(pieces_of(rest[:6])):
+    for slot, (own, rank, value) in enumerate(pieces_of(rest[:-4])):
         wide[slot] = value.astype(f32)
         zero = (core == 0) if own else (core != 0)
         column = pl.ds(pl.multiple_of((section ^ rank) * D, D), D)
@@ -443,13 +474,13 @@
         pl.when(flag)(copy.wait)
 
 
-def unpack_attention_kernel(*rest):
-    mixing, output, pair, fresh, output_three, g1, g2, g3, g4, wide, sems = rest[6:]
+def unpack_attention(pieces, targets, gains, wide, sems):
+    mixing, output, pair, fresh, output_three = targets
     section, core = place()
     part = D // 2
     steps = []
-    for slot, (own, rank, value) in enumerate(pieces_of(rest[:6])):
-        wide[slot] = value.astype(f32)
+    for slot, (own, rank, value) in enumerate(pieces):
+        wide[slot] = value[...].astype(f32)
         zero = (core == 0) if own else (core != 0)
         j0, j1 = section ^ rank, section ^ swapped(rank)
         column = pl.ds(pl.multiple_of((j0 >> 1) * D, D), D)
@@ -459,7 +490,7 @@
 
         @pl.when(one & (j1 == 0))
         def _():
-            for k, ref in enumerate((g1, g2, g3, g4)):
+            for k, ref in enumerate(gains):
                 ref[...] = wide[slot, part + k]
 
         for low, flag, target in (
@@ -479,10 +510,25 @@
         pl.when(flag)(copy.wait)
 
 
+def unpack_some_kernel(*rest):
+    pieces, outs, (wide, sems) = rest[:6], rest[6:-2], rest[-2:]
+    ranked = [(own, rank, pieces[3 * k + i]) for k, own in enumerate((True, False)) for i, rank in enumerate((0, 2, 1))]
+    for ref in outs[5:]:
+        ref[...] = jnp.zeros(ref.shape, f32)
+    unpack_attention(ranked, outs[:5], outs[5:], wide, sems)
+
+
+def unpack_rest_kernel(*rest):
+    pieces, before, outs, (wide, sems) = rest[:2], rest[7:11], rest[11:-2], rest[-2:]
+    for ref, old in zip(outs[5:], before):
+        ref[...] = old[...]
+    unpack_attention([(True, 3, pieces[0]), (False, 3, pieces[1])], outs[:5], outs[5:], wide, sems)
+
+
 SMEM, VMEM, HBM = pltpu.SMEM, pltpu.VMEM, pltpu.HBM
 
 
-def call(body, name, args, outs, scratch=(), spaces=None, limit=12, hint=20):
+def call(body, name, args, outs, scratch=(), spaces=None, limit=12, hint=20, aliases=None):
     spaces = spaces or {}
     args = [
         pltpu.with_memory_space_constraint(arg, HBM) if spaces.get(i) is HBM else arg
@@ -499,6 +545,7 @@
         in_specs=[pl.BlockSpec(memory_space=spaces.get(i, VMEM)) for i in range(len(args))],
         out_specs=[pl.BlockSpec(memory_space=places.get(where, VMEM)) for _, _, where in outs],
         scratch_shapes=list(scratch),
+        input_output_aliases=aliases or {},
         compiler_params=pltpu.CompilerParams(vmem_limit_bytes=limit * 1024 * 1024),
         cost_estimate=pl.CostEstimate(flops=hint * 10**9, bytes_accessed=1, transcendentals=1),
     )(*args)
@@ -542,6 +589,19 @@
     near[...] = total(keep[1], came[1])
 
 
+def begin_pair_kernel(keep, came, pair):
+    pair[0] = total(keep[3], came[3])
+    pair[1] = total(keep[1], came[1])
+
+
+def turn_pair_kernel(keep, came, pair, far):
+    far[...] = total(keep[2], came[2], pair[0])
+
+
+def own_pair_kernel(keep, came, pair, far, away, kept, halves):
+    own_kernel(keep, came, pair.at[1], far, away, kept, halves)
+
+
 def turn_kernel(keep, came, both, far):
     far[...] = total(keep[2], came[2], both[...])
 
@@ -565,6 +625,11 @@
     out[1] = right[...]
 
 
+def copy_both_kernel(left, right, left_out, right_out):
+    left_out[...] = left[...]
+    right_out[...] = right[...]
+
+
 def sum_kernel(left, right, out):
     out[...] = total(left[...], right[...])
 
@@ -617,6 +682,11 @@
         both, near = self.made(hint, begin_kernel, "sum_begin", [block] * 2, self.keep, self.came)
         self.both, self.near = partner(both, "near"), partner(near, "near")
 
+    def begin_merged(self, hint):
+        shape = (2,) + self.keep.shape[1:]
+        (pair,) = self.made(hint, begin_pair_kernel, "sum_begin", [shape], self.keep, self.came)
+        self.both = self.near = partner(pair, "near")
+
     def begin_near(self, hint):
         body = functools.partial(one_sum_kernel, 1)
         (near,) = self.made(hint, body, "sum_near", [self.keep.shape[1:]], self.keep, self.came)
@@ -627,16 +697,16 @@
         self.both = partner(both, "near")
 
     def turn(self, hint):
-        (far,) = self.made(
-            hint, turn_kernel, "sum_turn", [self.keep.shape[1:]], self.keep, self.came, self.both
-        )
+        body = turn_kernel if self.both is not self.near else turn_pair_kernel
+        (far,) = self.made(hint, body, "sum_turn", [self.keep.shape[1:]], self.keep, self.came, self.both)
         self.far = partner(far, "far")
 
     def own(self, hint):
         rows, width = self.keep.shape[1:]
         half = (rows // 2, width)
+        body = own_kernel if self.both is not self.near else own_pair_kernel
         away, self.kept = self.made(
-            hint, own_kernel, "sum_own", [half] * 2, self.keep, self.came, self.near, self.far,
+            hint, body, "sum_own", [half] * 2, self.keep, self.came, self.near, self.far,
             scratch=[VMEM((2,) + half, bf16)],
         )
         self.back = partner(away, 2)
@@ -673,6 +743,29 @@
         shape = (2,) + self.far.shape
         (pair,) = self.made(hint, pair_kernel, "sum_pair", [shape], self.near, self.both)
         self.pieces = [self.mine, self.far, pair] + self.others + [partner(pair, 1)]
+
+    def share_far(self, hint):
+        rows, width = self.kept.shape
+        (self.mine,) = self.made(hint, join_kernel, "sum_join", [(2 * rows, width)], self.kept, self.back)
+        self.far = partner(self.mine, "far")
+
+    def pass_pair(self, hint):
+        shape = (2,) + self.mine.shape
+        (self.mine,) = self.made(hint, pair_kernel, "sum_pair", [shape], self.mine, self.far)
+        self.near = partner(self.mine, "near")
+        self.others = [partner(self.mine, 1)]
+
+    def end_pair(self, hint):
+        pair = self.line.gate(self.near, hint)
+        self.pieces = [self.mine, pair] + self.others + [partner(pair, 1)]
+
+    def pass_near(self, hint):
+        self.near = self.line.gate(self.near, hint)
+        self.others.append(partner(self.near, 1))
+
+    def end_alone(self, hint):
+        both = self.line.gate(self.both, hint)
+        self.pieces = [both, partner(both, 1)]
 
 
 def shards(
@@ -698,6 +791,7 @@
     row, wide_row, held = (rows, D), (rows, 3 * D), (2, QUARTERS, D, D)
     gain_row, packed, chances = (8, D), (QUARTERS, D, D), (HEADS, rows, rows)
     hidden_row = (QUARTERS,) + row
+    back_scratch = [VMEM(wide_row, bf16), VMEM(chances, f32), VMEM((2,) + chances, bf16)]
     shared_width = SHARED * HEAD
     line = Line()
 
@@ -706,88 +800,90 @@
         (mixing_one.T, output_one.T, pair_three.T, fresh_three.T, output_three.T,
          gain_one, gain_two, gain_three, gain_four, up_two, down_two, up_four, down_four, lengths.T),
         [(square, bf16, "vmem")] * 5 + [((8, rows), jnp.int32, "vmem")],
-        [VMEM((8, D), f32)] + [VMEM(gain_one.shape, bf16)] * 4 + [pltpu.SemaphoreType.DMA((18,))],
-        {i: HBM for i in range(13)} | {13: SMEM},
+        [VMEM((8, D), f32)] + [VMEM(gain_one.shape, bf16)] * 4
+        + [SMEM(lengths.T.shape, jnp.int32), pltpu.SemaphoreType.DMA((19,))],
+        {i: HBM for i in range(14)},
     )
     near_one, far_one = partner(mine_one, "near"), partner(mine_one, "far")
     near_two, far_two = partner(mine_two, "near"), partner(mine_two, "far")
-    near_one = line.gate(near_one, 20)
+    limits = line.gate(limits, 0)
+    near_one = line.gate(near_one, 3)
     other_near_one = partner(near_one, 1)
     both_one = partner(near_one, "far")
-    near_two = line.gate(near_two, 20)
+    far_one = line.gate(far_one, 3)
+    other_far_one = partner(far_one, 1)
+    near_two = line.gate(near_two, 3)
     other_near_two = partner(near_two, 1)
     both_two = partner(near_two, "far")
-    far_one = line.gate(far_one, 20)
-    other_far_one = partner(far_one, 1)
-    limits = line.gate(limits, 20)
-    both_two = line.gate(both_two, 20)
+    mine_four = line.gate(mine_four, 3)
+    near_four, far_four = partner(mine_four, "near"), partner(mine_four, "far")
+    both_one = line.gate(both_one, 8)
+    other_both_one = partner(both_one, 1)
+    far_two = line.gate(far_two, 3)
+    other_far_two = partner(far_two, 1)
+    both_two = line.gate(both_two, 3)
     other_both_two = partner(both_two, 1)
-    far_two = line.gate(far_two, 20)
-    other_far_two = partner(far_two, 1)
-    mine_four = line.gate(mine_four, 20)
-    near_four, far_four = partner(mine_four, "near"), partner(mine_four, "far")
-    both_one = line.gate(both_one, 20)
-    other_both_one = partner(both_one, 1)
     h1, mixed_one, attended_one, chances_one, mixing, output, mixing_three, out_three, gains = line.step(
         lambda *args: call(
             first_kernel, "first_forward", args,
             [(row, bf16, "vmem"), (wide_row, bf16, "vmem"), (row, bf16, "vmem"), (chances, f32, "vmem"),
              ((3 * D, D), bf16, "vmem"), (square, bf16, "vmem"), ((3 * D, D), bf16, "vmem"),
              (square, bf16, "vmem"), (gain_row, f32, "vmem")],
-            [VMEM(held, bf16)], hint=20,
+            [VMEM(held, bf16)], hint=6,
         ),
         limits, tokens, half_one, half_three,
         near_one, far_one, both_one, other_near_one, other_far_one, other_both_one,
     )
+    near_four = line.gate(near_four, 3)
+    other_near_four = partner(near_four, 1)
+    both_four = partner(near_four, "far")
+    far_four = line.gate(far_four, 4)
+    other_far_four = partner(far_four, 1)
     h2, held_two, h3, mixed_three, attended_three, chances_three, actives, slopes = line.step(
         lambda *args: call(
             middle_kernel, "second_third_forward", args,
             [(row, bf16, "vmem"), (held, bf16, "vmem"), (row, bf16, "vmem"), (wide_row, bf16, "vmem"),
              (row, bf16, "vmem"), (chances, f32, "vmem"), (hidden_row, bf16, "vmem"),
              (hidden_row, f32, "vmem")],
-            [pltpu.SemaphoreType.DMA((2,))], {6: HBM, 7: HBM}, hint=20,
+            [pltpu.SemaphoreType.DMA((2,))], {6: HBM, 7: HBM}, hint=3,
         ),
         limits, h1, gains, mixing_three, out_three, mixed_one, up_two, down_two,
         near_two, far_two, both_two, other_near_two, other_far_two, other_both_two,
     )
-    far_four = line.gate(far_four, 20)
-    other_far_four = partner(far_four, 1)
-    near_four = line.gate(near_four, 0)
-    other_near_four = partner(near_four, 1)
-    both_four = partner(near_four, "far")
+    both_four = line.gate(both_four, 2)
+    other_both_four = partner(both_four, 1)
     three_quarters = (QUARTERS - 1, D, D)
-    after, grad_normed, keep, send = line.step(
+    after, grad_normed, keep, send, seed = line.step(
         lambda *args: call(
             fourth_kernel, "fourth_both", args,
             [(row, f32, "vmem"), (row, f32, "vmem"), (three_quarters, bf16, "vmem"),
-             (three_quarters, bf16, "vmem")],
-            [VMEM((2, 1, D, D), bf16), pltpu.SemaphoreType.DMA((2,))], {4: HBM, 5: HBM}, hint=20,
+             (three_quarters, bf16, "vmem"), (row, bf16, "vmem")],
+            [VMEM((2, 1, D, D), bf16), VMEM(row, bf16), pltpu.SemaphoreType.DMA((3,))],
+            {3: HBM, 4: HBM, 5: HBM}, hint=3,
         ),
         limits, h3, gains, cotangent, up_four, down_four,
         near_four, far_four, other_near_four, other_far_four,
     )
     four = Chunk(line, keep, send)
-    both_four = line.gate(both_four, 20)
-    other_both_four = partner(both_four, 1)
     out, grad_h3, last_keep, last_send, gain_grad_four = line.step(
         lambda *args: call(
             fourth_end_kernel, "fourth_end", args,
             [(row, f32, "plain"), (row, bf16, "vmem"), (square, bf16, "vmem"), (square, bf16, "vmem"),
              (gain_row, f32, "vmem")], hint=20,
         ),
-        limits, h3, gains, cotangent, after, grad_normed, both_four, other_both_four,
-    )
-    four.begin_near(20)
-    four.begin_both(last_keep, last_send, 20)
+        h3, gains, seed, after, grad_normed, both_four, other_both_four,
+    )
     grad_h2, third_weights, grad_shared, gain_grad_three = line.step(
         lambda *args: call(
             third_back_kernel, "third_backward", args,
             [(row, bf16, "vmem"), ((2, 2 * D, D), bf16, "vmem"), ((rows, shared_width), bf16, "vmem"),
              (gain_row, f32, "vmem")],
-            [VMEM(wide_row, bf16)], hint=3,
+            back_scratch, hint=8,
         ),
         h2, gains, grad_h3, mixed_three, attended_three, chances_three, mixing_three, out_three,
     )
+    four.begin_both(last_keep, last_send, 20)
+    four.begin_near(20)
     grad_h1, keep, send, gain_grad_two = line.step(
         lambda *args: call(
             second_back_kernel, "second_backward", args,
@@ -801,52 +897,63 @@
         lambda *args: call(
             first_back_kernel, "first_backward", args,
             [(row, f32, "plain"), (packed, bf16, "vmem"), (packed, bf16, "vmem")],
-            [VMEM(wide_row, bf16)], hint=20,
+            back_scratch, hint=8,
         ),
         tokens, gains, grad_h1, mixed_one, attended_one, chances_one, mixing, output,
         grad_shared, third_weights, gain_grad_two, gain_grad_three, gain_grad_four,
     )
     first = Chunk(line, keep, send)
     two.begin(20)
-    four.own(3)
+    four.own(5)
+    first.begin(5)
     two.turn(20)
-    four.along(20)
-    first.begin(20)
-    two.own(20)
+    four.along(5)
+    two.own(1)
     four.across(20)
-    first.turn(20)
-    two.along(20)
-    four.share(20)
+    first.turn(6)
+    two.along(8)
+    four.share_far(5)
     first.own(20)
     two.across(20)
-    four.pass_on(20)
+    four.pass_pair(2)
     first.along(20)
     two.share(20)
-    four.end(20)
-    first.across(20)
-    two.pass_on(20)
-    first.share(20)
+    first.across(5)
+    four.end_pair(5)
+    two.pass_on(1)
+    first.share(5)
     two.end(3)
     first.pass_on(2)
     feed_outs = [((D, 4 * D), f32, "hbm"), ((4 * D, D), f32, "hbm")]
     feed_scratch = [VMEM((8, D, D), f32), pltpu.SemaphoreType.DMA((8,))]
+    grad_up_four, grad_down_four = line.step(
+        lambda *args: call(unpack_feed_kernel, "unpack_four", args, feed_outs, feed_scratch, hint=3),
+        *four.pieces,
+    )
+    first.pass_near(2)
     grad_up_two, grad_down_two = line.step(
         lambda *args: call(unpack_feed_kernel, "unpack_two", args, feed_outs, feed_scratch, hint=1),
         *two.pieces,
     )
-    first.end(20)
-    grad_up_four, grad_down_four = line.step(
-        lambda *args: call(unpack_feed_kernel, "unpack_four", args, feed_outs, feed_scratch, hint=20),
-        *four.pieces,
+    first.end_alone(8)
+    attention_outs = [
+        ((D, 3 * D), f32, "hbm"), (square, f32, "hbm"), ((D, 2 * D), f32, "hbm"),
+        ((D // 2, D), f32, "hbm"), (square, f32, "hbm"),
+    ] + [((D,), f32, "plain")] * 4
+    unpacked = line.step(
+        lambda *args: call(
+            unpack_some_kernel, "unpack_some", args, attention_outs,
+            [VMEM((6, D, D), f32), pltpu.SemaphoreType.DMA((6, 2))], hint=3,
+        ),
+        first.mine, first.far, first.near, *first.others,
     )
     mixing_g, output_g, pair_g, fresh_g, output_three_g, g1, g2, g3, g4 = line.step(
         lambda *args: call(
-            unpack_attention_kernel, "unpack_attention", args,
-            [((D, 3 * D), f32, "hbm"), (square, f32, "hbm"), ((D, 2 * D), f32, "hbm"),
-             ((D // 2, D), f32, "hbm"), (square, f32, "hbm")] + [((D,), f32, "plain")] * 4,
-            [VMEM((8, D, D), f32), pltpu.SemaphoreType.DMA((8, 2))], hint=20,
+            unpack_rest_kernel, "unpack_rest", args, attention_outs,
+            [VMEM((2, D, D), f32), pltpu.SemaphoreType.DMA((2, 2))], {i: HBM for i in range(2, 7)},
+            hint=4, aliases={i + 2: i for i in range(5)},
         ),
-        *first.pieces,
+        *first.pieces, *unpacked,
     )
     return (
         out, input_grad, g1, mixing_g, output_g, g2, grad_up_two, grad_down_two,

time: 139 us -> 132 us (0.950)
  waiting for transfers between devices: 49.1 us -> 41 us
  starting transfers between devices: 51.7 us -> 57.5 us
  Pallas kernels: 35.5 us -> 31.8 us
    ppermute x58 -> x57, waiting for transfers between devices: 49.1 us -> 41 us  [partner(): lax.ppermute(value, ('section', 'dp'), partner_pairs(sections, groups, ki...]
    ppermute x58 -> x57, starting transfers between devices: 51.7 us -> 57.5 us  [partner(): lax.ppermute(value, ('section', 'dp'), partner_pairs(sections, groups, ki...]
    pallas_call x47 -> x49, Pallas kernels: 35.5 us -> 31.8 us  [call(): pl.pallas_call(body, name=name, out_shape=[places[where](shape, dtype) if...]
  transfers between devices with their start and end apart: 58 -> 57, of which waited for: 22 -> 21; matrix products, arithmetic and copies ran while one was open for 0% -> 0% of each run, Pallas kernels for 22% -> 22%
where the time goes in v4:
time: 132 us
  starting transfers between devices  57.5 us (44%)
  waiting for transfers between devices  41 us (31%)
  Pallas kernels  31.8 us (24%)
    ppermute x57, starting transfers between devices, partner(): lax.ppermute(value, ('section', 'dp'), partner_pairs(sections, groups, ki...  57.5 us
    ppermute x57, waiting for transfers between devices, partner(): lax.ppermute(value, ('section', 'dp'), partner_pairs(sections, groups, ki...  41 us
    pallas_call x49, Pallas kernels, call(): pl.pallas_call(body, name=name, out_shape=[places[where](shape, dtype) if...  31.8 us
  transfers between devices with their start and end apart: 57, of which 21 were waited for; matrix products, arithmetic and copies ran while one was open for 0% of the time, Pallas kernels for 22%

profile of v4, /device:TPU:0, one launch (start us, length us, event | category | flops | bytes accessed | tf_op | source)
XLA Modules:
  0.0 131.6 jit_solution(13519059365485070151)
XLA Ops:
  2.3 3.0 %collective-permute-start = (bf16[384,384]{1,0:T(8,128)(2,1)S(1)}, bf16[384,384]{1,0:T(8,128)(2,1)S(1)}, u32[]{:S(2)}, u32[]{:S(2)}) collective-permute-start(bf16[384,384]{1,0:T(8,128)(2,1)S(1)} %get-tuple-element.255), channel_id=1, source_target_pairs={{0,8},{1,17},{2,10},{3,19},{4,12},{5,21},{6,14},{7,23},{8,0},{9,25... | collective-permute-start | bytes 884744 | tf_op jit(solution)/shard_map/ppermute | solution.py:572
  7.4 5.2 %collective-permute-done.value = bf16[384,384]{1,0:T(8,128)(2,1)S(1)} collective-permute-done((bf16[384,384]{1,0:T(8,128)(2,1)S(1)}, bf16[384,384]{1,0:T(8,128)(2,1)S(1)}, u32[]{:S(2)}, u32[]{:S(2)}) %collective-permute-start) | collective-permute-done | bytes 294944 | tf_op jit(solution)/shard_map/ppermute | solution.py:572
  12.7 2.7 %collective-permute-start.2 = (bf16[384,384]{1,0:T(8,128)(2,1)S(1)}, bf16[384,384]{1,0:T(8,128)(2,1)S(1)}, u32[]{:S(2)}, u32[]{:S(2)}) collective-permute-start(bf16[384,384]{1,0:T(8,128)(2,1)S(1)} %gate.17.rest_0_), channel_id=1, source_target_pairs={{0,16},{1,9},{2,18},{3,11},{4,20},{5,13},{6,22},{7,15},{8,24},{9,1... | collective-permute-start | bytes 884744 | tf_op jit(solution)/shard_map/ppermute | solution.py:572
  15.5 3.4 %collective-permute-done.3.value = bf16[384,384]{1,0:T(8,128)(2,1)S(1)} collective-permute-done((bf16[384,384]{1,0:T(8,128)(2,1)S(1)}, bf16[384,384]{1,0:T(8,128)(2,1)S(1)}, u32[]{:S(2)}, u32[]{:S(2)}) %collective-permute-start.3) | collective-permute-done | bytes 294944 | tf_op jit(solution)/shard_map/ppermute | solution.py:572
  18.9 2.7 %collective-permute-start.7 = (bf16[384,384]{1,0:T(8,128)(2,1)S(1)}, bf16[384,384]{1,0:T(8,128)(2,1)S(1)}, u32[]{:S(2)}, u32[]{:S(2)}) collective-permute-start(bf16[384,384]{1,0:T(8,128)(2,1)S(1)} %gate.19.rest_0_), channel_id=1, source_target_pairs={{0,16},{1,9},{2,18},{3,11},{4,20},{5,13},{6,22},{7,15},{8,24},{9,1... | collective-permute-start | bytes 884744 | tf_op jit(solution)/shard_map/ppermute | solution.py:572
  21.8 1.7 %collective-permute-start.13 = (bf16[384,384]{1,0:T(8,128)(2,1)S(1)}, bf16[384,384]{1,0:T(8,128)(2,1)S(1)}, u32[]{:S(2)}, u32[]{:S(2)}) collective-permute-start(bf16[384,384]{1,0:T(8,128)(2,1)S(1)} %gate.20), channel_id=1, source_target_pairs={{0,8},{1,17},{2,10},{3,19},{4,12},{5,21},{6,14},{7,23},{8,0},{9,25... | collective-permute-start | bytes 884744 | tf_op jit(solution)/shard_map/ppermute | solution.py:572
  23.7 4.3 %collective-permute-done.7.value = bf16[384,384]{1,0:T(8,128)(2,1)S(1)} collective-permute-done((bf16[384,384]{1,0:T(8,128)(2,1)S(1)}, bf16[384,384]{1,0:T(8,128)(2,1)S(1)}, u32[]{:S(2)}, u32[]{:S(2)}) %collective-permute-start.7) | collective-permute-done | bytes 294944 | tf_op jit(solution)/shard_map/ppermute | solution.py:572
  27.9 2.5 %collective-permute-start.12 = (bf16[384,384]{1,0:T(8,128)(2,1)S(1)}, bf16[384,384]{1,0:T(8,128)(2,1)S(1)}, u32[]{:S(2)}, u32[]{:S(2)}) collective-permute-start(bf16[384,384]{1,0:T(8,128)(2,1)S(1)} %gate.20), channel_id=1, source_target_pairs={{0,16},{1,9},{2,18},{3,11},{4,20},{5,13},{6,22},{7,15},{8,24},{9,1... | collective-permute-start | bytes 884744 | tf_op jit(solution)/shard_map/ppermute | solution.py:572
  31.1 2.2 %first_forward.1 = (bf16[256,384]{1,0:T(8,128)(2,1)S(1)}, bf16[256,1152]{1,0:T(8,128)(2,1)S(1)}, bf16[256,384]{1,0:T(8,128)(2,1)S(1)}, f32[6,256,256]{2,1,0:T(8,...) custom-call(s32[8,256]{1,0:T(8,128)S(1)} %gate.16.limits, ...), custom_call_target="tpu_custom_call" | custom-call | flops 6000000000 | bytes 1 | tf_op jit(solution)/shard_map/first_forward/pallas_call | solution.py:538
  35.7 4.2 %second_third_forward.1 = (bf16[256,384]{1,0:T(8,128)(2,1)S(1)}, bf16[2,4,384,384]{3,2,1,0:T(8,128)(2,1)S(1)}, bf16[256,384]{1,0:T(8,128)(2,1)S(1)}, bf16[256,11...) custom-call(s32[8,256]{1,0:T(8,128)S(1)} %gate.16.limits, ...), custom_call_target="tpu_custom_call" | custom-call | flops 3000000000 | bytes 1 | tf_op jit(solution)/shard_map/second_third_forward/pallas_call | solution.py:538
  40.3 3.6 %fourth_both.1 = (f32[256,384]{1,0:T(8,128)S(1)}, f32[256,384]{1,0:T(8,128)S(1)}, bf16[3,384,384]{2,1,0:T(8,128)(2,1)S(1)}, bf16[3,384,384]{2,1,0:T(8,128)(2,1)S(1)}, bf16[256,384]{1,0:T(8,128)(2,1)S(1)}) custom-call(s32[8,256]{1,0:T(8,128)S(1)} %gate.16.limits, bf16[256,384]{1,0:T(8,128)(2,1)S(1)} %get-tuple-element.312.h3, ...), custom_call_target="tpu_custom_call" | custom-call | flops 3000000000 | bytes 1 | tf_op jit(solution)/shard_map/fourth_both/pallas_call | solution.py:538
  46.0 2.4 %third_backward.1 = (bf16[256,384]{1,0:T(8,128)(2,1)S(1)}, bf16[2,768,384]{2,1,0:T(8,128)(2,1)S(1)}, bf16[256,192]{1,0:T(8,128)(2,1)S(1)}, f32[8,384]{1,0:T(8,128)S(1)}) custom-call(bf16[256,384]{1,0:T(8,128)(2,1)S(1)} %get-tuple-element.324.h2, f32[8,384]{1,0:T(8,128)S(1)} %get-tuple-element.364.gains, bf16[256,384]{1,0:T(8,128)(2,1)S(1)} %get-tuple-element.326.grad_h3, ...), custom_call_target="tpu_custom_call" | custom-call | flops 8000000000 | bytes 1 | tf_op jit(solution)/shard_map/third_backward/pallas_call | solution.py:538
  50.8 2.3 %second_backward.1 = (bf16[256,384]{1,0:T(8,128)(2,1)S(1)}, bf16[4,384,384]{2,1,0:T(8,128)(2,1)S(1)}, bf16[4,384,384]{2,1,0:T(8,128)(2,1)S(1)}, f32[8,384]{1,0:T(8,128)S(1)}) custom-call(bf16[256,384]{1,0:T(8,128)(2,1)S(1)} %get-tuple-element.344.h1, f32[8,384]{1,0:T(8,128)S(1)} %get-tuple-element.364.gains, ...), custom_call_target="tpu_custom_call" | custom-call | flops 20000000000 | bytes 1 | tf_op jit(solution)/shard_map/second_backward/pallas_call | solution.py:538
  53.1 2.2 %collective-permute-done.20.both = bf16[384,384]{1,0:T(8,128)(2,1)S(1)} collective-permute-done((bf16[384,384]{1,0:T(8,128)(2,1)S(1)}, bf16[384,384]{1,0:T(8,128)(2,1)S(1)}, u32[]{:S(2)}, u32[]{:S(2)}) %collective-permute-start.20) | collective-permute-done | bytes 294944 | tf_op jit(solution)/shard_map/ppermute | solution.py:572
  55.5 1.9 %collective-permute-start.23 = (bf16[384,384]{1,0:T(8,128)(2,1)S(1)}, bf16[384,384]{1,0:T(8,128)(2,1)S(1)}, u32[]{:S(2)}, u32[]{:S(2)}) collective-permute-start(bf16[384,384]{1,0:T(8,128)(2,1)S(1)} %sum_turn.3), channel_id=1, source_target_pairs={{0,16},{1,9},{2,18},{3,11},{4,20},{5,13},{6,22},{7,15},{8,24},{9,1... | collective-permute-start | bytes 884744 | tf_op jit(solution)/shard_map/ppermute | solution.py:572
  57.4 3.4 %first_backward.1 = (f32[256,384]{1,0:T(8,128)}, bf16[4,384,384]{2,1,0:T(8,128)(2,1)S(1)}, bf16[4,384,384]{2,1,0:T(8,128)(2,1)S(1)}) custom-call(bf16[256,384]{1,0:T(8,128)(2,1)S(1)} %copy-done, f32[8,384]{1,0:T(8,128)S(1)} %get-tuple-element.364.gains, bf16[256,384]{1,0:T(8,128)(2,1)S(1)} %get-tuple-element.365.grad_h1, ...), custom_call_target="tpu_custom_call" | custom-call | flops 8000000000 | bytes 1 | tf_op jit(solution)/shard_map/first_backward/pallas_call | solution.py:538
  65.8 1.9 %collective-permute-done.28.both = bf16[384,384]{1,0:T(8,128)(2,1)S(1)} collective-permute-done((bf16[384,384]{1,0:T(8,128)(2,1)S(1)}, bf16[384,384]{1,0:T(8,128)(2,1)S(1)}, u32[]{:S(2)}, u32[]{:S(2)}) %collective-permute-start.28) | collective-permute-done | bytes 294944 | tf_op jit(solution)/shard_map/ppermute | solution.py:572
  67.8 1.7 %collective-permute-start.31 = (bf16[384,384]{1,0:T(8,128)(2,1)S(1)}, bf16[384,384]{1,0:T(8,128)(2,1)S(1)}, u32[]{:S(2)}, u32[]{:S(2)}) collective-permute-start(bf16[384,384]{1,0:T(8,128)(2,1)S(1)} %sum_turn.4), channel_id=1, source_target_pairs={{0,16},{1,9},{2,18},{3,11},{4,20},{5,13},{6,22},{7,15},{8,24},{9,1... | collective-permute-start | bytes 884744 | tf_op jit(solution)/shard_map/ppermute | solution.py:572
  69.6 2.7 %collective-permute-start.29 = (bf16[192,384]{1,0:T(8,128)(2,1)S(1)}, bf16[192,384]{1,0:T(8,128)(2,1)S(1)}, u32[]{:S(2)}, u32[]{:S(2)}) collective-permute-start(bf16[192,384]{1,0:T(8,128)(2,1)S(1)} %sum_chips.6.left), channel_id=1, source_target_pairs={{0,4},{1,5},{2,6},{3,7},{4,0},{5,1},{6,2},{7,3},{8,12},{9,13},{10,... | collective-permute-start | bytes 442376 | tf_op jit(solution)/shard_map/ppermute | solution.py:572
  74.3 1.8 %collective-permute-done.31.far = bf16[384,384]{1,0:T(8,128)(2,1)S(1)} collective-permute-done((bf16[384,384]{1,0:T(8,128)(2,1)S(1)}, bf16[384,384]{1,0:T(8,128)(2,1)S(1)}, u32[]{:S(2)}, u32[]{:S(2)}) %collective-permute-start.31) | collective-permute-done | bytes 294944 | tf_op jit(solution)/shard_map/ppermute | solution.py:572
  79.5 1.7 %collective-permute-start.32 = (bf16[384,384]{1,0:T(8,128)(2,1)S(1)}, bf16[384,384]{1,0:T(8,128)(2,1)S(1)}, u32[]{:S(2)}, u32[]{:S(2)}) collective-permute-start(bf16[384,384]{1,0:T(8,128)(2,1)S(1)} %sum_turn.5), channel_id=1, source_target_pairs={{0,16},{1,9},{2,18},{3,11},{4,20},{5,13},{6,22},{7,15},{8,24},{9,1... | collective-permute-start | bytes 884744 | tf_op jit(solution)/shard_map/ppermute | solution.py:572
  81.2 2.0 %collective-permute-done.34.right = bf16[192,384]{1,0:T(8,128)(2,1)S(1)} collective-permute-done((bf16[192,384]{1,0:T(8,128)(2,1)S(1)}, bf16[192,384]{1,0:T(8,128)(2,1)S(1)}, u32[]{:S(2)}, u32[]{:S(2)}) %collective-permute-start.34) | collective-permute-done | bytes 147488 | tf_op jit(solution)/shard_map/ppermute | solution.py:572
  83.2 4.1 %collective-permute-start.37 = (bf16[192,384]{1,0:T(8,128)(2,1)S(1)}, bf16[192,384]{1,0:T(8,128)(2,1)S(1)}, u32[]{:S(2)}, u32[]{:S(2)}) collective-permute-start(bf16[192,384]{1,0:T(8,128)(2,1)S(1)} %sum_chips.8.left), channel_id=1, source_target_pairs={{0,4},{1,5},{2,6},{3,7},{4,0},{5,1},{6,2},{7,3},{8,12},{9,13},{10,... | collective-permute-start | bytes 442376 | tf_op jit(solution)/shard_map/ppermute | solution.py:572
  90.0 2.0 %collective-permute-done.37.right = bf16[192,384]{1,0:T(8,128)(2,1)S(1)} collective-permute-done((bf16[192,384]{1,0:T(8,128)(2,1)S(1)}, bf16[192,384]{1,0:T(8,128)(2,1)S(1)}, u32[]{:S(2)}, u32[]{:S(2)}) %collective-permute-start.37) | collective-permute-done | bytes 147488 | tf_op jit(solution)/shard_map/ppermute | solution.py:572
  93.1 2.9 %collective-permute-done.36.right = bf16[384,384]{1,0:T(8,128)(2,1)S(1)} collective-permute-done((bf16[384,384]{1,0:T(8,128)(2,1)S(1)}, bf16[384,384]{1,0:T(8,128)(2,1)S(1)}, u32[]{:S(2)}, u32[]{:S(2)}) %collective-permute-start.36) | collective-permute-done | bytes 294944 | tf_op jit(solution)/shard_map/ppermute | solution.py:572
  97.1 2.8 %collective-permute-start.38 = (bf16[192,384]{1,0:T(8,128)(2,1)S(1)}, bf16[192,384]{1,0:T(8,128)(2,1)S(1)}, u32[]{:S(2)}, u32[]{:S(2)}) collective-permute-start(bf16[192,384]{1,0:T(8,128)(2,1)S(1)} %sum_chips.10.left), channel_id=1, source_target_pairs={{0,4},{1,5},{2,6},{3,7},{4,0},{5,1},{6,2},{7,3},{8,12},{9,13},{10,... | collective-permute-start | bytes 442376 | tf_op jit(solution)/shard_map/ppermute | solution.py:572
  100.7 2.3 %collective-permute-start.41 = (bf16[384,384]{1,0:T(8,128)(2,1)S(1)}, bf16[384,384]{1,0:T(8,128)(2,1)S(1)}, u32[]{:S(2)}, u32[]{:S(2)}) collective-permute-start(bf16[384,384]{1,0:T(8,128)(2,1)S(1)} %sum_join.4.rest_0_), channel_id=1, source_target_pairs={{0,16},{1,9},{2,18},{3,11},{4,20},{5,13},{6,22},{7,15},{8,24},{9,1... | collective-permute-start | bytes 884744 | tf_op jit(solution)/shard_map/ppermute | solution.py:572
  110.0 2.5 %collective-permute-start.43 = (bf16[384,384]{1,0:T(8,128)(2,1)S(1)}, bf16[384,384]{1,0:T(8,128)(2,1)S(1)}, u32[]{:S(2)}, u32[]{:S(2)}) collective-permute-start(bf16[384,384]{1,0:T(8,128)(2,1)S(1)} %sum_join.5.rest_0_), channel_id=1, source_target_pairs={{0,16},{1,9},{2,18},{3,11},{4,20},{5,13},{6,22},{7,15},{8,24},{9,1... | collective-permute-start | bytes 884744 | tf_op jit(solution)/shard_map/ppermute | solution.py:572
  112.5 5.1 %collective-permute-done.45.right = bf16[384,384]{1,0:T(8,128)(2,1)S(1)} collective-permute-done((bf16[384,384]{1,0:T(8,128)(2,1)S(1)}, bf16[384,384]{1,0:T(8,128)(2,1)S(1)}, u32[]{:S(2)}, u32[]{:S(2)}) %collective-permute-start.45) | collective-permute-done | bytes 294944 | tf_op jit(solution)/shard_map/ppermute | solution.py:572
  120.4 2.3 %unpack_four.1 = (f32[384,1536]{1,0:T(8,128)}, f32[1536,384]{1,0:T(8,128)}) custom-call(bf16[2,384,384]{2,1,0:T(8,128)(2,1)S(1)} %sum_pair.2.rest_0_, bf16[2,384,384]{2,1,0:T(8,128)(2,1)S(1)} %gate.27.rest_1_, bf16[2,384,384]{2,1,0:T(8,128)(2,1)S(1)} %collective-permute-done.51.rest_2_, bf16[2,384,384]{2,1,0:T(8,128)(2,1)S(1)} %collective-permute-done.52.rest_3_), custom_call_target="tpu_custom_call" | custom-call | flops 3000000000 | bytes 1 | tf_op jit(solution)/shard_map/unpack_four/pallas_call | solution.py:538
  125.0 2.3 %unpack_two.1 = (f32[384,1536]{1,0:T(8,128)}, f32[1536,384]{1,0:T(8,128)}) custom-call(bf16[384,384]{1,0:T(8,128)(2,1)S(1)} %sum_join.4.rest_0_, bf16[384,384]{1,0:T(8,128)(2,1)S(1)} %gate.28.rest_1_, bf16[2,384,384]{2,1,0:T(8,128)(2,1)S(1)} %sum_pair.3.rest_2_, bf16[384,384]{1,0:T(8,128)(2,1)S(1)} %collective-permute-done.47.rest_3_, ...), custom_call_target="tpu_custom_call" | custom-call | flops 1000000000 | bytes 1 | tf_op jit(solution)/shard_map/unpack_two/pallas_call | solution.py:538
  127.9 1.8 %unpack_some.1 = (f32[384,1152]{1,0:T(8,128)}, f32[384,384]{1,0:T(8,128)}, f32[384,768]{1,0:T(8,128)}, f32[192,384]{1,0:T(8,128)}, f32[384,384]{1,0:T(8,128)}, /...) custom-call(bf16[384,384]{1,0:T(8,128)(2,1)S(1)} %sum_join.5.rest_0_, ...), custom_call_target="tpu_custom_call" | custom-call | flops 3000000000 | bytes 1 | tf_op jit(solution)/shard_map/unpack_some/pallas_call | solution.py:538
  (133 shorter events, 42.8 us)
Async XLA Ops:
  2.3 10.3 %collective-permute-start = (bf16[384,384]{1,0:T(8,128)(2,1)S(1)}, bf16[384,384]{1,0:T(8,128)(2,1)S(1)}, u32[]{:S(2)}, u32[]{:S(2)}) collective-permute-start(bf16[384,384]{1,0:T(8,128)(2,1)S(1)} %get-tuple-element.255), channel_id=1, source_target_pairs={{0,8},{1,17},{2,10},{3,19},{4,12},{5,21},{6,14},{7,23},{8,0},{9,25... | collective-permute-start | bytes 884744 | tf_op jit(solution)/shard_map/ppermute | solution.py:572
  5.3 10.1 %collective-permute-start.1 = (bf16[384,384]{1,0:T(8,128)(2,1)S(1)}, bf16[384,384]{1,0:T(8,128)(2,1)S(1)}, u32[]{:S(2)}, u32[]{:S(2)}) collective-permute-start(bf16[384,384]{1,0:T(8,128)(2,1)S(1)} %get-tuple-element.255), channel_id=1, source_target_pairs={{0,16},{1,9},{2,18},{3,11},{4,20},{5,13},{6,22},{7,15},{8,24},{9,1... | collective-permute-start | bytes 884744 | tf_op jit(solution)/shard_map/ppermute | solution.py:572
  6.8 16.7 %collective-permute-start.8 = (bf16[384,384]{1,0:T(8,128)(2,1)S(1)}, bf16[384,384]{1,0:T(8,128)(2,1)S(1)}, u32[]{:S(2)}, u32[]{:S(2)}) collective-permute-start(bf16[384,384]{1,0:T(8,128)(2,1)S(1)} %get-tuple-element.259), channel_id=1, source_target_pairs={{0,16},{1,9},{2,18},{3,11},{4,20},{5,13},{6,22},{7,15},{8,24},{9,1... | collective-permute-start | bytes 884744 | tf_op jit(solution)/shard_map/ppermute | solution.py:572
  7.3 11.6 %collective-permute-start.3 = (bf16[384,384]{1,0:T(8,128)(2,1)S(1)}, bf16[384,384]{1,0:T(8,128)(2,1)S(1)}, u32[]{:S(2)}, u32[]{:S(2)}) collective-permute-start(bf16[384,384]{1,0:T(8,128)(2,1)S(1)} %get-tuple-element.259), channel_id=1, source_target_pairs={{0,8},{1,17},{2,10},{3,19},{4,12},{5,21},{6,14},{7,23},{8,0},{9,25... | collective-permute-start | bytes 884744 | tf_op jit(solution)/shard_map/ppermute | solution.py:572
  12.6 17.9 %collective-permute-start.4 = (bf16[384,384]{1,0:T(8,128)(2,1)S(1)}, bf16[384,384]{1,0:T(8,128)(2,1)S(1)}, u32[]{:S(2)}, u32[]{:S(2)}) collective-permute-start(bf16[384,384]{1,0:T(8,128)(2,1)S(1)} %gate.17.rest_0_), channel_id=1, source_target_pairs={{0,1},{1,0},{2,3},{3,2},{4,5},{5,4},{6,7},{7,6},{8,9},{9,8},{10,11... | collective-permute-start | bytes 884744 | tf_op jit(solution)/shard_map/ppermute | solution.py:572
  12.7 9.1 %collective-permute-start.2 = (bf16[384,384]{1,0:T(8,128)(2,1)S(1)}, bf16[384,384]{1,0:T(8,128)(2,1)S(1)}, u32[]{:S(2)}, u32[]{:S(2)}) collective-permute-start(bf16[384,384]{1,0:T(8,128)(2,1)S(1)} %gate.17.rest_0_), channel_id=1, source_target_pairs={{0,16},{1,9},{2,18},{3,11},{4,20},{5,13},{6,22},{7,15},{8,24},{9,1... | collective-permute-start | bytes 884744 | tf_op jit(solution)/shard_map/ppermute | solution.py:572
  15.4 15.0 %collective-permute-start.5 = (bf16[384,384]{1,0:T(8,128)(2,1)S(1)}, bf16[384,384]{1,0:T(8,128)(2,1)S(1)}, u32[]{:S(2)}, u32[]{:S(2)}) collective-permute-start(bf16[384,384]{1,0:T(8,128)(2,1)S(1)} %gate.18.rest_1_), channel_id=1, source_target_pairs={{0,1},{1,0},{2,3},{3,2},{4,5},{5,4},{6,7},{7,6},{8,9},{9,8},{10,11... | collective-permute-start | bytes 884744 | tf_op jit(solution)/shard_map/ppermute | solution.py:572
  18.9 9.0 %collective-permute-start.7 = (bf16[384,384]{1,0:T(8,128)(2,1)S(1)}, bf16[384,384]{1,0:T(8,128)(2,1)S(1)}, u32[]{:S(2)}, u32[]{:S(2)}) collective-permute-start(bf16[384,384]{1,0:T(8,128)(2,1)S(1)} %gate.19.rest_0_), channel_id=1, source_target_pairs={{0,16},{1,9},{2,18},{3,11},{4,20},{5,13},{6,22},{7,15},{8,24},{9,1... | collective-permute-start | bytes 884744 | tf_op jit(solution)/shard_map/ppermute | solution.py:572
  21.8 11.5 %collective-permute-start.13 = (bf16[384,384]{1,0:T(8,128)(2,1)S(1)}, bf16[384,384]{1,0:T(8,128)(2,1)S(1)}, u32[]{:S(2)}, u32[]{:S(2)}) collective-permute-start(bf16[384,384]{1,0:T(8,128)(2,1)S(1)} %gate.20), channel_id=1, source_target_pairs={{0,8},{1,17},{2,10},{3,19},{4,12},{5,21},{6,14},{7,23},{8,0},{9,25... | collective-permute-start | bytes 884744 | tf_op jit(solution)/shard_map/ppermute | solution.py:572
  23.5 7.5 %collective-permute-start.6 = (bf16[384,384]{1,0:T(8,128)(2,1)S(1)}, bf16[384,384]{1,0:T(8,128)(2,1)S(1)}, u32[]{:S(2)}, u32[]{:S(2)}) collective-permute-start(bf16[384,384]{1,0:T(8,128)(2,1)S(1)} %gate.21.rest_2_), channel_id=1, source_target_pairs={{0,1},{1,0},{2,3},{3,2},{4,5},{5,4},{6,7},{7,6},{8,9},{9,8},{10,11... | collective-permute-start | bytes 884744 | tf_op jit(solution)/shard_map/ppermute | solution.py:572
  27.9 7.2 %collective-permute-start.12 = (bf16[384,384]{1,0:T(8,128)(2,1)S(1)}, bf16[384,384]{1,0:T(8,128)(2,1)S(1)}, u32[]{:S(2)}, u32[]{:S(2)}) collective-permute-start(bf16[384,384]{1,0:T(8,128)(2,1)S(1)} %gate.20), channel_id=1, source_target_pairs={{0,16},{1,9},{2,18},{3,11},{4,20},{5,13},{6,22},{7,15},{8,24},{9,1... | collective-permute-start | bytes 884744 | tf_op jit(solution)/shard_map/ppermute | solution.py:572
  50.1 12.3 %collective-permute-start.22 = (bf16[384,384]{1,0:T(8,128)(2,1)S(1)}, bf16[384,384]{1,0:T(8,128)(2,1)S(1)}, u32[]{:S(2)}, u32[]{:S(2)}) collective-permute-start(bf16[384,384]{1,0:T(8,128)(2,1)S(1)} %sum_near.1), channel_id=1, source_target_pairs={{0,8},{1,17},{2,10},{3,19},{4,12},{5,21},{6,14},{7,23},{8,0},{9,25... | collective-permute-start | bytes 884744 | tf_op jit(solution)/shard_map/ppermute | solution.py:572
  64.3 9.9 %collective-permute-start.30 = (bf16[384,384]{1,0:T(8,128)(2,1)S(1)}, bf16[384,384]{1,0:T(8,128)(2,1)S(1)}, u32[]{:S(2)}, u32[]{:S(2)}) collective-permute-start(bf16[384,384]{1,0:T(8,128)(2,1)S(1)} %get-tuple-element.399), channel_id=1, source_target_pairs={{0,8},{1,17},{2,10},{3,19},{4,12},{5,21},{6,14},{7,23},{8,0},{9,25... | collective-permute-start | bytes 884744 | tf_op jit(solution)/shard_map/ppermute | solution.py:572
  67.8 8.3 %collective-permute-start.31 = (bf16[384,384]{1,0:T(8,128)(2,1)S(1)}, bf16[384,384]{1,0:T(8,128)(2,1)S(1)}, u32[]{:S(2)}, u32[]{:S(2)}) collective-permute-start(bf16[384,384]{1,0:T(8,128)(2,1)S(1)} %sum_turn.4), channel_id=1, source_target_pairs={{0,16},{1,9},{2,18},{3,11},{4,20},{5,13},{6,22},{7,15},{8,24},{9,1... | collective-permute-start | bytes 884744 | tf_op jit(solution)/shard_map/ppermute | solution.py:572
  69.6 9.1 %collective-permute-start.29 = (bf16[192,384]{1,0:T(8,128)(2,1)S(1)}, bf16[192,384]{1,0:T(8,128)(2,1)S(1)}, u32[]{:S(2)}, u32[]{:S(2)}) collective-permute-start(bf16[192,384]{1,0:T(8,128)(2,1)S(1)} %sum_chips.6.left), channel_id=1, source_target_pairs={{0,4},{1,5},{2,6},{3,7},{4,0},{5,1},{6,2},{7,3},{8,12},{9,13},{10,... | collective-permute-start | bytes 442376 | tf_op jit(solution)/shard_map/ppermute | solution.py:572
  72.2 7.2 %collective-permute-start.26 = (bf16[384,384]{1,0:T(8,128)(2,1)S(1)}, bf16[384,384]{1,0:T(8,128)(2,1)S(1)}, u32[]{:S(2)}, u32[]{:S(2)}) collective-permute-start(bf16[384,384]{1,0:T(8,128)(2,1)S(1)} %get-tuple-element.392), channel_id=1, source_target_pairs={{0,8},{1,17},{2,10},{3,19},{4,12},{5,21},{6,14},{7,23},{8,0},{9,25... | collective-permute-start | bytes 884744 | tf_op jit(solution)/shard_map/ppermute | solution.py:572
  72.8 16.3 %collective-permute-start.25 = (bf16[384,384]{1,0:T(8,128)(2,1)S(1)}, bf16[384,384]{1,0:T(8,128)(2,1)S(1)}, u32[]{:S(2)}, u32[]{:S(2)}) collective-permute-start(bf16[384,384]{1,0:T(8,128)(2,1)S(1)} %get-tuple-element.391), channel_id=1, source_target_pairs={{0,8},{1,17},{2,10},{3,19},{4,12},{5,21},{6,14},{7,23},{8,0},{9,25... | collective-permute-start | bytes 884744 | tf_op jit(solution)/shard_map/ppermute | solution.py:572
  78.8 8.6 %collective-permute-start.33 = (bf16[192,384]{1,0:T(8,128)(2,1)S(1)}, bf16[192,384]{1,0:T(8,128)(2,1)S(1)}, u32[]{:S(2)}, u32[]{:S(2)}) collective-permute-start(bf16[192,384]{1,0:T(8,128)(2,1)S(1)} %sum_chips.7.kept), channel_id=1, source_target_pairs={{0,2},{1,3},{2,0},{3,1},{4,6},{5,7},{6,4},{7,5},{8,10},{9,11},{10,... | collective-permute-start | bytes 442376 | tf_op jit(solution)/shard_map/ppermute | solution.py:572
  79.5 9.5 %collective-permute-start.32 = (bf16[384,384]{1,0:T(8,128)(2,1)S(1)}, bf16[384,384]{1,0:T(8,128)(2,1)S(1)}, u32[]{:S(2)}, u32[]{:S(2)}) collective-permute-start(bf16[384,384]{1,0:T(8,128)(2,1)S(1)} %sum_turn.5), channel_id=1, source_target_pairs={{0,16},{1,9},{2,18},{3,11},{4,20},{5,13},{6,22},{7,15},{8,24},{9,1... | collective-permute-start | bytes 884744 | tf_op jit(solution)/shard_map/ppermute | solution.py:572
  83.2 8.7 %collective-permute-start.37 = (bf16[192,384]{1,0:T(8,128)(2,1)S(1)}, bf16[192,384]{1,0:T(8,128)(2,1)S(1)}, u32[]{:S(2)}, u32[]{:S(2)}) collective-permute-start(bf16[192,384]{1,0:T(8,128)(2,1)S(1)} %sum_chips.8.left), channel_id=1, source_target_pairs={{0,4},{1,5},{2,6},{3,7},{4,0},{5,1},{6,2},{7,3},{8,12},{9,13},{10,... | collective-permute-start | bytes 442376 | tf_op jit(solution)/shard_map/ppermute | solution.py:572
  87.4 8.6 %collective-permute-start.36 = (bf16[384,384]{1,0:T(8,128)(2,1)S(1)}, bf16[384,384]{1,0:T(8,128)(2,1)S(1)}, u32[]{:S(2)}, u32[]{:S(2)}) collective-permute-start(bf16[384,384]{1,0:T(8,128)(2,1)S(1)} %sum_join.3.left), channel_id=1, source_target_pairs={{0,16},{1,9},{2,18},{3,11},{4,20},{5,13},{6,22},{7,15},{8,24},{9,1... | collective-permute-start | bytes 884744 | tf_op jit(solution)/shard_map/ppermute | solution.py:572
  89.3 7.7 %collective-permute-start.35 = (bf16[192,384]{1,0:T(8,128)(2,1)S(1)}, bf16[192,384]{1,0:T(8,128)(2,1)S(1)}, u32[]{:S(2)}, u32[]{:S(2)}) collective-permute-start(bf16[192,384]{1,0:T(8,128)(2,1)S(1)} %get-tuple-element.420), channel_id=1, source_target_pairs={{0,2},{1,3},{2,0},{3,1},{4,6},{5,7},{6,4},{7,5},{8,10},{9,11},{10,... | collective-permute-start | bytes 442376 | tf_op jit(solution)/shard_map/ppermute | solution.py:572
  92.0 7.9 %collective-permute-start.39 = (bf16[192,384]{1,0:T(8,128)(2,1)S(1)}, bf16[192,384]{1,0:T(8,128)(2,1)S(1)}, u32[]{:S(2)}, u32[]{:S(2)}) collective-permute-start(bf16[192,384]{1,0:T(8,128)(2,1)S(1)} %sum_chips.9.kept), channel_id=1, source_target_pairs={{0,2},{1,3},{2,0},{3,1},{4,6},{5,7},{6,4},{7,5},{8,10},{9,11},{10,... | collective-permute-start | bytes 442376 | tf_op jit(solution)/shard_map/ppermute | solution.py:572
  96.1 10.4 %collective-permute-start.42 = (bf16[2,384,384]{2,1,0:T(8,128)(2,1)S(1)}, bf16[2,384,384]{2,1,0:T(8,128)(2,1)S(1)}, u32[]{:S(2)}, u32[]{:S(2)}) collective-permute-start(bf16[2,384,384]{2,1,0:T(8,128)(2,1)S(1)} %sum_pair.2.rest_0_), channel_id=1, source_target_pairs={{0,8},{1,17},{2,10},{3,19},{4,12},{5,21},{6,14},{7,23},{8,0},{9,25... | collective-permute-start | bytes 1769480 | tf_op jit(solution)/shard_map/ppermute | solution.py:572
  97.1 7.7 %collective-permute-start.38 = (bf16[192,384]{1,0:T(8,128)(2,1)S(1)}, bf16[192,384]{1,0:T(8,128)(2,1)S(1)}, u32[]{:S(2)}, u32[]{:S(2)}) collective-permute-start(bf16[192,384]{1,0:T(8,128)(2,1)S(1)} %sum_chips.10.left), channel_id=1, source_target_pairs={{0,4},{1,5},{2,6},{3,7},{4,0},{5,1},{6,2},{7,3},{8,12},{9,13},{10,... | collective-permute-start | bytes 442376 | tf_op jit(solution)/shard_map/ppermute | solution.py:572
  99.9 12.6 %collective-permute-start.44 = (bf16[384,384]{1,0:T(8,128)(2,1)S(1)}, bf16[384,384]{1,0:T(8,128)(2,1)S(1)}, u32[]{:S(2)}, u32[]{:S(2)}) collective-permute-start(bf16[384,384]{1,0:T(8,128)(2,1)S(1)} %sum_join.4.rest_0_), channel_id=1, source_target_pairs={{0,8},{1,17},{2,10},{3,19},{4,12},{5,21},{6,14},{7,23},{8,0},{9,25... | collective-permute-start | bytes 884744 | tf_op jit(solution)/shard_map/ppermute | solution.py:572
  103.0 15.7 %collective-permute-start.51 = (bf16[2,384,384]{2,1,0:T(8,128)(2,1)S(1)}, bf16[2,384,384]{2,1,0:T(8,128)(2,1)S(1)}, u32[]{:S(2)}, u32[]{:S(2)}) collective-permute-start(bf16[2,384,384]{2,1,0:T(8,128)(2,1)S(1)} %sum_pair.2.rest_0_), channel_id=1, source_target_pairs={{0,1},{1,0},{2,3},{3,2},{4,5},{5,4},{6,7},{7,6},{8,9},{9,8},{10,11... | collective-permute-start | bytes 1769480 | tf_op jit(solution)/shard_map/ppermute | solution.py:572
  106.5 12.8 %collective-permute-start.52 = (bf16[2,384,384]{2,1,0:T(8,128)(2,1)S(1)}, bf16[2,384,384]{2,1,0:T(8,128)(2,1)S(1)}, u32[]{:S(2)}, u32[]{:S(2)}) collective-permute-start(bf16[2,384,384]{2,1,0:T(8,128)(2,1)S(1)} %gate.27.rest_1_), channel_id=1, source_target_pairs={{0,1},{1,0},{2,3},{3,2},{4,5},{5,4},{6,7},{7,6},{8,9},{9,8},{10,11... | collective-permute-start | bytes 1769480 | tf_op jit(solution)/shard_map/ppermute | solution.py:572
  107.8 9.8 %collective-permute-start.45 = (bf16[384,384]{1,0:T(8,128)(2,1)S(1)}, bf16[384,384]{1,0:T(8,128)(2,1)S(1)}, u32[]{:S(2)}, u32[]{:S(2)}) collective-permute-start(bf16[384,384]{1,0:T(8,128)(2,1)S(1)} %gate.28.rest_1_), channel_id=1, source_target_pairs={{0,8},{1,17},{2,10},{3,19},{4,12},{5,21},{6,14},{7,23},{8,0},{9,25... | collective-permute-start | bytes 884744 | tf_op jit(solution)/shard_map/ppermute | solution.py:572
  110.0 8.6 %collective-permute-start.43 = (bf16[384,384]{1,0:T(8,128)(2,1)S(1)}, bf16[384,384]{1,0:T(8,128)(2,1)S(1)}, u32[]{:S(2)}, u32[]{:S(2)}) collective-permute-start(bf16[384,384]{1,0:T(8,128)(2,1)S(1)} %sum_join.5.rest_0_), channel_id=1, source_target_pairs={{0,16},{1,9},{2,18},{3,11},{4,20},{5,13},{6,22},{7,15},{8,24},{9,1... | collective-permute-start | bytes 884744 | tf_op jit(solution)/shard_map/ppermute | solution.py:572
  112.5 11.8 %collective-permute-start.47 = (bf16[384,384]{1,0:T(8,128)(2,1)S(1)}, bf16[384,384]{1,0:T(8,128)(2,1)S(1)}, u32[]{:S(2)}, u32[]{:S(2)}) collective-permute-start(bf16[384,384]{1,0:T(8,128)(2,1)S(1)} %sum_join.4.rest_0_), channel_id=1, source_target_pairs={{0,1},{1,0},{2,3},{3,2},{4,5},{5,4},{6,7},{7,6},{8,9},{9,8},{10,11... | collective-permute-start | bytes 884744 | tf_op jit(solution)/shard_map/ppermute | solution.py:572
  119.3 8.2 %collective-permute-start.46 = (bf16[384,384]{1,0:T(8,128)(2,1)S(1)}, bf16[384,384]{1,0:T(8,128)(2,1)S(1)}, u32[]{:S(2)}, u32[]{:S(2)}) collective-permute-start(bf16[384,384]{1,0:T(8,128)(2,1)S(1)} %gate.29.rest_1_), channel_id=1, source_target_pairs={{0,8},{1,17},{2,10},{3,19},{4,12},{5,21},{6,14},{7,23},{8,0},{9,25... | collective-permute-start | bytes 884744 | tf_op jit(solution)/shard_map/ppermute | solution.py:572
  (26 other events, 138.9 us)

commit v5 on v4

--- a/solution.py
+++ b/solution.py
@@ -892,7 +892,6 @@
         h1, gains, grad_h2, held_two, actives, slopes,
     )
     two = Chunk(line, keep, send)
-    four.turn(20)
     input_grad, keep, send = line.step(
         lambda *args: call(
             first_back_kernel, "first_backward", args,
@@ -903,9 +902,10 @@
         grad_shared, third_weights, gain_grad_two, gain_grad_three, gain_grad_four,
     )
     first = Chunk(line, keep, send)
+    four.turn(20)
     two.begin(20)
+    first.begin(5)
     four.own(5)
-    first.begin(5)
     two.turn(20)
     four.along(5)
     two.own(1)

time: 132 us -> 129 us (0.977)
  waiting for transfers between devices: 41 us -> 37.3 us
    ppermute x57, waiting for transfers between devices: 41 us -> 37.3 us  [partner(): lax.ppermute(value, ('section', 'dp'), partner_pairs(sections, groups, ki...]
where the time goes in v5:
time: 129 us
  starting transfers between devices  58.3 us (45%)
  waiting for transfers between devices  37.3 us (29%)
  Pallas kernels  31.8 us (25%)
    ppermute x57, starting transfers between devices, partner(): lax.ppermute(value, ('section', 'dp'), partner_pairs(sections, groups, ki...  58.3 us
    ppermute x57, waiting for transfers between devices, partner(): lax.ppermute(value, ('section', 'dp'), partner_pairs(sections, groups, ki...  37.3 us
    pallas_call x49, Pallas kernels, call(): pl.pallas_call(body, name=name, out_shape=[places[where](shape, dtype) if...  31.8 us
  transfers between devices with their start and end apart: 57, of which 21 were waited for; matrix products, arithmetic and copies ran while one was open for 0% of the time, Pallas kernels for 22%

profile of v5, /device:TPU:0, one launch (start us, length us, event | category | flops | bytes accessed | tf_op | source)
XLA Modules:
  0.0 128.8 jit_solution(7416859426339288031)
XLA Ops:
  2.3 3.0 %collective-permute-start = (bf16[384,384]{1,0:T(8,128)(2,1)S(1)}, bf16[384,384]{1,0:T(8,128)(2,1)S(1)}, u32[]{:S(2)}, u32[]{:S(2)}) collective-permute-start(bf16[384,384]{1,0:T(8,128)(2,1)S(1)} %get-tuple-element.255), channel_id=1, source_target_pairs={{0,8},{1,17},{2,10},{3,19},{4,12},{5,21},{6,14},{7,23},{8,0},{9,25... | collective-permute-start | bytes 884744 | tf_op jit(solution)/shard_map/ppermute | solution.py:572
  7.4 5.2 %collective-permute-done.value = bf16[384,384]{1,0:T(8,128)(2,1)S(1)} collective-permute-done((bf16[384,384]{1,0:T(8,128)(2,1)S(1)}, bf16[384,384]{1,0:T(8,128)(2,1)S(1)}, u32[]{:S(2)}, u32[]{:S(2)}) %collective-permute-start) | collective-permute-done | bytes 294944 | tf_op jit(solution)/shard_map/ppermute | solution.py:572
  12.7 2.7 %collective-permute-start.2 = (bf16[384,384]{1,0:T(8,128)(2,1)S(1)}, bf16[384,384]{1,0:T(8,128)(2,1)S(1)}, u32[]{:S(2)}, u32[]{:S(2)}) collective-permute-start(bf16[384,384]{1,0:T(8,128)(2,1)S(1)} %gate.17.rest_0_), channel_id=1, source_target_pairs={{0,16},{1,9},{2,18},{3,11},{4,20},{5,13},{6,22},{7,15},{8,24},{9,1... | collective-permute-start | bytes 884744 | tf_op jit(solution)/shard_map/ppermute | solution.py:572
  15.5 3.4 %collective-permute-done.3.value = bf16[384,384]{1,0:T(8,128)(2,1)S(1)} collective-permute-done((bf16[384,384]{1,0:T(8,128)(2,1)S(1)}, bf16[384,384]{1,0:T(8,128)(2,1)S(1)}, u32[]{:S(2)}, u32[]{:S(2)}) %collective-permute-start.3) | collective-permute-done | bytes 294944 | tf_op jit(solution)/shard_map/ppermute | solution.py:572
  18.9 2.7 %collective-permute-start.7 = (bf16[384,384]{1,0:T(8,128)(2,1)S(1)}, bf16[384,384]{1,0:T(8,128)(2,1)S(1)}, u32[]{:S(2)}, u32[]{:S(2)}) collective-permute-start(bf16[384,384]{1,0:T(8,128)(2,1)S(1)} %gate.19.rest_0_), channel_id=1, source_target_pairs={{0,16},{1,9},{2,18},{3,11},{4,20},{5,13},{6,22},{7,15},{8,24},{9,1... | collective-permute-start | bytes 884744 | tf_op jit(solution)/shard_map/ppermute | solution.py:572
  21.8 1.7 %collective-permute-start.13 = (bf16[384,384]{1,0:T(8,128)(2,1)S(1)}, bf16[384,384]{1,0:T(8,128)(2,1)S(1)}, u32[]{:S(2)}, u32[]{:S(2)}) collective-permute-start(bf16[384,384]{1,0:T(8,128)(2,1)S(1)} %gate.20), channel_id=1, source_target_pairs={{0,8},{1,17},{2,10},{3,19},{4,12},{5,21},{6,14},{7,23},{8,0},{9,25... | collective-permute-start | bytes 884744 | tf_op jit(solution)/shard_map/ppermute | solution.py:572
  23.7 4.3 %collective-permute-done.7.value = bf16[384,384]{1,0:T(8,128)(2,1)S(1)} collective-permute-done((bf16[384,384]{1,0:T(8,128)(2,1)S(1)}, bf16[384,384]{1,0:T(8,128)(2,1)S(1)}, u32[]{:S(2)}, u32[]{:S(2)}) %collective-permute-start.7) | collective-permute-done | bytes 294944 | tf_op jit(solution)/shard_map/ppermute | solution.py:572
  27.9 2.5 %collective-permute-start.12 = (bf16[384,384]{1,0:T(8,128)(2,1)S(1)}, bf16[384,384]{1,0:T(8,128)(2,1)S(1)}, u32[]{:S(2)}, u32[]{:S(2)}) collective-permute-start(bf16[384,384]{1,0:T(8,128)(2,1)S(1)} %gate.20), channel_id=1, source_target_pairs={{0,16},{1,9},{2,18},{3,11},{4,20},{5,13},{6,22},{7,15},{8,24},{9,1... | collective-permute-start | bytes 884744 | tf_op jit(solution)/shard_map/ppermute | solution.py:572
  31.1 2.2 %first_forward.1 = (bf16[256,384]{1,0:T(8,128)(2,1)S(1)}, bf16[256,1152]{1,0:T(8,128)(2,1)S(1)}, bf16[256,384]{1,0:T(8,128)(2,1)S(1)}, f32[6,256,256]{2,1,0:T(8,...) custom-call(s32[8,256]{1,0:T(8,128)S(1)} %gate.16.limits, ...), custom_call_target="tpu_custom_call" | custom-call | flops 6000000000 | bytes 1 | tf_op jit(solution)/shard_map/first_forward/pallas_call | solution.py:538
  33.4 1.7 %collective-permute-done.12.value = bf16[384,384]{1,0:T(8,128)(2,1)S(1)} collective-permute-done((bf16[384,384]{1,0:T(8,128)(2,1)S(1)}, bf16[384,384]{1,0:T(8,128)(2,1)S(1)}, u32[]{:S(2)}, u32[]{:S(2)}) %collective-permute-start.12) | collective-permute-done | bytes 294944 | tf_op jit(solution)/shard_map/ppermute | solution.py:572
  35.7 4.2 %second_third_forward.1 = (bf16[256,384]{1,0:T(8,128)(2,1)S(1)}, bf16[2,4,384,384]{3,2,1,0:T(8,128)(2,1)S(1)}, bf16[256,384]{1,0:T(8,128)(2,1)S(1)}, bf16[256,11...) custom-call(s32[8,256]{1,0:T(8,128)S(1)} %gate.16.limits, ...), custom_call_target="tpu_custom_call" | custom-call | flops 3000000000 | bytes 1 | tf_op jit(solution)/shard_map/second_third_forward/pallas_call | solution.py:538
  40.3 3.6 %fourth_both.1 = (f32[256,384]{1,0:T(8,128)S(1)}, f32[256,384]{1,0:T(8,128)S(1)}, bf16[3,384,384]{2,1,0:T(8,128)(2,1)S(1)}, bf16[3,384,384]{2,1,0:T(8,128)(2,1)S(1)}, bf16[256,384]{1,0:T(8,128)(2,1)S(1)}) custom-call(s32[8,256]{1,0:T(8,128)S(1)} %gate.16.limits, bf16[256,384]{1,0:T(8,128)(2,1)S(1)} %get-tuple-element.312.h3, ...), custom_call_target="tpu_custom_call" | custom-call | flops 3000000000 | bytes 1 | tf_op jit(solution)/shard_map/fourth_both/pallas_call | solution.py:538
  46.0 2.4 %third_backward.1 = (bf16[256,384]{1,0:T(8,128)(2,1)S(1)}, bf16[2,768,384]{2,1,0:T(8,128)(2,1)S(1)}, bf16[256,192]{1,0:T(8,128)(2,1)S(1)}, f32[8,384]{1,0:T(8,128)S(1)}) custom-call(bf16[256,384]{1,0:T(8,128)(2,1)S(1)} %get-tuple-element.324.h2, f32[8,384]{1,0:T(8,128)S(1)} %get-tuple-element.361.gains, bf16[256,384]{1,0:T(8,128)(2,1)S(1)} %get-tuple-element.326.grad_h3, ...), custom_call_target="tpu_custom_call" | custom-call | flops 8000000000 | bytes 1 | tf_op jit(solution)/shard_map/third_backward/pallas_call | solution.py:538
  50.8 2.3 %second_backward.1 = (bf16[256,384]{1,0:T(8,128)(2,1)S(1)}, bf16[4,384,384]{2,1,0:T(8,128)(2,1)S(1)}, bf16[4,384,384]{2,1,0:T(8,128)(2,1)S(1)}, f32[8,384]{1,0:T(8,128)S(1)}) custom-call(bf16[256,384]{1,0:T(8,128)(2,1)S(1)} %get-tuple-element.344.h1, f32[8,384]{1,0:T(8,128)S(1)} %get-tuple-element.361.gains, ...), custom_call_target="tpu_custom_call" | custom-call | flops 20000000000 | bytes 1 | tf_op jit(solution)/shard_map/second_backward/pallas_call | solution.py:538
  53.1 3.4 %first_backward.1 = (f32[256,384]{1,0:T(8,128)}, bf16[4,384,384]{2,1,0:T(8,128)(2,1)S(1)}, bf16[4,384,384]{2,1,0:T(8,128)(2,1)S(1)}) custom-call(bf16[256,384]{1,0:T(8,128)(2,1)S(1)} %copy-done, f32[8,384]{1,0:T(8,128)S(1)} %get-tuple-element.361.gains, bf16[256,384]{1,0:T(8,128)(2,1)S(1)} %get-tuple-element.362.grad_h1, ...), custom_call_target="tpu_custom_call" | custom-call | flops 8000000000 | bytes 1 | tf_op jit(solution)/shard_map/first_backward/pallas_call | solution.py:538
  56.7 1.9 %collective-permute-start.26 = (bf16[384,384]{1,0:T(8,128)(2,1)S(1)}, bf16[384,384]{1,0:T(8,128)(2,1)S(1)}, u32[]{:S(2)}, u32[]{:S(2)}) collective-permute-start(bf16[384,384]{1,0:T(8,128)(2,1)S(1)} %sum_turn.3), channel_id=1, source_target_pairs={{0,16},{1,9},{2,18},{3,11},{4,20},{5,13},{6,22},{7,15},{8,24},{9,1... | collective-permute-start | bytes 884744 | tf_op jit(solution)/shard_map/ppermute | solution.py:572
  66.5 1.9 %collective-permute-start.31 = (bf16[384,384]{1,0:T(8,128)(2,1)S(1)}, bf16[384,384]{1,0:T(8,128)(2,1)S(1)}, u32[]{:S(2)}, u32[]{:S(2)}) collective-permute-start(bf16[384,384]{1,0:T(8,128)(2,1)S(1)} %sum_turn.4), channel_id=1, source_target_pairs={{0,16},{1,9},{2,18},{3,11},{4,20},{5,13},{6,22},{7,15},{8,24},{9,1... | collective-permute-start | bytes 884744 | tf_op jit(solution)/shard_map/ppermute | solution.py:572
  70.0 2.6 %collective-permute-start.29 = (bf16[192,384]{1,0:T(8,128)(2,1)S(1)}, bf16[192,384]{1,0:T(8,128)(2,1)S(1)}, u32[]{:S(2)}, u32[]{:S(2)}) collective-permute-start(bf16[192,384]{1,0:T(8,128)(2,1)S(1)} %sum_chips.6.left), channel_id=1, source_target_pairs={{0,4},{1,5},{2,6},{3,7},{4,0},{5,1},{6,2},{7,3},{8,12},{9,13},{10,... | collective-permute-start | bytes 442376 | tf_op jit(solution)/shard_map/ppermute | solution.py:572
  74.9 1.6 %collective-permute-start.34 = (bf16[192,384]{1,0:T(8,128)(2,1)S(1)}, bf16[192,384]{1,0:T(8,128)(2,1)S(1)}, u32[]{:S(2)}, u32[]{:S(2)}) collective-permute-start(bf16[192,384]{1,0:T(8,128)(2,1)S(1)} %get-tuple-element.404), channel_id=1, source_target_pairs={{0,2},{1,3},{2,0},{3,1},{4,6},{5,7},{6,4},{7,5},{8,10},{9,11},{10,... | collective-permute-start | bytes 442376 | tf_op jit(solution)/shard_map/ppermute | solution.py:572
  79.4 2.0 %collective-permute-start.32 = (bf16[384,384]{1,0:T(8,128)(2,1)S(1)}, bf16[384,384]{1,0:T(8,128)(2,1)S(1)}, u32[]{:S(2)}, u32[]{:S(2)}) collective-permute-start(bf16[384,384]{1,0:T(8,128)(2,1)S(1)} %sum_turn.5), channel_id=1, source_target_pairs={{0,16},{1,9},{2,18},{3,11},{4,20},{5,13},{6,22},{7,15},{8,24},{9,1... | collective-permute-start | bytes 884744 | tf_op jit(solution)/shard_map/ppermute | solution.py:572
  81.4 3.9 %collective-permute-start.37 = (bf16[192,384]{1,0:T(8,128)(2,1)S(1)}, bf16[192,384]{1,0:T(8,128)(2,1)S(1)}, u32[]{:S(2)}, u32[]{:S(2)}) collective-permute-start(bf16[192,384]{1,0:T(8,128)(2,1)S(1)} %sum_chips.8.left), channel_id=1, source_target_pairs={{0,4},{1,5},{2,6},{3,7},{4,0},{5,1},{6,2},{7,3},{8,12},{9,13},{10,... | collective-permute-start | bytes 442376 | tf_op jit(solution)/shard_map/ppermute | solution.py:572
  85.4 1.7 %collective-permute-start.36 = (bf16[384,384]{1,0:T(8,128)(2,1)S(1)}, bf16[384,384]{1,0:T(8,128)(2,1)S(1)}, u32[]{:S(2)}, u32[]{:S(2)}) collective-permute-start(bf16[384,384]{1,0:T(8,128)(2,1)S(1)} %sum_join.3.left), channel_id=1, source_target_pairs={{0,16},{1,9},{2,18},{3,11},{4,20},{5,13},{6,22},{7,15},{8,24},{9,1... | collective-permute-start | bytes 884744 | tf_op jit(solution)/shard_map/ppermute | solution.py:572
  94.3 3.3 %collective-permute-start.38 = (bf16[192,384]{1,0:T(8,128)(2,1)S(1)}, bf16[192,384]{1,0:T(8,128)(2,1)S(1)}, u32[]{:S(2)}, u32[]{:S(2)}) collective-permute-start(bf16[192,384]{1,0:T(8,128)(2,1)S(1)} %sum_chips.10.left), channel_id=1, source_target_pairs={{0,4},{1,5},{2,6},{3,7},{4,0},{5,1},{6,2},{7,3},{8,12},{9,13},{10,... | collective-permute-start | bytes 442376 | tf_op jit(solution)/shard_map/ppermute | solution.py:572
  98.7 2.1 %collective-permute-start.41 = (bf16[384,384]{1,0:T(8,128)(2,1)S(1)}, bf16[384,384]{1,0:T(8,128)(2,1)S(1)}, u32[]{:S(2)}, u32[]{:S(2)}) collective-permute-start(bf16[384,384]{1,0:T(8,128)(2,1)S(1)} %sum_join.4.rest_0_), channel_id=1, source_target_pairs={{0,16},{1,9},{2,18},{3,11},{4,20},{5,13},{6,22},{7,15},{8,24},{9,1... | collective-permute-start | bytes 884744 | tf_op jit(solution)/shard_map/ppermute | solution.py:572
  102.4 3.2 %collective-permute-done.42.value = bf16[2,384,384]{2,1,0:T(8,128)(2,1)S(1)} collective-permute-done((bf16[2,384,384]{2,1,0:T(8,128)(2,1)S(1)}, bf16[2,384,384]{2,1,0:T(8,128)(2,1)S(1)}, u32[]{:S(2)}, u32[]{:S(2)}) %collective-permute-start.42) | collective-permute-done | bytes 589856 | tf_op jit(solution)/shard_map/ppermute | solution.py:572
  107.6 2.4 %collective-permute-start.43 = (bf16[384,384]{1,0:T(8,128)(2,1)S(1)}, bf16[384,384]{1,0:T(8,128)(2,1)S(1)}, u32[]{:S(2)}, u32[]{:S(2)}) collective-permute-start(bf16[384,384]{1,0:T(8,128)(2,1)S(1)} %sum_join.5.rest_0_), channel_id=1, source_target_pairs={{0,16},{1,9},{2,18},{3,11},{4,20},{5,13},{6,22},{7,15},{8,24},{9,1... | collective-permute-start | bytes 884744 | tf_op jit(solution)/shard_map/ppermute | solution.py:572
  110.0 4.8 %collective-permute-done.45.right = bf16[384,384]{1,0:T(8,128)(2,1)S(1)} collective-permute-done((bf16[384,384]{1,0:T(8,128)(2,1)S(1)}, bf16[384,384]{1,0:T(8,128)(2,1)S(1)}, u32[]{:S(2)}, u32[]{:S(2)}) %collective-permute-start.45) | collective-permute-done | bytes 294944 | tf_op jit(solution)/shard_map/ppermute | solution.py:572
  117.6 2.3 %unpack_four.1 = (f32[384,1536]{1,0:T(8,128)}, f32[1536,384]{1,0:T(8,128)}) custom-call(bf16[2,384,384]{2,1,0:T(8,128)(2,1)S(1)} %sum_pair.2.rest_0_, bf16[2,384,384]{2,1,0:T(8,128)(2,1)S(1)} %gate.27.rest_1_, bf16[2,384,384]{2,1,0:T(8,128)(2,1)S(1)} %collective-permute-done.51.rest_2_, bf16[2,384,384]{2,1,0:T(8,128)(2,1)S(1)} %collective-permute-done.52.rest_3_), custom_call_target="tpu_custom_call" | custom-call | flops 3000000000 | bytes 1 | tf_op jit(solution)/shard_map/unpack_four/pallas_call | solution.py:538
  119.9 1.7 %collective-permute-done.50.value = bf16[384,384]{1,0:T(8,128)(2,1)S(1)} collective-permute-done((bf16[384,384]{1,0:T(8,128)(2,1)S(1)}, bf16[384,384]{1,0:T(8,128)(2,1)S(1)}, u32[]{:S(2)}, u32[]{:S(2)}) %collective-permute-start.50) | collective-permute-done | bytes 294944 | tf_op jit(solution)/shard_map/ppermute | solution.py:572
  122.2 2.3 %unpack_two.1 = (f32[384,1536]{1,0:T(8,128)}, f32[1536,384]{1,0:T(8,128)}) custom-call(bf16[384,384]{1,0:T(8,128)(2,1)S(1)} %sum_join.4.rest_0_, bf16[384,384]{1,0:T(8,128)(2,1)S(1)} %gate.28.rest_1_, bf16[2,384,384]{2,1,0:T(8,128)(2,1)S(1)} %sum_pair.3.rest_2_, bf16[384,384]{1,0:T(8,128)(2,1)S(1)} %collective-permute-done.47.rest_3_, ...), custom_call_target="tpu_custom_call" | custom-call | flops 1000000000 | bytes 1 | tf_op jit(solution)/shard_map/unpack_two/pallas_call | solution.py:538
  125.1 1.8 %unpack_some.1 = (f32[384,1152]{1,0:T(8,128)}, f32[384,384]{1,0:T(8,128)}, f32[384,768]{1,0:T(8,128)}, f32[192,384]{1,0:T(8,128)}, f32[384,384]{1,0:T(8,128)}, /...) custom-call(bf16[384,384]{1,0:T(8,128)(2,1)S(1)} %sum_join.5.rest_0_, ...), custom_call_target="tpu_custom_call" | custom-call | flops 3000000000 | bytes 1 | tf_op jit(solution)/shard_map/unpack_some/pallas_call | solution.py:538
  126.9 1.7 %unpack_rest.1 = (f32[384,1152]{1,0:T(8,128)}, f32[384,384]{1,0:T(8,128)}, f32[384,768]{1,0:T(8,128)}, f32[192,384]{1,0:T(8,128)}, f32[384,384]{1,0:T(8,128)}, /...) custom-call(bf16[384,384]{1,0:T(8,128)(2,1)S(1)} %gate.31.rest_0_, ...), custom_call_target="tpu_custom_call", output_to_operand_aliasing={{0}: (2, {}), {1}: (3, {}), {2}: (4, {}), {3}: (5, {}), {4}... | custom-call | flops 4000000000 | bytes 1 | tf_op jit(solution)/shard_map/unpack_rest/pallas_call | solution.py:538
  (133 shorter events, 41.1 us)
Async XLA Ops:
  2.3 10.3 %collective-permute-start = (bf16[384,384]{1,0:T(8,128)(2,1)S(1)}, bf16[384,384]{1,0:T(8,128)(2,1)S(1)}, u32[]{:S(2)}, u32[]{:S(2)}) collective-permute-start(bf16[384,384]{1,0:T(8,128)(2,1)S(1)} %get-tuple-element.255), channel_id=1, source_target_pairs={{0,8},{1,17},{2,10},{3,19},{4,12},{5,21},{6,14},{7,23},{8,0},{9,25... | collective-permute-start | bytes 884744 | tf_op jit(solution)/shard_map/ppermute | solution.py:572
  5.3 10.1 %collective-permute-start.1 = (bf16[384,384]{1,0:T(8,128)(2,1)S(1)}, bf16[384,384]{1,0:T(8,128)(2,1)S(1)}, u32[]{:S(2)}, u32[]{:S(2)}) collective-permute-start(bf16[384,384]{1,0:T(8,128)(2,1)S(1)} %get-tuple-element.255), channel_id=1, source_target_pairs={{0,16},{1,9},{2,18},{3,11},{4,20},{5,13},{6,22},{7,15},{8,24},{9,1... | collective-permute-start | bytes 884744 | tf_op jit(solution)/shard_map/ppermute | solution.py:572
  6.8 16.7 %collective-permute-start.8 = (bf16[384,384]{1,0:T(8,128)(2,1)S(1)}, bf16[384,384]{1,0:T(8,128)(2,1)S(1)}, u32[]{:S(2)}, u32[]{:S(2)}) collective-permute-start(bf16[384,384]{1,0:T(8,128)(2,1)S(1)} %get-tuple-element.259), channel_id=1, source_target_pairs={{0,16},{1,9},{2,18},{3,11},{4,20},{5,13},{6,22},{7,15},{8,24},{9,1... | collective-permute-start | bytes 884744 | tf_op jit(solution)/shard_map/ppermute | solution.py:572
  7.3 11.6 %collective-permute-start.3 = (bf16[384,384]{1,0:T(8,128)(2,1)S(1)}, bf16[384,384]{1,0:T(8,128)(2,1)S(1)}, u32[]{:S(2)}, u32[]{:S(2)}) collective-permute-start(bf16[384,384]{1,0:T(8,128)(2,1)S(1)} %get-tuple-element.259), channel_id=1, source_target_pairs={{0,8},{1,17},{2,10},{3,19},{4,12},{5,21},{6,14},{7,23},{8,0},{9,25... | collective-permute-start | bytes 884744 | tf_op jit(solution)/shard_map/ppermute | solution.py:572
  12.6 17.9 %collective-permute-start.4 = (bf16[384,384]{1,0:T(8,128)(2,1)S(1)}, bf16[384,384]{1,0:T(8,128)(2,1)S(1)}, u32[]{:S(2)}, u32[]{:S(2)}) collective-permute-start(bf16[384,384]{1,0:T(8,128)(2,1)S(1)} %gate.17.rest_0_), channel_id=1, source_target_pairs={{0,1},{1,0},{2,3},{3,2},{4,5},{5,4},{6,7},{7,6},{8,9},{9,8},{10,11... | collective-permute-start | bytes 884744 | tf_op jit(solution)/shard_map/ppermute | solution.py:572
  12.7 9.1 %collective-permute-start.2 = (bf16[384,384]{1,0:T(8,128)(2,1)S(1)}, bf16[384,384]{1,0:T(8,128)(2,1)S(1)}, u32[]{:S(2)}, u32[]{:S(2)}) collective-permute-start(bf16[384,384]{1,0:T(8,128)(2,1)S(1)} %gate.17.rest_0_), channel_id=1, source_target_pairs={{0,16},{1,9},{2,18},{3,11},{4,20},{5,13},{6,22},{7,15},{8,24},{9,1... | collective-permute-start | bytes 884744 | tf_op jit(solution)/shard_map/ppermute | solution.py:572
  15.4 15.0 %collective-permute-start.5 = (bf16[384,384]{1,0:T(8,128)(2,1)S(1)}, bf16[384,384]{1,0:T(8,128)(2,1)S(1)}, u32[]{:S(2)}, u32[]{:S(2)}) collective-permute-start(bf16[384,384]{1,0:T(8,128)(2,1)S(1)} %gate.18.rest_1_), channel_id=1, source_target_pairs={{0,1},{1,0},{2,3},{3,2},{4,5},{5,4},{6,7},{7,6},{8,9},{9,8},{10,11... | collective-permute-start | bytes 884744 | tf_op jit(solution)/shard_map/ppermute | solution.py:572
  18.9 9.0 %collective-permute-start.7 = (bf16[384,384]{1,0:T(8,128)(2,1)S(1)}, bf16[384,384]{1,0:T(8,128)(2,1)S(1)}, u32[]{:S(2)}, u32[]{:S(2)}) collective-permute-start(bf16[384,384]{1,0:T(8,128)(2,1)S(1)} %gate.19.rest_0_), channel_id=1, source_target_pairs={{0,16},{1,9},{2,18},{3,11},{4,20},{5,13},{6,22},{7,15},{8,24},{9,1... | collective-permute-start | bytes 884744 | tf_op jit(solution)/shard_map/ppermute | solution.py:572
  21.8 11.5 %collective-permute-start.13 = (bf16[384,384]{1,0:T(8,128)(2,1)S(1)}, bf16[384,384]{1,0:T(8,128)(2,1)S(1)}, u32[]{:S(2)}, u32[]{:S(2)}) collective-permute-start(bf16[384,384]{1,0:T(8,128)(2,1)S(1)} %gate.20), channel_id=1, source_target_pairs={{0,8},{1,17},{2,10},{3,19},{4,12},{5,21},{6,14},{7,23},{8,0},{9,25... | collective-permute-start | bytes 884744 | tf_op jit(solution)/shard_map/ppermute | solution.py:572
  23.5 7.5 %collective-permute-start.6 = (bf16[384,384]{1,0:T(8,128)(2,1)S(1)}, bf16[384,384]{1,0:T(8,128)(2,1)S(1)}, u32[]{:S(2)}, u32[]{:S(2)}) collective-permute-start(bf16[384,384]{1,0:T(8,128)(2,1)S(1)} %gate.21.rest_2_), channel_id=1, source_target_pairs={{0,1},{1,0},{2,3},{3,2},{4,5},{5,4},{6,7},{7,6},{8,9},{9,8},{10,11... | collective-permute-start | bytes 884744 | tf_op jit(solution)/shard_map/ppermute | solution.py:572
  27.9 7.2 %collective-permute-start.12 = (bf16[384,384]{1,0:T(8,128)(2,1)S(1)}, bf16[384,384]{1,0:T(8,128)(2,1)S(1)}, u32[]{:S(2)}, u32[]{:S(2)}) collective-permute-start(bf16[384,384]{1,0:T(8,128)(2,1)S(1)} %gate.20), channel_id=1, source_target_pairs={{0,16},{1,9},{2,18},{3,11},{4,20},{5,13},{6,22},{7,15},{8,24},{9,1... | collective-permute-start | bytes 884744 | tf_op jit(solution)/shard_map/ppermute | solution.py:572
  48.5 8.0 %collective-permute-start.22 = (bf16[384,384]{1,0:T(8,128)(2,1)S(1)}, bf16[384,384]{1,0:T(8,128)(2,1)S(1)}, u32[]{:S(2)}, u32[]{:S(2)}) collective-permute-start(bf16[384,384]{1,0:T(8,128)(2,1)S(1)} %sum_both.1), channel_id=1, source_target_pairs={{0,8},{1,17},{2,10},{3,19},{4,12},{5,21},{6,14},{7,23},{8,0},{9,25... | collective-permute-start | bytes 884744 | tf_op jit(solution)/shard_map/ppermute | solution.py:572
  50.1 14.3 %collective-permute-start.25 = (bf16[384,384]{1,0:T(8,128)(2,1)S(1)}, bf16[384,384]{1,0:T(8,128)(2,1)S(1)}, u32[]{:S(2)}, u32[]{:S(2)}) collective-permute-start(bf16[384,384]{1,0:T(8,128)(2,1)S(1)} %sum_near.1), channel_id=1, source_target_pairs={{0,8},{1,17},{2,10},{3,19},{4,12},{5,21},{6,14},{7,23},{8,0},{9,25... | collective-permute-start | bytes 884744 | tf_op jit(solution)/shard_map/ppermute | solution.py:572
  56.7 7.8 %collective-permute-start.26 = (bf16[384,384]{1,0:T(8,128)(2,1)S(1)}, bf16[384,384]{1,0:T(8,128)(2,1)S(1)}, u32[]{:S(2)}, u32[]{:S(2)}) collective-permute-start(bf16[384,384]{1,0:T(8,128)(2,1)S(1)} %sum_turn.3), channel_id=1, source_target_pairs={{0,16},{1,9},{2,18},{3,11},{4,20},{5,13},{6,22},{7,15},{8,24},{9,1... | collective-permute-start | bytes 884744 | tf_op jit(solution)/shard_map/ppermute | solution.py:572
  61.4 13.2 %collective-permute-start.30 = (bf16[384,384]{1,0:T(8,128)(2,1)S(1)}, bf16[384,384]{1,0:T(8,128)(2,1)S(1)}, u32[]{:S(2)}, u32[]{:S(2)}) collective-permute-start(bf16[384,384]{1,0:T(8,128)(2,1)S(1)} %get-tuple-element.399), channel_id=1, source_target_pairs={{0,8},{1,17},{2,10},{3,19},{4,12},{5,21},{6,14},{7,23},{8,0},{9,25... | collective-permute-start | bytes 884744 | tf_op jit(solution)/shard_map/ppermute | solution.py:572
  66.5 8.2 %collective-permute-start.31 = (bf16[384,384]{1,0:T(8,128)(2,1)S(1)}, bf16[384,384]{1,0:T(8,128)(2,1)S(1)}, u32[]{:S(2)}, u32[]{:S(2)}) collective-permute-start(bf16[384,384]{1,0:T(8,128)(2,1)S(1)} %sum_turn.4), channel_id=1, source_target_pairs={{0,16},{1,9},{2,18},{3,11},{4,20},{5,13},{6,22},{7,15},{8,24},{9,1... | collective-permute-start | bytes 884744 | tf_op jit(solution)/shard_map/ppermute | solution.py:572
  70.0 8.1 %collective-permute-start.29 = (bf16[192,384]{1,0:T(8,128)(2,1)S(1)}, bf16[192,384]{1,0:T(8,128)(2,1)S(1)}, u32[]{:S(2)}, u32[]{:S(2)}) collective-permute-start(bf16[192,384]{1,0:T(8,128)(2,1)S(1)} %sum_chips.6.left), channel_id=1, source_target_pairs={{0,4},{1,5},{2,6},{3,7},{4,0},{5,1},{6,2},{7,3},{8,12},{9,13},{10,... | collective-permute-start | bytes 442376 | tf_op jit(solution)/shard_map/ppermute | solution.py:572
  74.1 13.0 %collective-permute-start.23 = (bf16[384,384]{1,0:T(8,128)(2,1)S(1)}, bf16[384,384]{1,0:T(8,128)(2,1)S(1)}, u32[]{:S(2)}, u32[]{:S(2)}) collective-permute-start(bf16[384,384]{1,0:T(8,128)(2,1)S(1)} %get-tuple-element.386), channel_id=1, source_target_pairs={{0,8},{1,17},{2,10},{3,19},{4,12},{5,21},{6,14},{7,23},{8,0},{9,25... | collective-permute-start | bytes 884744 | tf_op jit(solution)/shard_map/ppermute | solution.py:572
  78.1 7.2 %collective-permute-start.33 = (bf16[192,384]{1,0:T(8,128)(2,1)S(1)}, bf16[192,384]{1,0:T(8,128)(2,1)S(1)}, u32[]{:S(2)}, u32[]{:S(2)}) collective-permute-start(bf16[192,384]{1,0:T(8,128)(2,1)S(1)} %sum_chips.7.kept), channel_id=1, source_target_pairs={{0,2},{1,3},{2,0},{3,1},{4,6},{5,7},{6,4},{7,5},{8,10},{9,11},{10,... | collective-permute-start | bytes 442376 | tf_op jit(solution)/shard_map/ppermute | solution.py:572
  79.4 7.7 %collective-permute-start.32 = (bf16[384,384]{1,0:T(8,128)(2,1)S(1)}, bf16[384,384]{1,0:T(8,128)(2,1)S(1)}, u32[]{:S(2)}, u32[]{:S(2)}) collective-permute-start(bf16[384,384]{1,0:T(8,128)(2,1)S(1)} %sum_turn.5), channel_id=1, source_target_pairs={{0,16},{1,9},{2,18},{3,11},{4,20},{5,13},{6,22},{7,15},{8,24},{9,1... | collective-permute-start | bytes 884744 | tf_op jit(solution)/shard_map/ppermute | solution.py:572
  81.4 8.9 %collective-permute-start.37 = (bf16[192,384]{1,0:T(8,128)(2,1)S(1)}, bf16[192,384]{1,0:T(8,128)(2,1)S(1)}, u32[]{:S(2)}, u32[]{:S(2)}) collective-permute-start(bf16[192,384]{1,0:T(8,128)(2,1)S(1)} %sum_chips.8.left), channel_id=1, source_target_pairs={{0,4},{1,5},{2,6},{3,7},{4,0},{5,1},{6,2},{7,3},{8,12},{9,13},{10,... | collective-permute-start | bytes 442376 | tf_op jit(solution)/shard_map/ppermute | solution.py:572
  85.4 7.1 %collective-permute-start.36 = (bf16[384,384]{1,0:T(8,128)(2,1)S(1)}, bf16[384,384]{1,0:T(8,128)(2,1)S(1)}, u32[]{:S(2)}, u32[]{:S(2)}) collective-permute-start(bf16[384,384]{1,0:T(8,128)(2,1)S(1)} %sum_join.3.left), channel_id=1, source_target_pairs={{0,16},{1,9},{2,18},{3,11},{4,20},{5,13},{6,22},{7,15},{8,24},{9,1... | collective-permute-start | bytes 884744 | tf_op jit(solution)/shard_map/ppermute | solution.py:572
  90.4 7.2 %collective-permute-start.39 = (bf16[192,384]{1,0:T(8,128)(2,1)S(1)}, bf16[192,384]{1,0:T(8,128)(2,1)S(1)}, u32[]{:S(2)}, u32[]{:S(2)}) collective-permute-start(bf16[192,384]{1,0:T(8,128)(2,1)S(1)} %sum_chips.9.kept), channel_id=1, source_target_pairs={{0,2},{1,3},{2,0},{3,1},{4,6},{5,7},{6,4},{7,5},{8,10},{9,11},{10,... | collective-permute-start | bytes 442376 | tf_op jit(solution)/shard_map/ppermute | solution.py:572
  92.5 13.1 %collective-permute-start.42 = (bf16[2,384,384]{2,1,0:T(8,128)(2,1)S(1)}, bf16[2,384,384]{2,1,0:T(8,128)(2,1)S(1)}, u32[]{:S(2)}, u32[]{:S(2)}) collective-permute-start(bf16[2,384,384]{2,1,0:T(8,128)(2,1)S(1)} %sum_pair.2.rest_0_), channel_id=1, source_target_pairs={{0,8},{1,17},{2,10},{3,19},{4,12},{5,21},{6,14},{7,23},{8,0},{9,25... | collective-permute-start | bytes 1769480 | tf_op jit(solution)/shard_map/ppermute | solution.py:572
  94.3 8.0 %collective-permute-start.38 = (bf16[192,384]{1,0:T(8,128)(2,1)S(1)}, bf16[192,384]{1,0:T(8,128)(2,1)S(1)}, u32[]{:S(2)}, u32[]{:S(2)}) collective-permute-start(bf16[192,384]{1,0:T(8,128)(2,1)S(1)} %sum_chips.10.left), channel_id=1, source_target_pairs={{0,4},{1,5},{2,6},{3,7},{4,0},{5,1},{6,2},{7,3},{8,12},{9,13},{10,... | collective-permute-start | bytes 442376 | tf_op jit(solution)/shard_map/ppermute | solution.py:572
  97.6 12.4 %collective-permute-start.44 = (bf16[384,384]{1,0:T(8,128)(2,1)S(1)}, bf16[384,384]{1,0:T(8,128)(2,1)S(1)}, u32[]{:S(2)}, u32[]{:S(2)}) collective-permute-start(bf16[384,384]{1,0:T(8,128)(2,1)S(1)} %sum_join.4.rest_0_), channel_id=1, source_target_pairs={{0,8},{1,17},{2,10},{3,19},{4,12},{5,21},{6,14},{7,23},{8,0},{9,25... | collective-permute-start | bytes 884744 | tf_op jit(solution)/shard_map/ppermute | solution.py:572
  100.8 15.6 %collective-permute-start.51 = (bf16[2,384,384]{2,1,0:T(8,128)(2,1)S(1)}, bf16[2,384,384]{2,1,0:T(8,128)(2,1)S(1)}, u32[]{:S(2)}, u32[]{:S(2)}) collective-permute-start(bf16[2,384,384]{2,1,0:T(8,128)(2,1)S(1)} %sum_pair.2.rest_0_), channel_id=1, source_target_pairs={{0,1},{1,0},{2,3},{3,2},{4,5},{5,4},{6,7},{7,6},{8,9},{9,8},{10,11... | collective-permute-start | bytes 1769480 | tf_op jit(solution)/shard_map/ppermute | solution.py:572
  105.7 11.2 %collective-permute-start.52 = (bf16[2,384,384]{2,1,0:T(8,128)(2,1)S(1)}, bf16[2,384,384]{2,1,0:T(8,128)(2,1)S(1)}, u32[]{:S(2)}, u32[]{:S(2)}) collective-permute-start(bf16[2,384,384]{2,1,0:T(8,128)(2,1)S(1)} %gate.27.rest_1_), channel_id=1, source_target_pairs={{0,1},{1,0},{2,3},{3,2},{4,5},{5,4},{6,7},{7,6},{8,9},{9,8},{10,11... | collective-permute-start | bytes 1769480 | tf_op jit(solution)/shard_map/ppermute | solution.py:572
  105.8 9.0 %collective-permute-start.45 = (bf16[384,384]{1,0:T(8,128)(2,1)S(1)}, bf16[384,384]{1,0:T(8,128)(2,1)S(1)}, u32[]{:S(2)}, u32[]{:S(2)}) collective-permute-start(bf16[384,384]{1,0:T(8,128)(2,1)S(1)} %gate.28.rest_1_), channel_id=1, source_target_pairs={{0,8},{1,17},{2,10},{3,19},{4,12},{5,21},{6,14},{7,23},{8,0},{9,25... | collective-permute-start | bytes 884744 | tf_op jit(solution)/shard_map/ppermute | solution.py:572
  107.6 8.6 %collective-permute-start.43 = (bf16[384,384]{1,0:T(8,128)(2,1)S(1)}, bf16[384,384]{1,0:T(8,128)(2,1)S(1)}, u32[]{:S(2)}, u32[]{:S(2)}) collective-permute-start(bf16[384,384]{1,0:T(8,128)(2,1)S(1)} %sum_join.5.rest_0_), channel_id=1, source_target_pairs={{0,16},{1,9},{2,18},{3,11},{4,20},{5,13},{6,22},{7,15},{8,24},{9,1... | collective-permute-start | bytes 884744 | tf_op jit(solution)/shard_map/ppermute | solution.py:572
  110.0 11.5 %collective-permute-start.47 = (bf16[384,384]{1,0:T(8,128)(2,1)S(1)}, bf16[384,384]{1,0:T(8,128)(2,1)S(1)}, u32[]{:S(2)}, u32[]{:S(2)}) collective-permute-start(bf16[384,384]{1,0:T(8,128)(2,1)S(1)} %sum_join.4.rest_0_), channel_id=1, source_target_pairs={{0,1},{1,0},{2,3},{3,2},{4,5},{5,4},{6,7},{7,6},{8,9},{9,8},{10,11... | collective-permute-start | bytes 884744 | tf_op jit(solution)/shard_map/ppermute | solution.py:572
  116.9 7.8 %collective-permute-start.46 = (bf16[384,384]{1,0:T(8,128)(2,1)S(1)}, bf16[384,384]{1,0:T(8,128)(2,1)S(1)}, u32[]{:S(2)}, u32[]{:S(2)}) collective-permute-start(bf16[384,384]{1,0:T(8,128)(2,1)S(1)} %gate.29.rest_1_), channel_id=1, source_target_pairs={{0,8},{1,17},{2,10},{3,19},{4,12},{5,21},{6,14},{7,23},{8,0},{9,25... | collective-permute-start | bytes 884744 | tf_op jit(solution)/shard_map/ppermute | solution.py:572
  (26 other events, 132.8 us)

commit v6 on v5

--- a/solution.py
+++ b/solution.py
@@ -295,7 +295,7 @@
 
 
 def fourth_kernel(limits, h3, gains, cotangent, own0, own1, near, far, other_near, other_far, *rest):
-    total, grad_normed, keep, send, seed, held, brought, sems = rest
+    total, grad_normed, keep, send, seed, held, brought, upwards, actives, slopes, sems = rest
     seeding = pltpu.make_async_copy(cotangent, brought, sems.at[2])
     seeding.start()
     copies = bring(own0, own1, held, sems)
@@ -304,28 +304,30 @@
     normed = (scaled * gains[3:4, :]).astype(bf16)
     normed_across = normed.T
     first = place()[1] == 0
+    held[0, 1] = jnp.where(first, near[...], other_near[...])
+    held[1, 1] = jnp.where(first, other_far[...], far[...])
+    held[0, 2] = jnp.where(first, far[...], other_far[...])
+    held[1, 2] = jnp.where(first, other_near[...], near[...])
+    for rank in (1, 2):
+        upwards[rank] = nn(normed, held[0, rank])
+    for copy in copies:
+        copy.wait()
+    upwards[0] = nn(normed, held[0, 0])
+    seeding.wait()
+    row = lax.broadcasted_iota(jnp.int32, hidden.shape, 0)
+    grad_out = jnp.where(row < limits[0:1, :1], brought[...], 0)
+    seed[...] = grad_out
+    for rank in (1, 2, 0):
+        actives[rank], slopes[rank] = feed_parts(upwards[rank])
+    for rank in (1, 2, 0):
+        upwards[rank] = nt(grad_out, held[1, rank]) * slopes[rank]
     after, grads = hidden, jnp.zeros(hidden.shape, f32)
     for rank in (1, 2, 0):
-        if rank == 1:
-            up = jnp.where(first, near[...], other_near[...])
-            down = jnp.where(first, other_far[...], far[...])
-        elif rank == 2:
-            up = jnp.where(first, far[...], other_far[...])
-            down = jnp.where(first, other_near[...], near[...])
-        else:
-            for copy in copies:
-                copy.wait()
-            up, down = held[0, 0], held[1, 0]
-        active, slope = feed_parts(nn(normed, up))
-        after += nn(active, down)
-        if rank == 1:
-            seeding.wait()
-            row = lax.broadcasted_iota(jnp.int32, hidden.shape, 0)
-            grad_out = jnp.where(row < limits[0:1, :1], brought[...], 0)
-            seed[...] = grad_out
-        grad_up, grad_down, grad = quarter_back(up, down, normed_across, grad_out, active, slope)
-        put(keep, send, rank, grad_up, grad_down)
-        grads += grad
+        grad_upward = upwards[rank].astype(bf16)
+        grad_down = nn(actives[rank].T, grad_out).astype(bf16)
+        put(keep, send, rank, nn(normed_across, grad_upward).astype(bf16), grad_down)
+        grads += nt(grad_upward, held[0, rank])
+        after += nn(actives[rank], held[1, rank])
     total[...] = after
     grad_normed[...] = grads
 
@@ -858,7 +860,8 @@
             fourth_kernel, "fourth_both", args,
             [(row, f32, "vmem"), (row, f32, "vmem"), (three_quarters, bf16, "vmem"),
              (three_quarters, bf16, "vmem"), (row, bf16, "vmem")],
-            [VMEM((2, 1, D, D), bf16), VMEM(row, bf16), pltpu.SemaphoreType.DMA((3,))],
+            [VMEM((2, QUARTERS - 1, D, D), bf16), VMEM(row, bf16), VMEM((QUARTERS - 1,) + row, f32),
+             VMEM((QUARTERS - 1,) + row, bf16), VMEM((QUARTERS - 1,) + row, f32), pltpu.SemaphoreType.DMA((3,))],
             {3: HBM, 4: HBM, 5: HBM}, hint=3,
         ),
         limits, h3, gains, cotangent, up_four, down_four,

time: 129 us -> 129 us (level)
  no operation moved by 1% of the time
where the time goes in v6:
time: 129 us
  starting transfers between devices  58.2 us (45%)
  waiting for transfers between devices  37.4 us (29%)
  Pallas kernels  31.9 us (25%)
    ppermute x57, starting transfers between devices, partner(): lax.ppermute(value, ('section', 'dp'), partner_pairs(sections, groups, ki...  58.2 us
    ppermute x57, waiting for transfers between devices, partner(): lax.ppermute(value, ('section', 'dp'), partner_pairs(sections, groups, ki...  37.4 us
    pallas_call x49, Pallas kernels, call(): pl.pallas_call(body, name=name, out_shape=[places[where](shape, dtype) if...  31.9 us
  transfers between devices with their start and end apart: 57, of which 21 were waited for; matrix products, arithmetic and copies ran while one was open for 0% of the time, Pallas kernels for 22%

profile of v6, /device:TPU:0, one launch (start us, length us, event | category | flops | bytes accessed | tf_op | source)
XLA Modules:
  0.0 128.8 jit_solution(13973086272861406033)
XLA Ops:
  2.3 3.0 %collective-permute-start = (bf16[384,384]{1,0:T(8,128)(2,1)S(1)}, bf16[384,384]{1,0:T(8,128)(2,1)S(1)}, u32[]{:S(2)}, u32[]{:S(2)}) collective-permute-start(bf16[384,384]{1,0:T(8,128)(2,1)S(1)} %get-tuple-element.255), channel_id=1, source_target_pairs={{0,8},{1,17},{2,10},{3,19},{4,12},{5,21},{6,14},{7,23},{8,0},{9,25... | collective-permute-start | bytes 884744 | tf_op jit(solution)/shard_map/ppermute | solution.py:574
  7.4 5.2 %collective-permute-done.value = bf16[384,384]{1,0:T(8,128)(2,1)S(1)} collective-permute-done((bf16[384,384]{1,0:T(8,128)(2,1)S(1)}, bf16[384,384]{1,0:T(8,128)(2,1)S(1)}, u32[]{:S(2)}, u32[]{:S(2)}) %collective-permute-start) | collective-permute-done | bytes 294944 | tf_op jit(solution)/shard_map/ppermute | solution.py:574
  12.7 2.7 %collective-permute-start.2 = (bf16[384,384]{1,0:T(8,128)(2,1)S(1)}, bf16[384,384]{1,0:T(8,128)(2,1)S(1)}, u32[]{:S(2)}, u32[]{:S(2)}) collective-permute-start(bf16[384,384]{1,0:T(8,128)(2,1)S(1)} %gate.17.rest_0_), channel_id=1, source_target_pairs={{0,16},{1,9},{2,18},{3,11},{4,20},{5,13},{6,22},{7,15},{8,24},{9,1... | collective-permute-start | bytes 884744 | tf_op jit(solution)/shard_map/ppermute | solution.py:574
  15.5 3.4 %collective-permute-done.3.value = bf16[384,384]{1,0:T(8,128)(2,1)S(1)} collective-permute-done((bf16[384,384]{1,0:T(8,128)(2,1)S(1)}, bf16[384,384]{1,0:T(8,128)(2,1)S(1)}, u32[]{:S(2)}, u32[]{:S(2)}) %collective-permute-start.3) | collective-permute-done | bytes 294944 | tf_op jit(solution)/shard_map/ppermute | solution.py:574
  18.9 2.7 %collective-permute-start.7 = (bf16[384,384]{1,0:T(8,128)(2,1)S(1)}, bf16[384,384]{1,0:T(8,128)(2,1)S(1)}, u32[]{:S(2)}, u32[]{:S(2)}) collective-permute-start(bf16[384,384]{1,0:T(8,128)(2,1)S(1)} %gate.19.rest_0_), channel_id=1, source_target_pairs={{0,16},{1,9},{2,18},{3,11},{4,20},{5,13},{6,22},{7,15},{8,24},{9,1... | collective-permute-start | bytes 884744 | tf_op jit(solution)/shard_map/ppermute | solution.py:574
  21.8 1.7 %collective-permute-start.13 = (bf16[384,384]{1,0:T(8,128)(2,1)S(1)}, bf16[384,384]{1,0:T(8,128)(2,1)S(1)}, u32[]{:S(2)}, u32[]{:S(2)}) collective-permute-start(bf16[384,384]{1,0:T(8,128)(2,1)S(1)} %gate.20), channel_id=1, source_target_pairs={{0,8},{1,17},{2,10},{3,19},{4,12},{5,21},{6,14},{7,23},{8,0},{9,25... | collective-permute-start | bytes 884744 | tf_op jit(solution)/shard_map/ppermute | solution.py:574
  23.7 4.3 %collective-permute-done.7.value = bf16[384,384]{1,0:T(8,128)(2,1)S(1)} collective-permute-done((bf16[384,384]{1,0:T(8,128)(2,1)S(1)}, bf16[384,384]{1,0:T(8,128)(2,1)S(1)}, u32[]{:S(2)}, u32[]{:S(2)}) %collective-permute-start.7) | collective-permute-done | bytes 294944 | tf_op jit(solution)/shard_map/ppermute | solution.py:574
  27.9 2.5 %collective-permute-start.12 = (bf16[384,384]{1,0:T(8,128)(2,1)S(1)}, bf16[384,384]{1,0:T(8,128)(2,1)S(1)}, u32[]{:S(2)}, u32[]{:S(2)}) collective-permute-start(bf16[384,384]{1,0:T(8,128)(2,1)S(1)} %gate.20), channel_id=1, source_target_pairs={{0,16},{1,9},{2,18},{3,11},{4,20},{5,13},{6,22},{7,15},{8,24},{9,1... | collective-permute-start | bytes 884744 | tf_op jit(solution)/shard_map/ppermute | solution.py:574
  31.1 2.2 %first_forward.1 = (bf16[256,384]{1,0:T(8,128)(2,1)S(1)}, bf16[256,1152]{1,0:T(8,128)(2,1)S(1)}, bf16[256,384]{1,0:T(8,128)(2,1)S(1)}, f32[6,256,256]{2,1,0:T(8,...) custom-call(s32[8,256]{1,0:T(8,128)S(1)} %gate.16.limits, ...), custom_call_target="tpu_custom_call" | custom-call | flops 6000000000 | bytes 1 | tf_op jit(solution)/shard_map/first_forward/pallas_call | solution.py:540
  33.4 1.7 %collective-permute-done.12.value = bf16[384,384]{1,0:T(8,128)(2,1)S(1)} collective-permute-done((bf16[384,384]{1,0:T(8,128)(2,1)S(1)}, bf16[384,384]{1,0:T(8,128)(2,1)S(1)}, u32[]{:S(2)}, u32[]{:S(2)}) %collective-permute-start.12) | collective-permute-done | bytes 294944 | tf_op jit(solution)/shard_map/ppermute | solution.py:574
  35.7 4.2 %second_third_forward.1 = (bf16[256,384]{1,0:T(8,128)(2,1)S(1)}, bf16[2,4,384,384]{3,2,1,0:T(8,128)(2,1)S(1)}, bf16[256,384]{1,0:T(8,128)(2,1)S(1)}, bf16[256,11...) custom-call(s32[8,256]{1,0:T(8,128)S(1)} %gate.16.limits, ...), custom_call_target="tpu_custom_call" | custom-call | flops 3000000000 | bytes 1 | tf_op jit(solution)/shard_map/second_third_forward/pallas_call | solution.py:540
  40.3 3.6 %fourth_both.1 = (f32[256,384]{1,0:T(8,128)S(1)}, f32[256,384]{1,0:T(8,128)S(1)}, bf16[3,384,384]{2,1,0:T(8,128)(2,1)S(1)}, bf16[3,384,384]{2,1,0:T(8,128)(2,1)S(1)}, bf16[256,384]{1,0:T(8,128)(2,1)S(1)}) custom-call(s32[8,256]{1,0:T(8,128)S(1)} %gate.16.limits, bf16[256,384]{1,0:T(8,128)(2,1)S(1)} %get-tuple-element.312.h3, ...), custom_call_target="tpu_custom_call" | custom-call | flops 3000000000 | bytes 1 | tf_op jit(solution)/shard_map/fourth_both/pallas_call | solution.py:540
  46.0 2.4 %third_backward.1 = (bf16[256,384]{1,0:T(8,128)(2,1)S(1)}, bf16[2,768,384]{2,1,0:T(8,128)(2,1)S(1)}, bf16[256,192]{1,0:T(8,128)(2,1)S(1)}, f32[8,384]{1,0:T(8,128)S(1)}) custom-call(bf16[256,384]{1,0:T(8,128)(2,1)S(1)} %get-tuple-element.324.h2, f32[8,384]{1,0:T(8,128)S(1)} %get-tuple-element.361.gains, bf16[256,384]{1,0:T(8,128)(2,1)S(1)} %get-tuple-element.326.grad_h3, ...), custom_call_target="tpu_custom_call" | custom-call | flops 8000000000 | bytes 1 | tf_op jit(solution)/shard_map/third_backward/pallas_call | solution.py:540
  50.8 2.3 %second_backward.1 = (bf16[256,384]{1,0:T(8,128)(2,1)S(1)}, bf16[4,384,384]{2,1,0:T(8,128)(2,1)S(1)}, bf16[4,384,384]{2,1,0:T(8,128)(2,1)S(1)}, f32[8,384]{1,0:T(8,128)S(1)}) custom-call(bf16[256,384]{1,0:T(8,128)(2,1)S(1)} %get-tuple-element.344.h1, f32[8,384]{1,0:T(8,128)S(1)} %get-tuple-element.361.gains, ...), custom_call_target="tpu_custom_call" | custom-call | flops 20000000000 | bytes 1 | tf_op jit(solution)/shard_map/second_backward/pallas_call | solution.py:540
  53.1 3.4 %first_backward.1 = (f32[256,384]{1,0:T(8,128)}, bf16[4,384,384]{2,1,0:T(8,128)(2,1)S(1)}, bf16[4,384,384]{2,1,0:T(8,128)(2,1)S(1)}) custom-call(bf16[256,384]{1,0:T(8,128)(2,1)S(1)} %copy-done, f32[8,384]{1,0:T(8,128)S(1)} %get-tuple-element.361.gains, bf16[256,384]{1,0:T(8,128)(2,1)S(1)} %get-tuple-element.362.grad_h1, ...), custom_call_target="tpu_custom_call" | custom-call | flops 8000000000 | bytes 1 | tf_op jit(solution)/shard_map/first_backward/pallas_call | solution.py:540
  56.7 1.9 %collective-permute-start.26 = (bf16[384,384]{1,0:T(8,128)(2,1)S(1)}, bf16[384,384]{1,0:T(8,128)(2,1)S(1)}, u32[]{:S(2)}, u32[]{:S(2)}) collective-permute-start(bf16[384,384]{1,0:T(8,128)(2,1)S(1)} %sum_turn.3), channel_id=1, source_target_pairs={{0,16},{1,9},{2,18},{3,11},{4,20},{5,13},{6,22},{7,15},{8,24},{9,1... | collective-permute-start | bytes 884744 | tf_op jit(solution)/shard_map/ppermute | solution.py:574
  66.5 1.9 %collective-permute-start.31 = (bf16[384,384]{1,0:T(8,128)(2,1)S(1)}, bf16[384,384]{1,0:T(8,128)(2,1)S(1)}, u32[]{:S(2)}, u32[]{:S(2)}) collective-permute-start(bf16[384,384]{1,0:T(8,128)(2,1)S(1)} %sum_turn.4), channel_id=1, source_target_pairs={{0,16},{1,9},{2,18},{3,11},{4,20},{5,13},{6,22},{7,15},{8,24},{9,1... | collective-permute-start | bytes 884744 | tf_op jit(solution)/shard_map/ppermute | solution.py:574
  70.0 2.6 %collective-permute-start.29 = (bf16[192,384]{1,0:T(8,128)(2,1)S(1)}, bf16[192,384]{1,0:T(8,128)(2,1)S(1)}, u32[]{:S(2)}, u32[]{:S(2)}) collective-permute-start(bf16[192,384]{1,0:T(8,128)(2,1)S(1)} %sum_chips.6.left), channel_id=1, source_target_pairs={{0,4},{1,5},{2,6},{3,7},{4,0},{5,1},{6,2},{7,3},{8,12},{9,13},{10,... | collective-permute-start | bytes 442376 | tf_op jit(solution)/shard_map/ppermute | solution.py:574
  74.9 1.7 %collective-permute-start.34 = (bf16[192,384]{1,0:T(8,128)(2,1)S(1)}, bf16[192,384]{1,0:T(8,128)(2,1)S(1)}, u32[]{:S(2)}, u32[]{:S(2)}) collective-permute-start(bf16[192,384]{1,0:T(8,128)(2,1)S(1)} %get-tuple-element.404), channel_id=1, source_target_pairs={{0,2},{1,3},{2,0},{3,1},{4,6},{5,7},{6,4},{7,5},{8,10},{9,11},{10,... | collective-permute-start | bytes 442376 | tf_op jit(solution)/shard_map/ppermute | solution.py:574
  79.4 2.0 %collective-permute-start.32 = (bf16[384,384]{1,0:T(8,128)(2,1)S(1)}, bf16[384,384]{1,0:T(8,128)(2,1)S(1)}, u32[]{:S(2)}, u32[]{:S(2)}) collective-permute-start(bf16[384,384]{1,0:T(8,128)(2,1)S(1)} %sum_turn.5), channel_id=1, source_target_pairs={{0,16},{1,9},{2,18},{3,11},{4,20},{5,13},{6,22},{7,15},{8,24},{9,1... | collective-permute-start | bytes 884744 | tf_op jit(solution)/shard_map/ppermute | solution.py:574
  81.4 3.9 %collective-permute-start.37 = (bf16[192,384]{1,0:T(8,128)(2,1)S(1)}, bf16[192,384]{1,0:T(8,128)(2,1)S(1)}, u32[]{:S(2)}, u32[]{:S(2)}) collective-permute-start(bf16[192,384]{1,0:T(8,128)(2,1)S(1)} %sum_chips.8.left), channel_id=1, source_target_pairs={{0,4},{1,5},{2,6},{3,7},{4,0},{5,1},{6,2},{7,3},{8,12},{9,13},{10,... | collective-permute-start | bytes 442376 | tf_op jit(solution)/shard_map/ppermute | solution.py:574
  85.4 1.7 %collective-permute-start.36 = (bf16[384,384]{1,0:T(8,128)(2,1)S(1)}, bf16[384,384]{1,0:T(8,128)(2,1)S(1)}, u32[]{:S(2)}, u32[]{:S(2)}) collective-permute-start(bf16[384,384]{1,0:T(8,128)(2,1)S(1)} %sum_join.3.left), channel_id=1, source_target_pairs={{0,16},{1,9},{2,18},{3,11},{4,20},{5,13},{6,22},{7,15},{8,24},{9,1... | collective-permute-start | bytes 884744 | tf_op jit(solution)/shard_map/ppermute | solution.py:574
  94.3 3.3 %collective-permute-start.38 = (bf16[192,384]{1,0:T(8,128)(2,1)S(1)}, bf16[192,384]{1,0:T(8,128)(2,1)S(1)}, u32[]{:S(2)}, u32[]{:S(2)}) collective-permute-start(bf16[192,384]{1,0:T(8,128)(2,1)S(1)} %sum_chips.10.left), channel_id=1, source_target_pairs={{0,4},{1,5},{2,6},{3,7},{4,0},{5,1},{6,2},{7,3},{8,12},{9,13},{10,... | collective-permute-start | bytes 442376 | tf_op jit(solution)/shard_map/ppermute | solution.py:574
  98.7 2.0 %collective-permute-start.41 = (bf16[384,384]{1,0:T(8,128)(2,1)S(1)}, bf16[384,384]{1,0:T(8,128)(2,1)S(1)}, u32[]{:S(2)}, u32[]{:S(2)}) collective-permute-start(bf16[384,384]{1,0:T(8,128)(2,1)S(1)} %sum_join.4.rest_0_), channel_id=1, source_target_pairs={{0,16},{1,9},{2,18},{3,11},{4,20},{5,13},{6,22},{7,15},{8,24},{9,1... | collective-permute-start | bytes 884744 | tf_op jit(solution)/shard_map/ppermute | solution.py:574
  102.4 3.2 %collective-permute-done.42.value = bf16[2,384,384]{2,1,0:T(8,128)(2,1)S(1)} collective-permute-done((bf16[2,384,384]{2,1,0:T(8,128)(2,1)S(1)}, bf16[2,384,384]{2,1,0:T(8,128)(2,1)S(1)}, u32[]{:S(2)}, u32[]{:S(2)}) %collective-permute-start.42) | collective-permute-done | bytes 589856 | tf_op jit(solution)/shard_map/ppermute | solution.py:574
  107.6 2.4 %collective-permute-start.43 = (bf16[384,384]{1,0:T(8,128)(2,1)S(1)}, bf16[384,384]{1,0:T(8,128)(2,1)S(1)}, u32[]{:S(2)}, u32[]{:S(2)}) collective-permute-start(bf16[384,384]{1,0:T(8,128)(2,1)S(1)} %sum_join.5.rest_0_), channel_id=1, source_target_pairs={{0,16},{1,9},{2,18},{3,11},{4,20},{5,13},{6,22},{7,15},{8,24},{9,1... | collective-permute-start | bytes 884744 | tf_op jit(solution)/shard_map/ppermute | solution.py:574
  110.0 4.8 %collective-permute-done.45.right = bf16[384,384]{1,0:T(8,128)(2,1)S(1)} collective-permute-done((bf16[384,384]{1,0:T(8,128)(2,1)S(1)}, bf16[384,384]{1,0:T(8,128)(2,1)S(1)}, u32[]{:S(2)}, u32[]{:S(2)}) %collective-permute-start.45) | collective-permute-done | bytes 294944 | tf_op jit(solution)/shard_map/ppermute | solution.py:574
  117.6 2.3 %unpack_four.1 = (f32[384,1536]{1,0:T(8,128)}, f32[1536,384]{1,0:T(8,128)}) custom-call(bf16[2,384,384]{2,1,0:T(8,128)(2,1)S(1)} %sum_pair.2.rest_0_, bf16[2,384,384]{2,1,0:T(8,128)(2,1)S(1)} %gate.27.rest_1_, bf16[2,384,384]{2,1,0:T(8,128)(2,1)S(1)} %collective-permute-done.51.rest_2_, bf16[2,384,384]{2,1,0:T(8,128)(2,1)S(1)} %collective-permute-done.52.rest_3_), custom_call_target="tpu_custom_call" | custom-call | flops 3000000000 | bytes 1 | tf_op jit(solution)/shard_map/unpack_four/pallas_call | solution.py:540
  119.9 1.7 %collective-permute-done.50.value = bf16[384,384]{1,0:T(8,128)(2,1)S(1)} collective-permute-done((bf16[384,384]{1,0:T(8,128)(2,1)S(1)}, bf16[384,384]{1,0:T(8,128)(2,1)S(1)}, u32[]{:S(2)}, u32[]{:S(2)}) %collective-permute-start.50) | collective-permute-done | bytes 294944 | tf_op jit(solution)/shard_map/ppermute | solution.py:574
  122.3 2.3 %unpack_two.1 = (f32[384,1536]{1,0:T(8,128)}, f32[1536,384]{1,0:T(8,128)}) custom-call(bf16[384,384]{1,0:T(8,128)(2,1)S(1)} %sum_join.4.rest_0_, bf16[384,384]{1,0:T(8,128)(2,1)S(1)} %gate.28.rest_1_, bf16[2,384,384]{2,1,0:T(8,128)(2,1)S(1)} %sum_pair.3.rest_2_, bf16[384,384]{1,0:T(8,128)(2,1)S(1)} %collective-permute-done.47.rest_3_, ...), custom_call_target="tpu_custom_call" | custom-call | flops 1000000000 | bytes 1 | tf_op jit(solution)/shard_map/unpack_two/pallas_call | solution.py:540
  125.1 1.8 %unpack_some.1 = (f32[384,1152]{1,0:T(8,128)}, f32[384,384]{1,0:T(8,128)}, f32[384,768]{1,0:T(8,128)}, f32[192,384]{1,0:T(8,128)}, f32[384,384]{1,0:T(8,128)}, /...) custom-call(bf16[384,384]{1,0:T(8,128)(2,1)S(1)} %sum_join.5.rest_0_, ...), custom_call_target="tpu_custom_call" | custom-call | flops 3000000000 | bytes 1 | tf_op jit(solution)/shard_map/unpack_some/pallas_call | solution.py:540
  127.0 1.7 %unpack_rest.1 = (f32[384,1152]{1,0:T(8,128)}, f32[384,384]{1,0:T(8,128)}, f32[384,768]{1,0:T(8,128)}, f32[192,384]{1,0:T(8,128)}, f32[384,384]{1,0:T(8,128)}, /...) custom-call(bf16[384,384]{1,0:T(8,128)(2,1)S(1)} %gate.31.rest_0_, ...), custom_call_target="tpu_custom_call", output_to_operand_aliasing={{0}: (2, {}), {1}: (3, {}), {2}: (4, {}), {3}: (5, {}), {4}... | custom-call | flops 4000000000 | bytes 1 | tf_op jit(solution)/shard_map/unpack_rest/pallas_call | solution.py:540
  (133 shorter events, 41.1 us)
Async XLA Ops:
  2.3 10.3 %collective-permute-start = (bf16[384,384]{1,0:T(8,128)(2,1)S(1)}, bf16[384,384]{1,0:T(8,128)(2,1)S(1)}, u32[]{:S(2)}, u32[]{:S(2)}) collective-permute-start(bf16[384,384]{1,0:T(8,128)(2,1)S(1)} %get-tuple-element.255), channel_id=1, source_target_pairs={{0,8},{1,17},{2,10},{3,19},{4,12},{5,21},{6,14},{7,23},{8,0},{9,25... | collective-permute-start | bytes 884744 | tf_op jit(solution)/shard_map/ppermute | solution.py:574
  5.3 10.1 %collective-permute-start.1 = (bf16[384,384]{1,0:T(8,128)(2,1)S(1)}, bf16[384,384]{1,0:T(8,128)(2,1)S(1)}, u32[]{:S(2)}, u32[]{:S(2)}) collective-permute-start(bf16[384,384]{1,0:T(8,128)(2,1)S(1)} %get-tuple-element.255), channel_id=1, source_target_pairs={{0,16},{1,9},{2,18},{3,11},{4,20},{5,13},{6,22},{7,15},{8,24},{9,1... | collective-permute-start | bytes 884744 | tf_op jit(solution)/shard_map/ppermute | solution.py:574
  6.8 16.7 %collective-permute-start.8 = (bf16[384,384]{1,0:T(8,128)(2,1)S(1)}, bf16[384,384]{1,0:T(8,128)(2,1)S(1)}, u32[]{:S(2)}, u32[]{:S(2)}) collective-permute-start(bf16[384,384]{1,0:T(8,128)(2,1)S(1)} %get-tuple-element.259), channel_id=1, source_target_pairs={{0,16},{1,9},{2,18},{3,11},{4,20},{5,13},{6,22},{7,15},{8,24},{9,1... | collective-permute-start | bytes 884744 | tf_op jit(solution)/shard_map/ppermute | solution.py:574
  7.3 11.6 %collective-permute-start.3 = (bf16[384,384]{1,0:T(8,128)(2,1)S(1)}, bf16[384,384]{1,0:T(8,128)(2,1)S(1)}, u32[]{:S(2)}, u32[]{:S(2)}) collective-permute-start(bf16[384,384]{1,0:T(8,128)(2,1)S(1)} %get-tuple-element.259), channel_id=1, source_target_pairs={{0,8},{1,17},{2,10},{3,19},{4,12},{5,21},{6,14},{7,23},{8,0},{9,25... | collective-permute-start | bytes 884744 | tf_op jit(solution)/shard_map/ppermute | solution.py:574
  12.6 17.9 %collective-permute-start.4 = (bf16[384,384]{1,0:T(8,128)(2,1)S(1)}, bf16[384,384]{1,0:T(8,128)(2,1)S(1)}, u32[]{:S(2)}, u32[]{:S(2)}) collective-permute-start(bf16[384,384]{1,0:T(8,128)(2,1)S(1)} %gate.17.rest_0_), channel_id=1, source_target_pairs={{0,1},{1,0},{2,3},{3,2},{4,5},{5,4},{6,7},{7,6},{8,9},{9,8},{10,11... | collective-permute-start | bytes 884744 | tf_op jit(solution)/shard_map/ppermute | solution.py:574
  12.7 9.1 %collective-permute-start.2 = (bf16[384,384]{1,0:T(8,128)(2,1)S(1)}, bf16[384,384]{1,0:T(8,128)(2,1)S(1)}, u32[]{:S(2)}, u32[]{:S(2)}) collective-permute-start(bf16[384,384]{1,0:T(8,128)(2,1)S(1)} %gate.17.rest_0_), channel_id=1, source_target_pairs={{0,16},{1,9},{2,18},{3,11},{4,20},{5,13},{6,22},{7,15},{8,24},{9,1... | collective-permute-start | bytes 884744 | tf_op jit(solution)/shard_map/ppermute | solution.py:574
  15.4 15.0 %collective-permute-start.5 = (bf16[384,384]{1,0:T(8,128)(2,1)S(1)}, bf16[384,384]{1,0:T(8,128)(2,1)S(1)}, u32[]{:S(2)}, u32[]{:S(2)}) collective-permute-start(bf16[384,384]{1,0:T(8,128)(2,1)S(1)} %gate.18.rest_1_), channel_id=1, source_target_pairs={{0,1},{1,0},{2,3},{3,2},{4,5},{5,4},{6,7},{7,6},{8,9},{9,8},{10,11... | collective-permute-start | bytes 884744 | tf_op jit(solution)/shard_map/ppermute | solution.py:574
  18.9 9.0 %collective-permute-start.7 = (bf16[384,384]{1,0:T(8,128)(2,1)S(1)}, bf16[384,384]{1,0:T(8,128)(2,1)S(1)}, u32[]{:S(2)}, u32[]{:S(2)}) collective-permute-start(bf16[384,384]{1,0:T(8,128)(2,1)S(1)} %gate.19.rest_0_), channel_id=1, source_target_pairs={{0,16},{1,9},{2,18},{3,11},{4,20},{5,13},{6,22},{7,15},{8,24},{9,1... | collective-permute-start | bytes 884744 | tf_op jit(solution)/shard_map/ppermute | solution.py:574
  21.8 11.5 %collective-permute-start.13 = (bf16[384,384]{1,0:T(8,128)(2,1)S(1)}, bf16[384,384]{1,0:T(8,128)(2,1)S(1)}, u32[]{:S(2)}, u32[]{:S(2)}) collective-permute-start(bf16[384,384]{1,0:T(8,128)(2,1)S(1)} %gate.20), channel_id=1, source_target_pairs={{0,8},{1,17},{2,10},{3,19},{4,12},{5,21},{6,14},{7,23},{8,0},{9,25... | collective-permute-start | bytes 884744 | tf_op jit(solution)/shard_map/ppermute | solution.py:574
  23.5 7.5 %collective-permute-start.6 = (bf16[384,384]{1,0:T(8,128)(2,1)S(1)}, bf16[384,384]{1,0:T(8,128)(2,1)S(1)}, u32[]{:S(2)}, u32[]{:S(2)}) collective-permute-start(bf16[384,384]{1,0:T(8,128)(2,1)S(1)} %gate.21.rest_2_), channel_id=1, source_target_pairs={{0,1},{1,0},{2,3},{3,2},{4,5},{5,4},{6,7},{7,6},{8,9},{9,8},{10,11... | collective-permute-start | bytes 884744 | tf_op jit(solution)/shard_map/ppermute | solution.py:574
  27.9 7.2 %collective-permute-start.12 = (bf16[384,384]{1,0:T(8,128)(2,1)S(1)}, bf16[384,384]{1,0:T(8,128)(2,1)S(1)}, u32[]{:S(2)}, u32[]{:S(2)}) collective-permute-start(bf16[384,384]{1,0:T(8,128)(2,1)S(1)} %gate.20), channel_id=1, source_target_pairs={{0,16},{1,9},{2,18},{3,11},{4,20},{5,13},{6,22},{7,15},{8,24},{9,1... | collective-permute-start | bytes 884744 | tf_op jit(solution)/shard_map/ppermute | solution.py:574
  48.5 8.0 %collective-permute-start.22 = (bf16[384,384]{1,0:T(8,128)(2,1)S(1)}, bf16[384,384]{1,0:T(8,128)(2,1)S(1)}, u32[]{:S(2)}, u32[]{:S(2)}) collective-permute-start(bf16[384,384]{1,0:T(8,128)(2,1)S(1)} %sum_both.1), channel_id=1, source_target_pairs={{0,8},{1,17},{2,10},{3,19},{4,12},{5,21},{6,14},{7,23},{8,0},{9,25... | collective-permute-start | bytes 884744 | tf_op jit(solution)/shard_map/ppermute | solution.py:574
  50.2 14.3 %collective-permute-start.25 = (bf16[384,384]{1,0:T(8,128)(2,1)S(1)}, bf16[384,384]{1,0:T(8,128)(2,1)S(1)}, u32[]{:S(2)}, u32[]{:S(2)}) collective-permute-start(bf16[384,384]{1,0:T(8,128)(2,1)S(1)} %sum_near.1), channel_id=1, source_target_pairs={{0,8},{1,17},{2,10},{3,19},{4,12},{5,21},{6,14},{7,23},{8,0},{9,25... | collective-permute-start | bytes 884744 | tf_op jit(solution)/shard_map/ppermute | solution.py:574
  56.7 7.8 %collective-permute-start.26 = (bf16[384,384]{1,0:T(8,128)(2,1)S(1)}, bf16[384,384]{1,0:T(8,128)(2,1)S(1)}, u32[]{:S(2)}, u32[]{:S(2)}) collective-permute-start(bf16[384,384]{1,0:T(8,128)(2,1)S(1)} %sum_turn.3), channel_id=1, source_target_pairs={{0,16},{1,9},{2,18},{3,11},{4,20},{5,13},{6,22},{7,15},{8,24},{9,1... | collective-permute-start | bytes 884744 | tf_op jit(solution)/shard_map/ppermute | solution.py:574
  61.4 13.2 %collective-permute-start.30 = (bf16[384,384]{1,0:T(8,128)(2,1)S(1)}, bf16[384,384]{1,0:T(8,128)(2,1)S(1)}, u32[]{:S(2)}, u32[]{:S(2)}) collective-permute-start(bf16[384,384]{1,0:T(8,128)(2,1)S(1)} %get-tuple-element.399), channel_id=1, source_target_pairs={{0,8},{1,17},{2,10},{3,19},{4,12},{5,21},{6,14},{7,23},{8,0},{9,25... | collective-permute-start | bytes 884744 | tf_op jit(solution)/shard_map/ppermute | solution.py:574
  66.5 8.1 %collective-permute-start.31 = (bf16[384,384]{1,0:T(8,128)(2,1)S(1)}, bf16[384,384]{1,0:T(8,128)(2,1)S(1)}, u32[]{:S(2)}, u32[]{:S(2)}) collective-permute-start(bf16[384,384]{1,0:T(8,128)(2,1)S(1)} %sum_turn.4), channel_id=1, source_target_pairs={{0,16},{1,9},{2,18},{3,11},{4,20},{5,13},{6,22},{7,15},{8,24},{9,1... | collective-permute-start | bytes 884744 | tf_op jit(solution)/shard_map/ppermute | solution.py:574
  70.0 8.1 %collective-permute-start.29 = (bf16[192,384]{1,0:T(8,128)(2,1)S(1)}, bf16[192,384]{1,0:T(8,128)(2,1)S(1)}, u32[]{:S(2)}, u32[]{:S(2)}) collective-permute-start(bf16[192,384]{1,0:T(8,128)(2,1)S(1)} %sum_chips.6.left), channel_id=1, source_target_pairs={{0,4},{1,5},{2,6},{3,7},{4,0},{5,1},{6,2},{7,3},{8,12},{9,13},{10,... | collective-permute-start | bytes 442376 | tf_op jit(solution)/shard_map/ppermute | solution.py:574
  74.1 13.0 %collective-permute-start.23 = (bf16[384,384]{1,0:T(8,128)(2,1)S(1)}, bf16[384,384]{1,0:T(8,128)(2,1)S(1)}, u32[]{:S(2)}, u32[]{:S(2)}) collective-permute-start(bf16[384,384]{1,0:T(8,128)(2,1)S(1)} %get-tuple-element.386), channel_id=1, source_target_pairs={{0,8},{1,17},{2,10},{3,19},{4,12},{5,21},{6,14},{7,23},{8,0},{9,25... | collective-permute-start | bytes 884744 | tf_op jit(solution)/shard_map/ppermute | solution.py:574
  78.2 7.2 %collective-permute-start.33 = (bf16[192,384]{1,0:T(8,128)(2,1)S(1)}, bf16[192,384]{1,0:T(8,128)(2,1)S(1)}, u32[]{:S(2)}, u32[]{:S(2)}) collective-permute-start(bf16[192,384]{1,0:T(8,128)(2,1)S(1)} %sum_chips.7.kept), channel_id=1, source_target_pairs={{0,2},{1,3},{2,0},{3,1},{4,6},{5,7},{6,4},{7,5},{8,10},{9,11},{10,... | collective-permute-start | bytes 442376 | tf_op jit(solution)/shard_map/ppermute | solution.py:574
  79.4 7.7 %collective-permute-start.32 = (bf16[384,384]{1,0:T(8,128)(2,1)S(1)}, bf16[384,384]{1,0:T(8,128)(2,1)S(1)}, u32[]{:S(2)}, u32[]{:S(2)}) collective-permute-start(bf16[384,384]{1,0:T(8,128)(2,1)S(1)} %sum_turn.5), channel_id=1, source_target_pairs={{0,16},{1,9},{2,18},{3,11},{4,20},{5,13},{6,22},{7,15},{8,24},{9,1... | collective-permute-start | bytes 884744 | tf_op jit(solution)/shard_map/ppermute | solution.py:574
  81.4 8.9 %collective-permute-start.37 = (bf16[192,384]{1,0:T(8,128)(2,1)S(1)}, bf16[192,384]{1,0:T(8,128)(2,1)S(1)}, u32[]{:S(2)}, u32[]{:S(2)}) collective-permute-start(bf16[192,384]{1,0:T(8,128)(2,1)S(1)} %sum_chips.8.left), channel_id=1, source_target_pairs={{0,4},{1,5},{2,6},{3,7},{4,0},{5,1},{6,2},{7,3},{8,12},{9,13},{10,... | collective-permute-start | bytes 442376 | tf_op jit(solution)/shard_map/ppermute | solution.py:574
  85.4 7.1 %collective-permute-start.36 = (bf16[384,384]{1,0:T(8,128)(2,1)S(1)}, bf16[384,384]{1,0:T(8,128)(2,1)S(1)}, u32[]{:S(2)}, u32[]{:S(2)}) collective-permute-start(bf16[384,384]{1,0:T(8,128)(2,1)S(1)} %sum_join.3.left), channel_id=1, source_target_pairs={{0,16},{1,9},{2,18},{3,11},{4,20},{5,13},{6,22},{7,15},{8,24},{9,1... | collective-permute-start | bytes 884744 | tf_op jit(solution)/shard_map/ppermute | solution.py:574
  90.4 7.2 %collective-permute-start.39 = (bf16[192,384]{1,0:T(8,128)(2,1)S(1)}, bf16[192,384]{1,0:T(8,128)(2,1)S(1)}, u32[]{:S(2)}, u32[]{:S(2)}) collective-permute-start(bf16[192,384]{1,0:T(8,128)(2,1)S(1)} %sum_chips.9.kept), channel_id=1, source_target_pairs={{0,2},{1,3},{2,0},{3,1},{4,6},{5,7},{6,4},{7,5},{8,10},{9,11},{10,... | collective-permute-start | bytes 442376 | tf_op jit(solution)/shard_map/ppermute | solution.py:574
  92.5 13.1 %collective-permute-start.42 = (bf16[2,384,384]{2,1,0:T(8,128)(2,1)S(1)}, bf16[2,384,384]{2,1,0:T(8,128)(2,1)S(1)}, u32[]{:S(2)}, u32[]{:S(2)}) collective-permute-start(bf16[2,384,384]{2,1,0:T(8,128)(2,1)S(1)} %sum_pair.2.rest_0_), channel_id=1, source_target_pairs={{0,8},{1,17},{2,10},{3,19},{4,12},{5,21},{6,14},{7,23},{8,0},{9,25... | collective-permute-start | bytes 1769480 | tf_op jit(solution)/shard_map/ppermute | solution.py:574
  94.3 8.0 %collective-permute-start.38 = (bf16[192,384]{1,0:T(8,128)(2,1)S(1)}, bf16[192,384]{1,0:T(8,128)(2,1)S(1)}, u32[]{:S(2)}, u32[]{:S(2)}) collective-permute-start(bf16[192,384]{1,0:T(8,128)(2,1)S(1)} %sum_chips.10.left), channel_id=1, source_target_pairs={{0,4},{1,5},{2,6},{3,7},{4,0},{5,1},{6,2},{7,3},{8,12},{9,13},{10,... | collective-permute-start | bytes 442376 | tf_op jit(solution)/shard_map/ppermute | solution.py:574
  97.7 12.4 %collective-permute-start.44 = (bf16[384,384]{1,0:T(8,128)(2,1)S(1)}, bf16[384,384]{1,0:T(8,128)(2,1)S(1)}, u32[]{:S(2)}, u32[]{:S(2)}) collective-permute-start(bf16[384,384]{1,0:T(8,128)(2,1)S(1)} %sum_join.4.rest_0_), channel_id=1, source_target_pairs={{0,8},{1,17},{2,10},{3,19},{4,12},{5,21},{6,14},{7,23},{8,0},{9,25... | collective-permute-start | bytes 884744 | tf_op jit(solution)/shard_map/ppermute | solution.py:574
  100.8 15.5 %collective-permute-start.51 = (bf16[2,384,384]{2,1,0:T(8,128)(2,1)S(1)}, bf16[2,384,384]{2,1,0:T(8,128)(2,1)S(1)}, u32[]{:S(2)}, u32[]{:S(2)}) collective-permute-start(bf16[2,384,384]{2,1,0:T(8,128)(2,1)S(1)} %sum_pair.2.rest_0_), channel_id=1, source_target_pairs={{0,1},{1,0},{2,3},{3,2},{4,5},{5,4},{6,7},{7,6},{8,9},{9,8},{10,11... | collective-permute-start | bytes 1769480 | tf_op jit(solution)/shard_map/ppermute | solution.py:574
  105.7 11.2 %collective-permute-start.52 = (bf16[2,384,384]{2,1,0:T(8,128)(2,1)S(1)}, bf16[2,384,384]{2,1,0:T(8,128)(2,1)S(1)}, u32[]{:S(2)}, u32[]{:S(2)}) collective-permute-start(bf16[2,384,384]{2,1,0:T(8,128)(2,1)S(1)} %gate.27.rest_1_), channel_id=1, source_target_pairs={{0,1},{1,0},{2,3},{3,2},{4,5},{5,4},{6,7},{7,6},{8,9},{9,8},{10,11... | collective-permute-start | bytes 1769480 | tf_op jit(solution)/shard_map/ppermute | solution.py:574
  105.8 9.0 %collective-permute-start.45 = (bf16[384,384]{1,0:T(8,128)(2,1)S(1)}, bf16[384,384]{1,0:T(8,128)(2,1)S(1)}, u32[]{:S(2)}, u32[]{:S(2)}) collective-permute-start(bf16[384,384]{1,0:T(8,128)(2,1)S(1)} %gate.28.rest_1_), channel_id=1, source_target_pairs={{0,8},{1,17},{2,10},{3,19},{4,12},{5,21},{6,14},{7,23},{8,0},{9,25... | collective-permute-start | bytes 884744 | tf_op jit(solution)/shard_map/ppermute | solution.py:574
  107.6 8.5 %collective-permute-start.43 = (bf16[384,384]{1,0:T(8,128)(2,1)S(1)}, bf16[384,384]{1,0:T(8,128)(2,1)S(1)}, u32[]{:S(2)}, u32[]{:S(2)}) collective-permute-start(bf16[384,384]{1,0:T(8,128)(2,1)S(1)} %sum_join.5.rest_0_), channel_id=1, source_target_pairs={{0,16},{1,9},{2,18},{3,11},{4,20},{5,13},{6,22},{7,15},{8,24},{9,1... | collective-permute-start | bytes 884744 | tf_op jit(solution)/shard_map/ppermute | solution.py:574
  110.0 11.5 %collective-permute-start.47 = (bf16[384,384]{1,0:T(8,128)(2,1)S(1)}, bf16[384,384]{1,0:T(8,128)(2,1)S(1)}, u32[]{:S(2)}, u32[]{:S(2)}) collective-permute-start(bf16[384,384]{1,0:T(8,128)(2,1)S(1)} %sum_join.4.rest_0_), channel_id=1, source_target_pairs={{0,1},{1,0},{2,3},{3,2},{4,5},{5,4},{6,7},{7,6},{8,9},{9,8},{10,11... | collective-permute-start | bytes 884744 | tf_op jit(solution)/shard_map/ppermute | solution.py:574
  116.9 7.9 %collective-permute-start.46 = (bf16[384,384]{1,0:T(8,128)(2,1)S(1)}, bf16[384,384]{1,0:T(8,128)(2,1)S(1)}, u32[]{:S(2)}, u32[]{:S(2)}) collective-permute-start(bf16[384,384]{1,0:T(8,128)(2,1)S(1)} %gate.29.rest_1_), channel_id=1, source_target_pairs={{0,8},{1,17},{2,10},{3,19},{4,12},{5,21},{6,14},{7,23},{8,0},{9,25... | collective-permute-start | bytes 884744 | tf_op jit(solution)/shard_map/ppermute | solution.py:574
  (26 other events, 133.0 us)
